TPU v7x, 32 devices: a whole 2x2x4 slice. The times are simulated.
32 devices in a mesh: dp: 8 (over z, x), tensor: 4 (over y, core).
Axes of the slice: x: 2, y: 2, z: 4, core: 2. Of those that a mesh axis runs over, the one named last changes fastest.
Arguments:
- gate_pre: bfloat16 [2048, 12800], P('dp', 'tensor'), may hold values from -6 to 6
- up_pre: bfloat16 [2048, 12800], P('dp', 'tensor'), may hold values from -6 to 6
- down_codes: bfloat16 [12800, 2560], P(('tensor', 'dp')), may hold values from -127 to 127
- down_scales: float32 [12800, 10], P(('tensor', 'dp')), may hold values from 4e-05 to 0.00024
- cotangent: bfloat16 [2048, 2560], P(('dp', 'tensor')), may hold values from -6 to 6
Outputs:
- layer_out: bfloat16 [2048, 2560], P(('dp', 'tensor'))
- gate_grad: bfloat16 [2048, 12800], P('dp', 'tensor')
- up_grad: bfloat16 [2048, 12800], P('dp', 'tensor')
- weight_grad: float32 [12800, 2560], P(('tensor', 'dp'))
All inputs are finite; a program needn't handle non-finite values.
Results may differ from a plain program's by a relative error of at most 0.022.
Values may be sent and summed in bfloat16 or wider, within the bound.
No kernel may reach another device: no remote copies, remote signals or barrier semaphores. Data moves between devices by JAX's collectives and lax.ppermute only.
A program may use at most 192 MiB of HBM per device.

v0:
```python
import functools

import jax
import jax.numpy as jnp
from jax import lax
from jax.experimental import pallas as pl
from jax.experimental.pallas import tpu as pltpu
from jax.sharding import Mesh, PartitionSpec as P

VMEM_BYTES = 32 * 2**20


def dequantize(codes, scales):
    rows, width = codes.shape
    nblocks = scales.shape[1]
    blocks = codes.astype(jnp.float32).reshape(rows, nblocks, width // nblocks) * scales[:, :, None]
    return blocks.reshape(rows, width).astype(jnp.bfloat16)


def swap(value, axis):
    return lax.ppermute(value, axis, [(0, 1), (1, 0)])


def gather_pair(value, axis):
    if lax.axis_size(axis) != 2:
        return lax.all_gather(value, axis, axis=0)
    other = swap(value, axis)
    first = lax.axis_index(axis) == 0
    return jnp.stack([jnp.where(first, value, other), jnp.where(first, other, value)])


def scatter_sum(parts, axis):
    size = lax.axis_size(axis)
    if size == 1:
        return parts[0].astype(jnp.float32)
    if size != 2:
        received = lax.all_to_all(parts.astype(jnp.bfloat16), axis, 0, 0, tiled=True)
        return jnp.sum(received.astype(jnp.float32), axis=0)
    me = lax.axis_index(axis)
    theirs = lax.dynamic_index_in_dim(parts, 1 - me, 0, keepdims=False).astype(jnp.bfloat16)
    mine = lax.dynamic_index_in_dim(parts, me, 0, keepdims=False)
    return mine.astype(jnp.float32) + swap(theirs, axis).astype(jnp.float32)


def exchange(value, axis, offset):
    size = lax.axis_size(axis)
    return lax.ppermute(value, axis, [(i, i ^ offset) for i in range(size)])


def call_kernel(kernel, place, inputs, in_specs, out_shapes, out_specs, grid, scratch, cost):
    flops, nbytes, transcendentals = cost
    return pl.pallas_call(
        kernel,
        out_shape=out_shapes,
        grid_spec=pltpu.PrefetchScalarGridSpec(
            num_scalar_prefetch=1,
            grid=grid,
            in_specs=in_specs,
            out_specs=out_specs,
            scratch_shapes=scratch,
        ),
        compiler_params=pltpu.CompilerParams(vmem_limit_bytes=VMEM_BYTES),
        cost_estimate=pl.CostEstimate(
            flops=flops, bytes_accessed=nbytes, transcendentals=transcendentals
        ),
    )(place, *inputs)


def whole(shape):
    return pl.BlockSpec(shape, lambda i, place: (0,) * len(shape))


def token_start(place, block, rows):
    return pl.multiple_of(((place[2] ^ (block % 2)) * 2 + (place[3] ^ (block // 2))) * rows, 16)


def hidden_kernel(parts, units, place, gate, up, *refs):
    outs, (natural, columns) = refs[: len(parts)], refs[len(parts) :]
    step = pl.program_id(0)
    group, span = gate.shape
    rows = group // 4
    value = gate[...].astype(jnp.float32)
    hidden = value * jax.nn.sigmoid(value) * up[...].astype(jnp.float32)
    natural[...] = hidden.astype(jnp.bfloat16)
    ordered = [natural[pl.ds(token_start(place, b, rows), rows), :] for b in range(4)]
    columns[pl.ds(pl.multiple_of(step * span, 128), span), :] = jnp.concatenate(ordered, axis=0).T

    @pl.when(step == pl.num_programs(0) - 1)
    def _():
        half = units // 2
        for out, (k, first, count) in zip(outs, parts):
            for r in range(count):
                start = (place[0] ^ k) * units + (place[1] ^ (first + r)) * half
                out[r * half : (r + 1) * half, :] = columns[
                    pl.ds(pl.multiple_of(start, 16), half), :
                ]


def weight_kernel(place, codes, scales, *halves):
    span = codes.shape[1] // scales.shape[1]
    for block in range(scales.shape[1]):
        value = codes[:, block * span : (block + 1) * span].astype(jnp.float32)
        value = (value * scales[:, block : block + 1]).astype(jnp.bfloat16)
        at = block * span
        half, at = (0, at) if at < halves[0].shape[1] else (1, at - halves[0].shape[1])
        halves[half][:, at : at + span] = value


def join_kernel(place, own_a, own_b, other_a, other_b, weight):
    half, middle = own_a.shape
    weight[:half, :middle] = own_a[...]
    weight[:half, middle:] = own_b[...]
    weight[half:, :middle] = other_a[...]
    weight[half:, middle:] = other_b[...]


def tokens_kernel(picks, place, *refs):
    tokens = refs[-1]
    rows = refs[0].shape[-2]
    for at, (array, block) in enumerate(picks):
        source = refs[array]
        tokens[at * rows : (at + 1) * rows, :] = source[block] if len(source.shape) == 3 else source[...]


def columns_kernel(parts, by_rows, by_lanes, place, *refs):
    pieces, (keep, send, *rest) = refs[: len(parts)], refs[len(parts) :]
    half, group = rest[0].shape[0], pieces[0].shape[1]
    rows = group // 4
    for piece, (k, first, count) in zip(pieces, parts):
        turned = piece[...].T
        row, lane = by_rows.index(k), by_lanes.index(k)
        lanes = slice(lane % 2 * group, (lane % 2 + 1) * group)
        for b in range(4):
            target = send if b >= 2 else keep
            start = ((b % 2) * len(by_rows) + row) * rows
            target[start : start + rows, first * half : (first + count) * half] = turned[
                b * rows : (b + 1) * rows, :
            ]
        for r in range(count):
            rest[lane // 2 * 2 + first + r][:, lanes] = piece[r * half : (r + 1) * half, :]


def grads_kernel(nz, units, place, gate, up, *refs):
    pieces, (gate_grad, up_grad, columns, natural) = refs[:nz], refs[nz:]
    step = pl.program_id(0)
    group, span = gate.shape
    rows = group // 4

    @pl.when(step == 0)
    def _():
        half = units // 2
        for k in range(nz):
            for r in range(2):
                start = (place[0] ^ k) * units + (place[1] ^ r) * half
                columns[pl.ds(pl.multiple_of(start, 16), half), :] = pieces[k][
                    r * half : (r + 1) * half, :
                ]

    ordered = columns[pl.ds(pl.multiple_of(step * span, 128), span), :].T
    for b in range(4):
        natural[pl.ds(token_start(place, b, rows), rows), :] = ordered[b * rows : (b + 1) * rows]
    dhidden = natural[...].astype(jnp.float32)
    value = gate[...].astype(jnp.float32)
    up_value = up[...].astype(jnp.float32)
    sigmoid_gate = jax.nn.sigmoid(value)
    gate_grad[...] = (
        dhidden * up_value * sigmoid_gate * (1.0 + value * (1.0 - sigmoid_gate))
    ).astype(jnp.bfloat16)
    up_grad[...] = (dhidden * (value * sigmoid_gate)).astype(jnp.bfloat16)


def matmul(lhs, rhs, lhs_dim=1, rhs_dim=0, dtype=jnp.float32):
    dims = (((lhs_dim,), (rhs_dim,)), ((), ()))
    return lax.dot_general(lhs, rhs, dims, preferred_element_type=jnp.float32).astype(dtype)


def paired_body(gate_pre, up_pre, down_codes, down_scales, cotangent):
    group_rows, local_hidden = gate_pre.shape
    owned, width = down_codes.shape
    rows = cotangent.shape[0]
    nz, units, nblocks = 4, 2 * owned, down_scales.shape[1]
    middle = 3 * nblocks // 5 * (width // nblocks)
    total_tokens = group_rows * nz * 2
    bf16, f32 = jnp.bfloat16, jnp.float32
    place = jnp.stack([lax.axis_index(name) for name in ("z", "x", "y", "c")]).astype(jnp.int32)
    struct = jax.ShapeDtypeStruct
    barrier = lax.optimization_barrier

    far, near = exchange(cotangent, "z", 2), exchange(cotangent, "z", 1)
    own_y, own_c = exchange(cotangent, "y", 1), exchange(cotangent, "c", 1)

    sides = ((owned, middle), (owned, width - middle))
    own_a, own_b = call_kernel(
        weight_kernel, place, (down_codes, down_scales),
        [whole(down_codes.shape), whole(down_scales.shape)],
        [struct(shape, bf16) for shape in sides], [whole(shape) for shape in sides], (1,), [],
        (2 * owned * width, 4 * owned * width, 0),
    )
    other_a = exchange(own_a, "x", 1)

    parts = tuple((k, 0, 2) for k in (0, 2, 3, 1))
    pieces = [struct((count * owned, group_rows), bf16) for _, _, count in parts]
    piece_specs = [whole(piece.shape) for piece in pieces]
    span = column_span(local_hidden)
    steps = local_hidden // span
    wide = pl.BlockSpec((group_rows, span), lambda i, place: (0, i))
    act_bytes = group_rows * local_hidden * 2
    act_scratch = [pltpu.VMEM((group_rows, span), bf16), pltpu.VMEM((local_hidden, group_rows), bf16)]
    sent = call_kernel(
        functools.partial(hidden_kernel, parts, units), place, (gate_pre, up_pre), [wide] * 2,
        pieces, piece_specs, (steps,), act_scratch,
        (4 * act_bytes, 3 * act_bytes, act_bytes // 2),
    )

    far, near, own_y, own_c, sent = barrier((far, near, own_y, own_c, sent))
    last = exchange(far, "z", 1)
    other_y = exchange(jnp.stack([far, near]), "y", 1)
    other_b = exchange(own_b, "x", 1)
    columns = [sent[0], exchange(sent[1], "z", 2)]
    first_c = exchange(jnp.stack([own_y, far, near]), "c", 1)
    last, other_y, columns, other_a, sent, first_c = barrier(
        (last, other_y, columns, other_a, sent, first_c)
    )

    last_y = exchange(last, "y", 1)
    columns += [exchange(sent[i], "z", parts[i][0]) for i in range(2, len(parts))]
    other_c = exchange(jnp.stack([other_y[0], other_y[1], last]), "c", 1)
    last_y, columns, other_b = barrier((last_y, columns, other_b))
    last_c = exchange(last_y, "c", 1)

    weight = call_kernel(
        join_kernel, place, (own_a, own_b, other_a, other_b),
        [whole(shape) for shape in sides] * 2,
        struct((units, width), bf16), whole((units, width)), (1,), [],
        (0, 4 * units * width, 0),
    )

    half_tokens = nz * group_rows // 2
    by_rows, by_lanes = (1, 3, 0, 2), (0, 2, 1, 3)
    keep, send, *by_units = call_kernel(
        functools.partial(columns_kernel, parts, by_rows, by_lanes), place, columns, piece_specs,
        [struct((half_tokens, units), bf16)] * 2 + [struct((owned, half_tokens), bf16)] * 4,
        [whole((half_tokens, units))] * 2 + [whole((owned, half_tokens))] * 4, (1,), [],
        (0, 12 * units * half_tokens, 0),
    )

    def gather_tokens(arrays, picks):
        return call_kernel(
            functools.partial(tokens_kernel, picks), place, arrays,
            [whole(array.shape) for array in arrays], struct((half_tokens, width), bf16),
            whole((half_tokens, width)), (1,), [], (0, 4 * half_tokens * width, 0),
        )

    even = gather_tokens(
        (cotangent, own_y, own_c, far, other_y, first_c, other_c),
        ((0, 0), (1, 0), (2, 0), (5, 0), (3, 0), (4, 0), (5, 1), (6, 0)),
    )
    odd = gather_tokens(
        (near, last, last_y, other_y, first_c, other_c, last_c),
        ((0, 0), (3, 1), (4, 2), (5, 1), (1, 0), (2, 0), (5, 2), (6, 0)),
    )
    even, odd, send, keep = barrier((even, odd, send, keep))
    flat = [even, odd]

    factor = float(total_tokens) ** (-0.5)


    def grad_half(r):
        return (matmul(by_units[r], flat[0]) + matmul(by_units[2 + r], flat[1])) * factor

    def back_of(k):
        rows_of_k = flat[k % 2][k // 2 * group_rows : (k // 2 + 1) * group_rows]
        return matmul(weight, rows_of_k, 1, 1, bf16)

    over_c = exchange(matmul(send, weight, dtype=bf16), "c", 1)
    back = [None, None, back_of(2), None]
    back[2], flat = barrier((back[2], flat))
    theirs = grad_half(1).astype(bf16)
    theirs, keep, flat = barrier((theirs, keep, flat))
    over_x = exchange(theirs, "x", 1)
    kept = matmul(keep, weight, dtype=bf16)
    back = [back_of(0), back_of(1), back[2], back_of(3)]
    back = [back[0]] + [exchange(back[k], "z", k) for k in range(1, nz)]
    sums = (kept.astype(f32) + over_c.astype(f32)).reshape(2, nz, rows, width)
    odd_y = exchange(sums[1, :2].astype(bf16), "y", 1)
    even_y = exchange(sums[1, 2:].astype(bf16), "y", 1)
    odd_sum = (sums[0, :2] + odd_y.astype(f32)).astype(bf16)
    odd_sum, back[2] = barrier((odd_sum, back[2]))
    even_y, _ = barrier((even_y, odd_sum))
    near_sum = exchange(odd_sum, "z", 1).astype(f32)
    even_sum = sums[0, 2:] + even_y.astype(f32)
    ours, across = even_sum[0] + near_sum[0], (even_sum[1] + near_sum[1]).astype(bf16)
    across, back[3] = barrier((across, back[3]))
    layer_out = (ours + exchange(across, "z", 2).astype(f32)).astype(bf16)

    back, _ = barrier((back, across))
    gate_grad, up_grad = call_kernel(
        functools.partial(grads_kernel, nz, units), place, (gate_pre, up_pre, *back),
        [wide] * 2 + [whole((units, group_rows))] * nz,
        [struct((group_rows, local_hidden), bf16)] * 2, [wide] * 2, (steps,), act_scratch[::-1],
        (12 * act_bytes, 5 * act_bytes, act_bytes // 2),
    )
    over_x, _ = barrier((over_x, gate_grad))
    weight_grad = grad_half(0) + over_x.astype(f32)
    return layer_out, gate_grad, up_grad, weight_grad


def column_span(width):
    return max((s for s in range(128, 641, 128) if width % s == 0), default=0)


def body(gate_pre, up_pre, down_codes, down_scales, cotangent):
    group_rows, local_hidden = gate_pre.shape
    owned, width = down_codes.shape
    nz, nx, ny, nc = (lax.axis_size(name) for name in ("z", "x", "y", "c"))
    rows = cotangent.shape[0]
    units = nx * owned
    total_tokens = group_rows * nz * nx

    gate_value = gate_pre.astype(jnp.float32)
    up_value = up_pre.astype(jnp.float32)
    sigmoid_gate = jax.nn.sigmoid(gate_value)
    activated = gate_value * sigmoid_gate
    hidden = (activated * up_value).astype(jnp.bfloat16)

    sent = hidden.T.reshape(nz, units, group_rows)
    columns = lax.all_to_all(sent, "z", 0, 0, tiled=True) if nz > 1 else sent

    line = lax.all_gather(cotangent, ("z", "y"), axis=0)
    both = gather_pair(line, "c")
    received = jnp.moveaxis(both, 0, 1).reshape(nz, group_rows, width)

    weight = gather_pair(dequantize(down_codes, down_scales), "x").reshape(units, width)

    partial_out = lax.dot_general(
        columns, weight, (((1,), (0,)), ((), ())), preferred_element_type=jnp.float32
    ).astype(jnp.bfloat16)
    partial_out = partial_out.reshape(nz, ny, nc, rows, width)
    over_c = scatter_sum(jnp.moveaxis(partial_out, 2, 0), "c")
    over_y = scatter_sum(jnp.moveaxis(over_c.astype(jnp.bfloat16), 1, 0), "y")
    layer_out = scatter_sum(over_y.astype(jnp.bfloat16), "z").astype(jnp.bfloat16)

    dcolumns = lax.dot_general(
        weight, received, (((1,), (2,)), ((), ())), preferred_element_type=jnp.float32
    ).astype(jnp.bfloat16)
    dcolumns = jnp.moveaxis(dcolumns, 1, 0)
    back = lax.all_to_all(dcolumns, "z", 0, 0, tiled=True) if nz > 1 else dcolumns
    dhidden = back.reshape(local_hidden, group_rows).T.astype(jnp.float32)
    gate_grad = (
        dhidden * up_value * sigmoid_gate * (1.0 + gate_value * (1.0 - sigmoid_gate))
    ).astype(jnp.bfloat16)
    up_grad = (dhidden * activated).astype(jnp.bfloat16)

    partial_grad = lax.dot_general(
        columns, received, (((0, 2), (0, 1)), ((), ())), preferred_element_type=jnp.float32
    )
    weight_grad = scatter_sum(partial_grad.reshape(nx, owned, width), "x") * float(total_tokens) ** (-0.5)
    return layer_out, gate_grad, up_grad, weight_grad


def outer_split(mesh, tokens, hidden, width):
    dp, tensor = mesh.shape["dp"], mesh.shape["tensor"]

    def rows_sent(nz):
        moved = 2 * (tokens // dp) * (hidden // tensor) / width if nz > 1 else 0
        return 2 * hidden // (tensor * nz) + 2 * tokens * nz // dp + moved

    return min((nz for nz in range(1, dp + 1) if dp % nz == 0), key=rows_sent)


def solution(mesh):
    def call(gate_pre, up_pre, down_codes, down_scales, cotangent):
        tokens, hidden = gate_pre.shape
        nz = outer_split(mesh, tokens, hidden, cotangent.shape[1])
        dp, tensor = mesh.shape["dp"], mesh.shape["tensor"]
        fine = Mesh(mesh.devices.reshape(nz, dp // nz, tensor // 2, 2), ("z", "x", "y", "c"))
        act = P(("z", "x"), ("y", "c"))
        weight = P(("y", "c", "z", "x"), None)
        layer = P(("z", "x", "y", "c"), None)
        owned = hidden // (dp * tensor)
        rows = tokens // (dp * tensor)
        pairs = fine.shape["x"] == 2 and fine.shape["y"] == 2 and nz == 4
        aligned = owned % 16 == 0 and rows % 16 == 0 and column_span(hidden // tensor)
        nblocks = down_scales.shape[1]
        blocks = nblocks > 2 and cotangent.shape[1] // nblocks % 128 == 0
        return jax.shard_map(
            paired_body if pairs and aligned and blocks else body,
            mesh=fine,
            in_specs=(act, act, weight, weight, layer),
            out_specs=(layer, act, act, weight),
            check_vma=False,
        )(gate_pre, up_pre, down_codes, down_scales, cotangent)

    return call
```

profile of v0, /device:TPU:0, one launch (start us, length us, event | category | flops | bytes accessed | tf_op | source)
XLA Modules:
  0.0 141.1 jit_solution(17999917176600348054)
XLA Ops:
  0.6 4.1 %collective-permute-start = (bf16[64,2560]{1,0:T(8,128)(2,1)}, bf16[64,2560]{1,0:T(8,128)(2,1)S(1)}, u32[]{:S(2)}, u32[]{:S(2)}) collective-permute-start(bf16[64,2560]{1,0:T(8,128)(2,1)} %refs_0_.1), channel_id=1, source_target_pairs={{0,16},{8,24},{16,0},{24,8},{1,17},{9,25},{17,1},{25,9},{2,18},{10... | collective-permute-start | bytes 983048 | tf_op jit(solution)/shard_map/ppermute | solution.py:47
  4.7 1.6 %collective-permute-start.1 = (bf16[64,2560]{1,0:T(8,128)(2,1)}, bf16[64,2560]{1,0:T(8,128)(2,1)S(1)}, u32[]{:S(2)}, u32[]{:S(2)}) collective-permute-start(bf16[64,2560]{1,0:T(8,128)(2,1)} %refs_0_.1), channel_id=1, source_target_pairs={{0,8},{8,0},{16,24},{24,16},{1,9},{9,1},{17,25},{25,17},{2,10},{10... | collective-permute-start | bytes 983048 | tf_op jit(solution)/shard_map/ppermute | solution.py:47
  6.3 1.5 %collective-permute-start.2 = (bf16[64,2560]{1,0:T(8,128)(2,1)}, bf16[64,2560]{1,0:T(8,128)(2,1)S(1)}, u32[]{:S(2)}, u32[]{:S(2)}) collective-permute-start(bf16[64,2560]{1,0:T(8,128)(2,1)} %refs_0_.1), channel_id=1, source_target_pairs={{0,2},{2,0},{1,3},{3,1},{4,6},{6,4},{5,7},{7,5},{8,10},{10,8},{9,1... | collective-permute-start | bytes 983048 | tf_op jit(solution)/shard_map/ppermute | solution.py:47
  7.8 0.9 copy.9.scales
  8.8 1.6 %copy-done.3 = bf16[400,2560]{1,0:T(8,128)(2,1)S(1)} copy-done((bf16[400,2560]{1,0:T(8,128)(2,1)S(1)}, bf16[400,2560]{1,0:T(8,128)(2,1)}, u32[]{:S(2)}) %copy-start.3) | copy-done | bytes 2048024
  10.4 1.1 shard_map.85
  11.5 1.6 %collective-permute-start.7 = (bf16[400,1536]{1,0:T(8,128)(2,1)S(1)}, bf16[400,1536]{1,0:T(8,128)(2,1)S(1)}, u32[]{:S(2)}, u32[]{:S(2)}) collective-permute-start(bf16[400,1536]{1,0:T(8,128)(2,1)S(1)} %get-tuple-element.69.own_a), channel_id=1, source_target_pairs={{0,4},{4,0},{1,5},{5,1},{2,6},{6,2},{3,7},{7,3},{8,12},{12,8},{9,1... | collective-permute-start | bytes 3686408 | tf_op jit(solution)/shard_map/ppermute | solution.py:47
  13.1 1.4 %copy-done.1 = bf16[256,3200]{1,0:T(8,128)(2,1)S(1)} copy-done((bf16[256,3200]{1,0:T(8,128)(2,1)S(1)}, bf16[256,3200]{1,0:T(8,128)(2,1)}, u32[]{:S(2)}) %copy-start.1) | copy-done | bytes 1638424
  14.5 2.8 %shard_map.84 = (bf16[800,256]{1,0:T(8,128)(2,1)S(1)}, bf16[800,256]{1,0:T(8,128)(2,1)S(1)}, bf16[800,256]{1,0:T(8,128)(2,1)S(1)}, bf16[800,256]{1,0:T(8,128)(2,1)S(1)}) custom-call(s32[4]{0:T(128)S(1)} %pad_add_fusion.place, bf16[256,3200]{1,0:T(8,128)(2,1)S(1)} %copy-done, bf16[256,3200]{1,0:T(8,128)(2,1)S(1)} %copy-done.1), custom_call_target="tpu_custom_call" | custom-call | flops 6553600 | bytes 4915200 | tf_op jit(solution)/shard_map/pallas_call | solution.py:52
  17.4 2.4 %collective-permute-done.refs_3_ = bf16[64,2560]{1,0:T(8,128)(2,1)S(1)} collective-permute-done((bf16[64,2560]{1,0:T(8,128)(2,1)}, bf16[64,2560]{1,0:T(8,128)(2,1)S(1)}, u32[]{:S(2)}, u32[]{:S(2)}) %collective-permute-start) | collective-permute-done | bytes 327712 | tf_op jit(solution)/shard_map/ppermute | solution.py:47
  20.3 1.6 %collective-permute-start.5 = (bf16[2,64,2560]{2,1,0:T(8,128)(2,1)S(1)}, bf16[2,64,2560]{2,1,0:T(8,128)(2,1)S(1)}, u32[]{:S(2)}, u32[]{:S(2)}) collective-permute-start(bf16[2,64,2560]{2,1,0:T(8,128)(2,1)S(1)} %pad_maximum_fusion.2), channel_id=1, source_target_pairs={{0,2},{2,0},{1,3},{3,1},{4,6},{6,4},{5,7},{7,5},{8,10},{10,8},{9,1... | collective-permute-start | bytes 1966088 | tf_op jit(solution)/shard_map/ppermute | solution.py:47
  21.9 1.3 collective-permute-start.6
  23.2 2.4 %collective-permute-start.4 = (bf16[64,2560]{1,0:T(8,128)(2,1)S(1)}, bf16[64,2560]{1,0:T(8,128)(2,1)S(1)}, u32[]{:S(2)}, u32[]{:S(2)}) collective-permute-start(bf16[64,2560]{1,0:T(8,128)(2,1)S(1)} %collective-permute-done.refs_3_), channel_id=1, source_target_pairs={{0,8},{8,0},{16,24},{24,16},{1,9},{9,1},{17,25},{25,17},{2,10},{10... | collective-permute-start | bytes 983048 | tf_op jit(solution)/shard_map/ppermute | solution.py:47
  25.7 13.7 %collective-permute-done.4.refs_1_ = bf16[64,2560]{1,0:T(8,128)(2,1)S(1)} collective-permute-done((bf16[64,2560]{1,0:T(8,128)(2,1)S(1)}, bf16[64,2560]{1,0:T(8,128)(2,1)S(1)}, u32[]{:S(2)}, u32[]{:S(2)}) %collective-permute-start.4) | collective-permute-done | bytes 327712 | tf_op jit(solution)/shard_map/ppermute | solution.py:47
  39.4 1.5 %collective-permute-start.12 = (bf16[400,1024]{1,0:T(8,128)(2,1)S(1)}, bf16[400,1024]{1,0:T(8,128)(2,1)S(1)}, u32[]{:S(2)}, u32[]{:S(2)}) collective-permute-start(bf16[400,1024]{1,0:T(8,128)(2,1)S(1)} %get-tuple-element.78.own_b), channel_id=1, source_target_pairs={{0,4},{4,0},{1,5},{5,1},{2,6},{6,2},{3,7},{7,3},{8,12},{12,8},{9,1... | collective-permute-start | bytes 2457608 | tf_op jit(solution)/shard_map/ppermute | solution.py:47
  40.9 2.3 %collective-permute-done.6.refs_1_ = bf16[800,256]{1,0:T(8,128)(2,1)S(1)} collective-permute-done((bf16[800,256]{1,0:T(8,128)(2,1)S(1)}, bf16[800,256]{1,0:T(8,128)(2,1)S(1)}, u32[]{:S(2)}, u32[]{:S(2)}) %collective-permute-start.6) | collective-permute-done | bytes 409632 | tf_op jit(solution)/shard_map/ppermute | solution.py:47
  43.3 2.3 %collective-permute-start.10 = (bf16[800,256]{1,0:T(8,128)(2,1)S(1)}, bf16[800,256]{1,0:T(8,128)(2,1)S(1)}, u32[]{:S(2)}, u32[]{:S(2)}) collective-permute-start(bf16[800,256]{1,0:T(8,128)(2,1)S(1)} %get-tuple-element.76), channel_id=1, source_target_pairs={{0,24},{8,16},{16,8},{24,0},{1,25},{9,17},{17,9},{25,1},{2,26},{10... | collective-permute-start | bytes 1228808 | tf_op jit(solution)/shard_map/ppermute | solution.py:47
  46.1 12.8 %collective-permute-done.12.other_b = bf16[400,1024]{1,0:T(8,128)(2,1)S(1)} collective-permute-done((bf16[400,1024]{1,0:T(8,128)(2,1)S(1)}, bf16[400,1024]{1,0:T(8,128)(2,1)S(1)}, u32[]{:S(2)}, u32[]{:S(2)}) %collective-permute-start.12) | collective-permute-done | bytes 819232 | tf_op jit(solution)/shard_map/ppermute | solution.py:47
  58.9 7.0 %collective-permute-done.11.refs_3_ = bf16[800,256]{1,0:T(8,128)(2,1)S(1)} collective-permute-done((bf16[800,256]{1,0:T(8,128)(2,1)S(1)}, bf16[800,256]{1,0:T(8,128)(2,1)S(1)}, u32[]{:S(2)}, u32[]{:S(2)}) %collective-permute-start.11) | collective-permute-done | bytes 409632 | tf_op jit(solution)/shard_map/ppermute | solution.py:47
  65.9 0.8 shard_map.87
  66.8 1.1 shard_map.86
  67.9 0.7 shard_map.88
  68.6 0.7 shard_map.89
  69.4 3.3 %convolution_convert_fusion = bf16[512,2560]{1,0:T(8,128)(2,1)S(1)} fusion(bf16[512,800]{1,0:T(8,128)(2,1)S(1)} %get-tuple-element.99, bf16[800,2560]{1,0:T(8,128)(2,1)S(1)} %shard_map.87), kind=kOutput, calls=%fused_computation.5 | convolution fusion | flops 2098462720 | bytes 7536640 | tf_op jit(solution)/shard_map/dot_general | solution.py:174
  72.7 0.5 collective-permute-start.15
  73.2 1.3 fusion.14
  74.5 1.2 fusion.31
  75.7 1.2 fusion.2
  76.9 0.6 collective-permute-start.18
  77.5 1.2 fusion.17
  78.8 2.2 %collective-permute-start.20 = (bf16[800,256]{1,0:T(8,128)(2,1)S(1)}, bf16[800,256]{1,0:T(8,128)(2,1)S(1)}, u32[]{:S(2)}, u32[]{:S(2)}) collective-permute-start(bf16[800,256]{1,0:T(8,128)(2,1)S(1)} %fusion.17), channel_id=1, source_target_pairs={{0,24},{8,16},{16,8},{24,0},{1,25},{9,17},{17,9},{25,1},{2,26},{10... | collective-permute-start | bytes 1228808 | tf_op jit(solution)/shard_map/ppermute | solution.py:47
  81.0 1.3 fusion.23
  82.3 0.8 collective-permute-start.22
  83.1 1.3 fusion.20.refs_0_
  84.4 2.9 %convert_add_fusion = f32[512,2560]{1,0:T(8,128)S(1)} fusion(bf16[512,2560]{1,0:T(8,128)(2,1)S(1)} %collective-permute-done.15, bf16[512,800]{1,0:T(8,128)(2,1)S(1)} %get-tuple-element.98, bf16[800,2560]{1,0:T(8,128)(2,1)S(1)} %shard_map.87), kind=kOutput, calls=%fused_computation | convolution fusion | flops 2102394880 | bytes 12779520 | tf_op jit(solution)/shard_map/dot_general | solution.py:174
  87.7 0.5 collective-permute-start.17
  88.2 1.2 fusion.32
  89.4 1.6 %collective-permute-start.23 = (bf16[400,2560]{1,0:T(8,128)(2,1)S(1)}, bf16[400,2560]{1,0:T(8,128)(2,1)S(1)}, u32[]{:S(2)}, u32[]{:S(2)}) collective-permute-start(bf16[400,2560]{1,0:T(8,128)(2,1)S(1)} %fusion.2), channel_id=1, source_target_pairs={{0,4},{4,0},{1,5},{5,1},{2,6},{6,2},{3,7},{7,3},{8,12},{12,8},{9,1... | collective-permute-start | bytes 6144008 | tf_op jit(solution)/shard_map/ppermute | solution.py:47
  91.0 1.2 fusion
  92.3 11.3 %collective-permute-done.17 = bf16[2,64,2560]{2,1,0:T(8,128)(2,1)S(1)} collective-permute-done((bf16[2,64,2560]{2,1,0:T(8,128)(2,1)S(1)}, bf16[2,64,2560]{2,1,0:T(8,128)(2,1)S(1)}, u32[]{:S(2)}, u32[]{:S(2)}) %collective-permute-start.17) | collective-permute-done | bytes 655392 | tf_op jit(solution)/shard_map/ppermute | solution.py:47
  104.2 2.6 %collective-permute-done.18.refs_2_ = bf16[800,256]{1,0:T(8,128)(2,1)S(1)} collective-permute-done((bf16[800,256]{1,0:T(8,128)(2,1)S(1)}, bf16[800,256]{1,0:T(8,128)(2,1)S(1)}, u32[]{:S(2)}, u32[]{:S(2)}) %collective-permute-start.18) | collective-permute-done | bytes 409632 | tf_op jit(solution)/shard_map/ppermute | solution.py:47
  106.8 11.7 %collective-permute-done.16 = bf16[2,64,2560]{2,1,0:T(8,128)(2,1)S(1)} collective-permute-done((bf16[2,64,2560]{2,1,0:T(8,128)(2,1)S(1)}, bf16[2,64,2560]{2,1,0:T(8,128)(2,1)S(1)}, u32[]{:S(2)}, u32[]{:S(2)}) %collective-permute-start.16) | collective-permute-done | bytes 655392 | tf_op jit(solution)/shard_map/ppermute | solution.py:47
  118.6 6.1 %collective-permute-done.19 = bf16[2,64,2560]{2,1,0:T(8,128)(2,1)S(1)} collective-permute-done((bf16[2,64,2560]{2,1,0:T(8,128)(2,1)S(1)}, bf16[2,64,2560]{2,1,0:T(8,128)(2,1)S(1)}, u32[]{:S(2)}, u32[]{:S(2)}) %collective-permute-start.19) | collective-permute-done | bytes 655392 | tf_op jit(solution)/shard_map/ppermute | solution.py:47
  125.0 5.7 %shard_map.90 = (bf16[256,3200]{1,0:T(8,128)(2,1)}, bf16[256,3200]{1,0:T(8,128)(2,1)}) custom-call(s32[4]{0:T(128)S(1)} %pad_add_fusion.place, bf16[256,3200]{1,0:T(8,128)(2,1)S(1)} %copy-done, bf16[256,3200]{1,0:T(8,128)(2,1)S(1)} %copy-done.2, bf16[800,256]{1,0:T(8,128)(2,1)S(1)} %fusion.20.refs_0_, bf16[800,256]{1,0:T(8,128)(2,1)S(1)} %collective-permute-done.22.refs_1_, ...), custom_call_target="tpu_custom_call" | custom-call | flops 19660800 | bytes 8192000 | tf_op jit(solution)/shard_map/pallas_call | solution.py:52
  130.7 4.2 %collective-permute-done.23 = bf16[400,2560]{1,0:T(8,128)(2,1)S(1)} collective-permute-done((bf16[400,2560]{1,0:T(8,128)(2,1)S(1)}, bf16[400,2560]{1,0:T(8,128)(2,1)S(1)}, u32[]{:S(2)}, u32[]{:S(2)}) %collective-permute-start.23) | collective-permute-done | bytes 2048032 | tf_op jit(solution)/shard_map/ppermute | solution.py:47
  134.9 2.5 %convert_add_fusion.1 = f32[400,2560]{1,0:T(8,128)} fusion(f32[400,2560]{1,0:T(8,128)S(1)} %fusion, bf16[400,2560]{1,0:T(8,128)(2,1)S(1)} %collective-permute-done.23), kind=kLoop, calls=%fused_computation.8 | loop fusion | flops 2048000 | bytes 10240000 | tf_op jit(solution)/shard_map/add | solution.py:304
  137.4 3.0 %collective-permute-done.21 = bf16[64,2560]{1,0:T(8,128)(2,1)S(1)} collective-permute-done((bf16[64,2560]{1,0:T(8,128)(2,1)S(1)}, bf16[64,2560]{1,0:T(8,128)(2,1)S(1)}, u32[]{:S(2)}, u32[]{:S(2)}) %collective-permute-start.21) | collective-permute-done | bytes 327712 | tf_op jit(solution)/shard_map/ppermute | solution.py:47
  140.3 0.8 fusion.29
  (40 shorter events, 2.6 us)
Async XLA Ops:
  0.6 12.5 %copy-start = (bf16[256,3200]{1,0:T(8,128)(2,1)S(1)}, bf16[256,3200]{1,0:T(8,128)(2,1)}, u32[]{:S(2)}) copy-start(bf16[256,3200]{1,0:T(8,128)(2,1)} %gate.3) | copy-start | bytes 4915204
  0.6 19.2 %collective-permute-start = (bf16[64,2560]{1,0:T(8,128)(2,1)}, bf16[64,2560]{1,0:T(8,128)(2,1)S(1)}, u32[]{:S(2)}, u32[]{:S(2)}) collective-permute-start(bf16[64,2560]{1,0:T(8,128)(2,1)} %refs_0_.1), channel_id=1, source_target_pairs={{0,16},{8,24},{16,0},{24,8},{1,17},{9,25},{17,1},{25,9},{2,18},{10... | collective-permute-start | bytes 983048 | tf_op jit(solution)/shard_map/ppermute | solution.py:47
  4.7 15.2 %collective-permute-start.1 = (bf16[64,2560]{1,0:T(8,128)(2,1)}, bf16[64,2560]{1,0:T(8,128)(2,1)S(1)}, u32[]{:S(2)}, u32[]{:S(2)}) collective-permute-start(bf16[64,2560]{1,0:T(8,128)(2,1)} %refs_0_.1), channel_id=1, source_target_pairs={{0,8},{8,0},{16,24},{24,16},{1,9},{9,1},{17,25},{25,17},{2,10},{10... | collective-permute-start | bytes 983048 | tf_op jit(solution)/shard_map/ppermute | solution.py:47
  6.3 13.7 %collective-permute-start.2 = (bf16[64,2560]{1,0:T(8,128)(2,1)}, bf16[64,2560]{1,0:T(8,128)(2,1)S(1)}, u32[]{:S(2)}, u32[]{:S(2)}) collective-permute-start(bf16[64,2560]{1,0:T(8,128)(2,1)} %refs_0_.1), channel_id=1, source_target_pairs={{0,2},{2,0},{1,3},{3,1},{4,6},{6,4},{5,7},{7,5},{8,10},{10,8},{9,1... | collective-permute-start | bytes 983048 | tf_op jit(solution)/shard_map/ppermute | solution.py:47
  7.8 12.1 %collective-permute-start.3 = (bf16[64,2560]{1,0:T(8,128)(2,1)}, bf16[64,2560]{1,0:T(8,128)(2,1)S(1)}, u32[]{:S(2)}, u32[]{:S(2)}) collective-permute-start(bf16[64,2560]{1,0:T(8,128)(2,1)} %refs_0_.1), channel_id=1, source_target_pairs={{0,1},{1,0},{2,3},{3,2},{4,5},{5,4},{6,7},{7,6},{8,9},{9,8},{10,11... | collective-permute-start | bytes 983048 | tf_op jit(solution)/shard_map/ppermute | solution.py:47
  8.8 1.6 %copy-start.3 = (bf16[400,2560]{1,0:T(8,128)(2,1)S(1)}, bf16[400,2560]{1,0:T(8,128)(2,1)}, u32[]{:S(2)}) copy-start(bf16[400,2560]{1,0:T(8,128)(2,1)} %codes.1) | copy-start | bytes 6144004
  11.5 31.6 %collective-permute-start.7 = (bf16[400,1536]{1,0:T(8,128)(2,1)S(1)}, bf16[400,1536]{1,0:T(8,128)(2,1)S(1)}, u32[]{:S(2)}, u32[]{:S(2)}) collective-permute-start(bf16[400,1536]{1,0:T(8,128)(2,1)S(1)} %get-tuple-element.69.own_a), channel_id=1, source_target_pairs={{0,4},{4,0},{1,5},{5,1},{2,6},{6,2},{3,7},{7,3},{8,12},{12,8},{9,1... | collective-permute-start | bytes 3686408 | tf_op jit(solution)/shard_map/ppermute | solution.py:47
  13.1 1.4 %copy-start.1 = (bf16[256,3200]{1,0:T(8,128)(2,1)S(1)}, bf16[256,3200]{1,0:T(8,128)(2,1)}, u32[]{:S(2)}) copy-start(bf16[256,3200]{1,0:T(8,128)(2,1)} %up.3) | copy-start | bytes 4915204
  20.1 23.1 %collective-permute-start.8 = (bf16[3,64,2560]{2,1,0:T(8,128)(2,1)S(1)}, bf16[3,64,2560]{2,1,0:T(8,128)(2,1)S(1)}, u32[]{:S(2)}, u32[]{:S(2)}) collective-permute-start(bf16[3,64,2560]{2,1,0:T(8,128)(2,1)S(1)} %pad_maximum_fusion), channel_id=1, source_target_pairs={{0,1},{1,0},{2,3},{3,2},{4,5},{5,4},{6,7},{7,6},{8,9},{9,8},{10,11... | collective-permute-start | bytes 2949128 | tf_op jit(solution)/shard_map/ppermute | solution.py:47
  20.3 22.9 %collective-permute-start.5 = (bf16[2,64,2560]{2,1,0:T(8,128)(2,1)S(1)}, bf16[2,64,2560]{2,1,0:T(8,128)(2,1)S(1)}, u32[]{:S(2)}, u32[]{:S(2)}) collective-permute-start(bf16[2,64,2560]{2,1,0:T(8,128)(2,1)S(1)} %pad_maximum_fusion.2), channel_id=1, source_target_pairs={{0,2},{2,0},{1,3},{3,1},{4,6},{6,4},{5,7},{7,5},{8,10},{10,8},{9,1... | collective-permute-start | bytes 1966088 | tf_op jit(solution)/shard_map/ppermute | solution.py:47
  21.9 21.3 %collective-permute-start.6 = (bf16[800,256]{1,0:T(8,128)(2,1)S(1)}, bf16[800,256]{1,0:T(8,128)(2,1)S(1)}, u32[]{:S(2)}, u32[]{:S(2)}) collective-permute-start(bf16[800,256]{1,0:T(8,128)(2,1)S(1)} %get-tuple-element.68), channel_id=1, source_target_pairs={{0,16},{8,24},{16,0},{24,8},{1,17},{9,25},{17,1},{25,9},{2,18},{10... | collective-permute-start | bytes 1228808 | tf_op jit(solution)/shard_map/ppermute | solution.py:47
  23.2 16.2 %collective-permute-start.4 = (bf16[64,2560]{1,0:T(8,128)(2,1)S(1)}, bf16[64,2560]{1,0:T(8,128)(2,1)S(1)}, u32[]{:S(2)}, u32[]{:S(2)}) collective-permute-start(bf16[64,2560]{1,0:T(8,128)(2,1)S(1)} %collective-permute-done.refs_3_), channel_id=1, source_target_pairs={{0,8},{8,0},{16,24},{24,16},{1,9},{9,1},{17,25},{25,17},{2,10},{10... | collective-permute-start | bytes 983048 | tf_op jit(solution)/shard_map/ppermute | solution.py:47
  39.4 19.5 %collective-permute-start.12 = (bf16[400,1024]{1,0:T(8,128)(2,1)S(1)}, bf16[400,1024]{1,0:T(8,128)(2,1)S(1)}, u32[]{:S(2)}, u32[]{:S(2)}) collective-permute-start(bf16[400,1024]{1,0:T(8,128)(2,1)S(1)} %get-tuple-element.78.own_b), channel_id=1, source_target_pairs={{0,4},{4,0},{1,5},{5,1},{2,6},{6,2},{3,7},{7,3},{8,12},{12,8},{9,1... | collective-permute-start | bytes 2457608 | tf_op jit(solution)/shard_map/ppermute | solution.py:47
  43.3 24.7 %copy-start.4 = (bf16[64,2560]{1,0:T(8,128)(2,1)S(1)}, bf16[64,2560]{1,0:T(8,128)(2,1)}, u32[]{:S(2)}) copy-start(bf16[64,2560]{1,0:T(8,128)(2,1)} %refs_0_.1) | copy-start | bytes 983044
  43.3 24.6 %collective-permute-start.13 = (bf16[3,64,2560]{2,1,0:T(8,128)(2,1)S(1)}, bf16[3,64,2560]{2,1,0:T(8,128)(2,1)S(1)}, u32[]{:S(2)}, u32[]{:S(2)}) collective-permute-start(bf16[3,64,2560]{2,1,0:T(8,128)(2,1)S(1)} %pad_maximum_fusion.1), channel_id=1, source_target_pairs={{0,1},{1,0},{2,3},{3,2},{4,5},{5,4},{6,7},{7,6},{8,9},{9,8},{10,11... | collective-permute-start | bytes 2949128 | tf_op jit(solution)/shard_map/ppermute | solution.py:47
  43.3 15.6 %collective-permute-start.10 = (bf16[800,256]{1,0:T(8,128)(2,1)S(1)}, bf16[800,256]{1,0:T(8,128)(2,1)S(1)}, u32[]{:S(2)}, u32[]{:S(2)}) collective-permute-start(bf16[800,256]{1,0:T(8,128)(2,1)S(1)} %get-tuple-element.76), channel_id=1, source_target_pairs={{0,24},{8,16},{16,8},{24,0},{1,25},{9,17},{17,9},{25,1},{2,26},{10... | collective-permute-start | bytes 1228808 | tf_op jit(solution)/shard_map/ppermute | solution.py:47
  45.6 20.3 %collective-permute-start.11 = (bf16[800,256]{1,0:T(8,128)(2,1)S(1)}, bf16[800,256]{1,0:T(8,128)(2,1)S(1)}, u32[]{:S(2)}, u32[]{:S(2)}) collective-permute-start(bf16[800,256]{1,0:T(8,128)(2,1)S(1)} %get-tuple-element.77), channel_id=1, source_target_pairs={{0,8},{8,0},{16,24},{24,16},{1,9},{9,1},{17,25},{25,17},{2,10},{10... | collective-permute-start | bytes 1228808 | tf_op jit(solution)/shard_map/ppermute | solution.py:47
  45.6 13.3 %collective-permute-start.9 = (bf16[64,2560]{1,0:T(8,128)(2,1)S(1)}, bf16[64,2560]{1,0:T(8,128)(2,1)S(1)}, u32[]{:S(2)}, u32[]{:S(2)}) collective-permute-start(bf16[64,2560]{1,0:T(8,128)(2,1)S(1)} %collective-permute-done.4.refs_1_), channel_id=1, source_target_pairs={{0,2},{2,0},{1,3},{3,1},{4,6},{6,4},{5,7},{7,5},{8,10},{10,8},{9,1... | collective-permute-start | bytes 983048 | tf_op jit(solution)/shard_map/ppermute | solution.py:47
  65.9 2.7 %collective-permute-start.14 = (bf16[64,2560]{1,0:T(8,128)(2,1)S(1)}, bf16[64,2560]{1,0:T(8,128)(2,1)S(1)}, u32[]{:S(2)}, u32[]{:S(2)}) collective-permute-start(bf16[64,2560]{1,0:T(8,128)(2,1)S(1)} %collective-permute-done.9.refs_2_), channel_id=1, source_target_pairs={{0,1},{1,0},{2,3},{3,2},{4,5},{5,4},{6,7},{7,6},{8,9},{9,8},{10,11... | collective-permute-start | bytes 983048 | tf_op jit(solution)/shard_map/ppermute | solution.py:47
  72.7 11.7 %collective-permute-start.15 = (bf16[512,2560]{1,0:T(8,128)(2,1)S(1)}, bf16[512,2560]{1,0:T(8,128)(2,1)S(1)}, u32[]{:S(2)}, u32[]{:S(2)}) collective-permute-start(bf16[512,2560]{1,0:T(8,128)(2,1)S(1)} %convolution_convert_fusion), channel_id=1, source_target_pairs={{0,1},{1,0},{2,3},{3,2},{4,5},{5,4},{6,7},{7,6},{8,9},{9,8},{10,11... | collective-permute-start | bytes 7864328 | tf_op jit(solution)/shard_map/ppermute | solution.py:47
  76.9 29.8 %collective-permute-start.18 = (bf16[800,256]{1,0:T(8,128)(2,1)S(1)}, bf16[800,256]{1,0:T(8,128)(2,1)S(1)}, u32[]{:S(2)}, u32[]{:S(2)}) collective-permute-start(bf16[800,256]{1,0:T(8,128)(2,1)S(1)} %fusion.14), channel_id=1, source_target_pairs={{0,16},{8,24},{16,0},{24,8},{1,17},{9,25},{17,1},{25,9},{2,18},{10... | collective-permute-start | bytes 1228808 | tf_op jit(solution)/shard_map/ppermute | solution.py:47
  78.8 46.1 %collective-permute-start.20 = (bf16[800,256]{1,0:T(8,128)(2,1)S(1)}, bf16[800,256]{1,0:T(8,128)(2,1)S(1)}, u32[]{:S(2)}, u32[]{:S(2)}) collective-permute-start(bf16[800,256]{1,0:T(8,128)(2,1)S(1)} %fusion.17), channel_id=1, source_target_pairs={{0,24},{8,16},{16,8},{24,0},{1,25},{9,17},{17,9},{25,1},{2,26},{10... | collective-permute-start | bytes 1228808 | tf_op jit(solution)/shard_map/ppermute | solution.py:47
  82.3 42.7 %collective-permute-start.22 = (bf16[800,256]{1,0:T(8,128)(2,1)S(1)}, bf16[800,256]{1,0:T(8,128)(2,1)S(1)}, u32[]{:S(2)}, u32[]{:S(2)}) collective-permute-start(bf16[800,256]{1,0:T(8,128)(2,1)S(1)} %fusion.23), channel_id=1, source_target_pairs={{0,8},{8,0},{16,24},{24,16},{1,9},{9,1},{17,25},{25,17},{2,10},{10... | collective-permute-start | bytes 1228808 | tf_op jit(solution)/shard_map/ppermute | solution.py:47
  87.7 15.9 %collective-permute-start.17 = (bf16[2,64,2560]{2,1,0:T(8,128)(2,1)S(1)}, bf16[2,64,2560]{2,1,0:T(8,128)(2,1)S(1)}, u32[]{:S(2)}, u32[]{:S(2)}) collective-permute-start(bf16[2,64,2560]{2,1,0:T(8,128)(2,1)S(1)} %get-tuple-element.119), channel_id=1, source_target_pairs={{0,2},{2,0},{1,3},{3,1},{4,6},{6,4},{5,7},{7,5},{8,10},{10,8},{9,1... | collective-permute-start | bytes 1966088 | tf_op jit(solution)/shard_map/ppermute | solution.py:47
  89.4 45.5 %collective-permute-start.23 = (bf16[400,2560]{1,0:T(8,128)(2,1)S(1)}, bf16[400,2560]{1,0:T(8,128)(2,1)S(1)}, u32[]{:S(2)}, u32[]{:S(2)}) collective-permute-start(bf16[400,2560]{1,0:T(8,128)(2,1)S(1)} %fusion.2), channel_id=1, source_target_pairs={{0,4},{4,0},{1,5},{5,1},{2,6},{6,2},{3,7},{7,3},{8,12},{12,8},{9,1... | collective-permute-start | bytes 6144008 | tf_op jit(solution)/shard_map/ppermute | solution.py:47
  103.6 14.9 %collective-permute-start.16 = (bf16[2,64,2560]{2,1,0:T(8,128)(2,1)S(1)}, bf16[2,64,2560]{2,1,0:T(8,128)(2,1)S(1)}, u32[]{:S(2)}, u32[]{:S(2)}) collective-permute-start(bf16[2,64,2560]{2,1,0:T(8,128)(2,1)S(1)} %get-tuple-element.118), channel_id=1, source_target_pairs={{0,2},{2,0},{1,3},{3,1},{4,6},{6,4},{5,7},{7,5},{8,10},{10,8},{9,1... | collective-permute-start | bytes 1966088 | tf_op jit(solution)/shard_map/ppermute | solution.py:47
  104.1 20.9 %copy-start.2 = (bf16[256,3200]{1,0:T(8,128)(2,1)S(1)}, bf16[256,3200]{1,0:T(8,128)(2,1)}, u32[]{:S(2)}) copy-start(bf16[256,3200]{1,0:T(8,128)(2,1)} %up.3) | copy-start | bytes 4915204
  106.8 17.9 %collective-permute-start.19 = (bf16[2,64,2560]{2,1,0:T(8,128)(2,1)S(1)}, bf16[2,64,2560]{2,1,0:T(8,128)(2,1)S(1)}, u32[]{:S(2)}, u32[]{:S(2)}) collective-permute-start(bf16[2,64,2560]{2,1,0:T(8,128)(2,1)S(1)} %fusion.4), channel_id=1, source_target_pairs={{0,8},{8,0},{16,24},{24,16},{1,9},{9,1},{17,25},{25,17},{2,10},{10... | collective-permute-start | bytes 1966088 | tf_op jit(solution)/shard_map/ppermute | solution.py:47
  124.9 15.4 %collective-permute-start.21 = (bf16[64,2560]{1,0:T(8,128)(2,1)S(1)}, bf16[64,2560]{1,0:T(8,128)(2,1)S(1)}, u32[]{:S(2)}, u32[]{:S(2)}) collective-permute-start(bf16[64,2560]{1,0:T(8,128)(2,1)S(1)} %fusion.30), channel_id=1, source_target_pairs={{0,16},{8,24},{16,0},{24,8},{1,17},{9,25},{17,1},{25,9},{2,18},{10... | collective-permute-start | bytes 983048 | tf_op jit(solution)/shard_map/ppermute | solution.py:47
where the time goes:
time: 141 us
  waiting for transfers between devices  77.3 us (55%)
  starting transfers between devices  25.5 us (18%)
  matrix products  16.1 us (11%)
  Pallas kernels  13 us (9%)
  other arithmetic  4.36 us (3%)
  local copies, waits for them, and re-layouts  3.99 us (3%)
    ppermute x24, waiting for transfers between devices, exchange(): return lax.ppermute(value, axis, [(i, i ^ offset) for i in range(size)])  77.3 us
    ppermute x24, starting transfers between devices, exchange(): return lax.ppermute(value, axis, [(i, i ^ offset) for i in range(size)])  25.5 us
    dot_general x10, matrix products, matmul(): lax.dot_general(lhs, rhs, dims, preferred_element_type=jnp.float32)  16.1 us
    pallas_call x7, Pallas kernels, call_kernel(): pl.pallas_call(kernel, out_shape=out_shapes, grid_spec=pltpu.PrefetchScal...  13 us
    unnamed x11, local copies, waits for them, and re-layouts  3.91 us
  transfers between devices with their start and end apart: 24, of which 12 were waited for; matrix products, arithmetic and copies ran while one was open for 12% of the time, Pallas kernels for 9%

commit v1 on v0

--- a/solution.py
+++ b/solution.py
@@ -265,23 +265,30 @@
     factor = float(total_tokens) ** (-0.5)
 
 
-    def grad_half(r):
-        return (matmul(by_units[r], flat[0]) + matmul(by_units[2 + r], flat[1])) * factor
+    def grad_half(r, low=0, high=owned):
+        first, second = by_units[r][low:high], by_units[2 + r][low:high]
+        return (matmul(first, flat[0]) + matmul(second, flat[1])) * factor
 
     def back_of(k):
         rows_of_k = flat[k % 2][k // 2 * group_rows : (k // 2 + 1) * group_rows]
         return matmul(weight, rows_of_k, 1, 1, bf16)
 
-    over_c = exchange(matmul(send, weight, dtype=bf16), "c", 1)
-    back = [None, None, back_of(2), None]
-    back[2], flat = barrier((back[2], flat))
-    theirs = grad_half(1).astype(bf16)
+    far_back = back_of(2)
+    far_back, send = barrier((far_back, send))
+    given = matmul(send, weight, dtype=bf16)
+    given, flat = barrier((given, flat))
+    over_c = exchange(given, "c", 1)
+    early = owned // 96 * 16
+    theirs = [grad_half(1, 0, early).astype(bf16), grad_half(1, early, owned).astype(bf16)]
     theirs, keep, flat = barrier((theirs, keep, flat))
-    over_x = exchange(theirs, "x", 1)
+    over_x = [exchange(part, "x", 1) for part in theirs]
     kept = matmul(keep, weight, dtype=bf16)
-    back = [back_of(0), back_of(1), back[2], back_of(3)]
-    back = [back[0]] + [exchange(back[k], "z", k) for k in range(1, nz)]
+    kept, flat = barrier((kept, flat))
+    back = [back_of(0), exchange(back_of(1), "z", 1), exchange(far_back, "z", 2)]
+    last_back, _ = barrier((back_of(3), back[2]))
+    back.append(exchange(last_back, "z", 3))
     sums = (kept.astype(f32) + over_c.astype(f32)).reshape(2, nz, rows, width)
+    sums, over_x[0] = barrier((sums, over_x[0]))
     odd_y = exchange(sums[1, :2].astype(bf16), "y", 1)
     even_y = exchange(sums[1, 2:].astype(bf16), "y", 1)
     odd_sum = (sums[0, :2] + odd_y.astype(f32)).astype(bf16)
@@ -293,15 +300,14 @@
     across, back[3] = barrier((across, back[3]))
     layer_out = (ours + exchange(across, "z", 2).astype(f32)).astype(bf16)
 
-    back, _ = barrier((back, across))
+    weight_grad = grad_half(0) + jnp.concatenate(over_x).astype(f32)
+    back, weight_grad, _ = barrier((back, weight_grad, across))
     gate_grad, up_grad = call_kernel(
         functools.partial(grads_kernel, nz, units), place, (gate_pre, up_pre, *back),
         [wide] * 2 + [whole((units, group_rows))] * nz,
         [struct((group_rows, local_hidden), bf16)] * 2, [wide] * 2, (steps,), act_scratch[::-1],
         (12 * act_bytes, 5 * act_bytes, act_bytes // 2),
     )
-    over_x, _ = barrier((over_x, gate_grad))
-    weight_grad = grad_half(0) + over_x.astype(f32)
     return layer_out, gate_grad, up_grad, weight_grad
 
 

time: 141 us -> 146 us (1.035)
  starting transfers between devices: 25.5 us -> 29.1 us
  matrix products: 16.1 us -> 19.1 us
  other arithmetic: 4.36 us -> 2.71 us
    ppermute x24 -> x25, starting transfers between devices: 25.5 us -> 29.1 us  [exchange(): return lax.ppermute(value, axis, [(i, i ^ offset) for i in range(size)])]
    dot_general x10 -> x12, matrix products: 16.1 us -> 19.1 us  [matmul(): lax.dot_general(lhs, rhs, dims, preferred_element_type=jnp.float32)]
    add x1, other arithmetic: 2.5 us -> 0.74 us  [paired_body(): sums = (kept.astype(f32) + over_c.astype(f32)).reshape(2, nz, rows, width)]
    ppermute x24 -> x25, waiting for transfers between devices: 77.3 us -> 76.3 us  [exchange(): return lax.ppermute(value, axis, [(i, i ^ offset) for i in range(size)])]
  transfers between devices with their start and end apart: 24 -> 25, of which waited for: 12 -> 12; matrix products, arithmetic and copies ran while one was open for 12% -> 14% of each run, Pallas kernels for 9% -> 8%
where the time goes in v1:
time: 146 us; the launch traced here: 145 us
  waiting for transfers between devices  76.3 us (52%)
  starting transfers between devices  29.1 us (20%)
  matrix products  19.1 us (13%)
  Pallas kernels  13 us (9%)
  local copies, waits for them, and re-layouts  4.23 us (3%)
  other arithmetic  2.71 us (2%)
    ppermute x25, waiting for transfers between devices, exchange(): return lax.ppermute(value, axis, [(i, i ^ offset) for i in range(size)])  76.3 us
    ppermute x25, starting transfers between devices, exchange(): return lax.ppermute(value, axis, [(i, i ^ offset) for i in range(size)])  29.1 us
    dot_general x12, matrix products, matmul(): lax.dot_general(lhs, rhs, dims, preferred_element_type=jnp.float32)  19.1 us
    pallas_call x7, Pallas kernels, call_kernel(): pl.pallas_call(kernel, out_shape=out_shapes, grid_spec=pltpu.PrefetchScal...  13 us
    unnamed x11, local copies, waits for them, and re-layouts  4.13 us
  transfers between devices with their start and end apart: 25, of which 12 were waited for; matrix products, arithmetic and copies ran while one was open for 14% of the time, Pallas kernels for 8%

profile of v1, /device:TPU:0, one launch (start us, length us, event | category | flops | bytes accessed | tf_op | source)
XLA Modules:
  0.0 145.3 jit_solution(1101466264793021152)
XLA Ops:
  0.6 3.0 %collective-permute-start.2 = (bf16[64,2560]{1,0:T(8,128)(2,1)}, bf16[64,2560]{1,0:T(8,128)(2,1)S(1)}, u32[]{:S(2)}, u32[]{:S(2)}) collective-permute-start(bf16[64,2560]{1,0:T(8,128)(2,1)} %refs_0_.1), channel_id=1, source_target_pairs={{0,2},{2,0},{1,3},{3,1},{4,6},{6,4},{5,7},{7,5},{8,10},{10,8},{9,1... | collective-permute-start | bytes 983048 | tf_op jit(solution)/shard_map/ppermute | solution.py:47
  3.7 1.6 %collective-permute-start.1 = (bf16[64,2560]{1,0:T(8,128)(2,1)}, bf16[64,2560]{1,0:T(8,128)(2,1)S(1)}, u32[]{:S(2)}, u32[]{:S(2)}) collective-permute-start(bf16[64,2560]{1,0:T(8,128)(2,1)} %refs_0_.1), channel_id=1, source_target_pairs={{0,8},{8,0},{16,24},{24,16},{1,9},{9,1},{17,25},{25,17},{2,10},{10... | collective-permute-start | bytes 983048 | tf_op jit(solution)/shard_map/ppermute | solution.py:47
  5.2 2.6 %collective-permute-start = (bf16[64,2560]{1,0:T(8,128)(2,1)}, bf16[64,2560]{1,0:T(8,128)(2,1)S(1)}, u32[]{:S(2)}, u32[]{:S(2)}) collective-permute-start(bf16[64,2560]{1,0:T(8,128)(2,1)} %refs_0_.1), channel_id=1, source_target_pairs={{0,16},{8,24},{16,0},{24,8},{1,17},{9,25},{17,1},{25,9},{2,18},{10... | collective-permute-start | bytes 983048 | tf_op jit(solution)/shard_map/ppermute | solution.py:47
  7.8 0.9 copy.9.scales
  8.8 1.6 %copy-done.3 = bf16[400,2560]{1,0:T(8,128)(2,1)S(1)} copy-done((bf16[400,2560]{1,0:T(8,128)(2,1)S(1)}, bf16[400,2560]{1,0:T(8,128)(2,1)}, u32[]{:S(2)}) %copy-start.3) | copy-done | bytes 2048024
  10.4 1.1 shard_map.85
  11.5 1.6 %collective-permute-start.7 = (bf16[400,1536]{1,0:T(8,128)(2,1)S(1)}, bf16[400,1536]{1,0:T(8,128)(2,1)S(1)}, u32[]{:S(2)}, u32[]{:S(2)}) collective-permute-start(bf16[400,1536]{1,0:T(8,128)(2,1)S(1)} %get-tuple-element.78.own_a), channel_id=1, source_target_pairs={{0,4},{4,0},{1,5},{5,1},{2,6},{6,2},{3,7},{7,3},{8,12},{12,8},{9,1... | collective-permute-start | bytes 3686408 | tf_op jit(solution)/shard_map/ppermute | solution.py:47
  13.1 1.4 copy-done.1
  14.5 2.8 %shard_map.84 = (bf16[800,256]{1,0:T(8,128)(2,1)S(1)}, bf16[800,256]{1,0:T(8,128)(2,1)S(1)}, bf16[800,256]{1,0:T(8,128)(2,1)S(1)}, bf16[800,256]{1,0:T(8,128)(2,1)S(1)}) custom-call(s32[4]{0:T(128)S(1)} %pad_add_fusion.place, bf16[256,3200]{1,0:T(8,128)(2,1)S(1)} %copy-done, bf16[256,3200]{1,0:T(8,128)(2,1)S(1)} %copy-done.1), custom_call_target="tpu_custom_call" | custom-call | flops 6553600 | bytes 4915200 | tf_op jit(solution)/shard_map/pallas_call | solution.py:52
  17.4 2.5 %collective-permute-done.1.refs_0_ = bf16[64,2560]{1,0:T(8,128)(2,1)S(1)} collective-permute-done((bf16[64,2560]{1,0:T(8,128)(2,1)}, bf16[64,2560]{1,0:T(8,128)(2,1)S(1)}, u32[]{:S(2)}, u32[]{:S(2)}) %collective-permute-start.1) | collective-permute-done | bytes 327712 | tf_op jit(solution)/shard_map/ppermute | solution.py:47
  19.9 2.4 %collective-permute-done.refs_3_ = bf16[64,2560]{1,0:T(8,128)(2,1)S(1)} collective-permute-done((bf16[64,2560]{1,0:T(8,128)(2,1)}, bf16[64,2560]{1,0:T(8,128)(2,1)S(1)}, u32[]{:S(2)}, u32[]{:S(2)}) %collective-permute-start) | collective-permute-done | bytes 327712 | tf_op jit(solution)/shard_map/ppermute | solution.py:47
  23.5 2.7 %collective-permute-start.4 = (bf16[64,2560]{1,0:T(8,128)(2,1)S(1)}, bf16[64,2560]{1,0:T(8,128)(2,1)S(1)}, u32[]{:S(2)}, u32[]{:S(2)}) collective-permute-start(bf16[64,2560]{1,0:T(8,128)(2,1)S(1)} %collective-permute-done.refs_3_), channel_id=1, source_target_pairs={{0,8},{8,0},{16,24},{24,16},{1,9},{9,1},{17,25},{25,17},{2,10},{10... | collective-permute-start | bytes 983048 | tf_op jit(solution)/shard_map/ppermute | solution.py:47
  26.2 13.5 %collective-permute-done.4.refs_1_ = bf16[64,2560]{1,0:T(8,128)(2,1)S(1)} collective-permute-done((bf16[64,2560]{1,0:T(8,128)(2,1)S(1)}, bf16[64,2560]{1,0:T(8,128)(2,1)S(1)}, u32[]{:S(2)}, u32[]{:S(2)}) %collective-permute-start.4) | collective-permute-done | bytes 327712 | tf_op jit(solution)/shard_map/ppermute | solution.py:47
  39.7 1.5 %collective-permute-start.12 = (bf16[400,1024]{1,0:T(8,128)(2,1)S(1)}, bf16[400,1024]{1,0:T(8,128)(2,1)S(1)}, u32[]{:S(2)}, u32[]{:S(2)}) collective-permute-start(bf16[400,1024]{1,0:T(8,128)(2,1)S(1)} %get-tuple-element.87.own_b), channel_id=1, source_target_pairs={{0,4},{4,0},{1,5},{5,1},{2,6},{6,2},{3,7},{7,3},{8,12},{12,8},{9,1... | collective-permute-start | bytes 2457608 | tf_op jit(solution)/shard_map/ppermute | solution.py:47
  41.1 3.2 %collective-permute-done.6.refs_1_ = bf16[800,256]{1,0:T(8,128)(2,1)S(1)} collective-permute-done((bf16[800,256]{1,0:T(8,128)(2,1)S(1)}, bf16[800,256]{1,0:T(8,128)(2,1)S(1)}, u32[]{:S(2)}, u32[]{:S(2)}) %collective-permute-start.6) | collective-permute-done | bytes 409632 | tf_op jit(solution)/shard_map/ppermute | solution.py:47
  44.5 1.4 collective-permute-start.10
  45.9 1.5 %collective-permute-start.9 = (bf16[64,2560]{1,0:T(8,128)(2,1)S(1)}, bf16[64,2560]{1,0:T(8,128)(2,1)S(1)}, u32[]{:S(2)}, u32[]{:S(2)}) collective-permute-start(bf16[64,2560]{1,0:T(8,128)(2,1)S(1)} %collective-permute-done.4.refs_1_), channel_id=1, source_target_pairs={{0,2},{2,0},{1,3},{3,1},{4,6},{6,4},{5,7},{7,5},{8,10},{10,8},{9,1... | collective-permute-start | bytes 983048 | tf_op jit(solution)/shard_map/ppermute | solution.py:47
  47.4 11.8 %collective-permute-done.12.other_b = bf16[400,1024]{1,0:T(8,128)(2,1)S(1)} collective-permute-done((bf16[400,1024]{1,0:T(8,128)(2,1)S(1)}, bf16[400,1024]{1,0:T(8,128)(2,1)S(1)}, u32[]{:S(2)}, u32[]{:S(2)}) %collective-permute-start.12) | collective-permute-done | bytes 819232 | tf_op jit(solution)/shard_map/ppermute | solution.py:47
  59.2 7.0 %collective-permute-done.11.refs_3_ = bf16[800,256]{1,0:T(8,128)(2,1)S(1)} collective-permute-done((bf16[800,256]{1,0:T(8,128)(2,1)S(1)}, bf16[800,256]{1,0:T(8,128)(2,1)S(1)}, u32[]{:S(2)}, u32[]{:S(2)}) %collective-permute-start.11) | collective-permute-done | bytes 409632 | tf_op jit(solution)/shard_map/ppermute | solution.py:47
  66.2 0.8 shard_map.87
  67.0 1.1 shard_map.86
  68.2 0.7 shard_map.89
  69.9 1.2 fusion.14
  71.1 1.4 collective-permute-start.19
  72.5 3.1 %convolution_convert_fusion.1 = bf16[512,2560]{1,0:T(8,128)(2,1)S(1)} fusion(bf16[512,800]{1,0:T(8,128)(2,1)S(1)} %get-tuple-element.103, bf16[800,2560]{1,0:T(8,128)(2,1)S(1)} %shard_map.87), kind=kOutput, calls=%fused_computation.4 | convolution fusion | flops 2098462720 | bytes 7536640 | tf_op jit(solution)/shard_map/dot_general | solution.py:174
  77.1 1.1 fusion.31
  78.1 1.1 fusion.2
  79.2 1.6 %collective-permute-start.16 = (bf16[64,2560]{1,0:T(8,128)(2,1)S(1)}, bf16[64,2560]{1,0:T(8,128)(2,1)S(1)}, u32[]{:S(2)}, u32[]{:S(2)}) collective-permute-start(bf16[64,2560]{1,0:T(8,128)(2,1)S(1)} %fusion.4), channel_id=1, source_target_pairs={{0,4},{4,0},{1,5},{5,1},{2,6},{6,2},{3,7},{7,3},{8,12},{12,8},{9,1... | collective-permute-start | bytes 983048 | tf_op jit(solution)/shard_map/ppermute | solution.py:47
  80.8 3.3 %convolution_convert_fusion = bf16[512,2560]{1,0:T(8,128)(2,1)S(1)} fusion(bf16[512,800]{1,0:T(8,128)(2,1)S(1)} %get-tuple-element.109, bf16[800,2560]{1,0:T(8,128)(2,1)S(1)} %shard_map.87), kind=kOutput, calls=%fused_computation.3 | convolution fusion | flops 2098462720 | bytes 7536640 | tf_op jit(solution)/shard_map/dot_general | solution.py:174
  84.0 1.3 fusion.23
  85.3 1.3 fusion.17
  86.6 0.7 convert_add_fusion
  87.3 1.8 %collective-permute-done.16 = bf16[64,2560]{1,0:T(8,128)(2,1)S(1)} collective-permute-done((bf16[64,2560]{1,0:T(8,128)(2,1)S(1)}, bf16[64,2560]{1,0:T(8,128)(2,1)S(1)}, u32[]{:S(2)}, u32[]{:S(2)}) %collective-permute-start.16) | collective-permute-done | bytes 327712 | tf_op jit(solution)/shard_map/ppermute | solution.py:47
  89.6 1.6 %collective-permute-start.18 = (bf16[2,64,2560]{2,1,0:T(8,128)(2,1)S(1)}, bf16[2,64,2560]{2,1,0:T(8,128)(2,1)S(1)}, u32[]{:S(2)}, u32[]{:S(2)}) collective-permute-start(bf16[2,64,2560]{2,1,0:T(8,128)(2,1)S(1)} %get-tuple-element.137), channel_id=1, source_target_pairs={{0,2},{2,0},{1,3},{3,1},{4,6},{6,4},{5,7},{7,5},{8,10},{10,8},{9,1... | collective-permute-start | bytes 1966088 | tf_op jit(solution)/shard_map/ppermute | solution.py:47
  91.2 1.3 fusion.20.refs_0_
  92.4 1.5 %collective-permute-start.23 = (bf16[800,256]{1,0:T(8,128)(2,1)S(1)}, bf16[800,256]{1,0:T(8,128)(2,1)S(1)}, u32[]{:S(2)}, u32[]{:S(2)}) collective-permute-start(bf16[800,256]{1,0:T(8,128)(2,1)S(1)} %fusion.23), channel_id=1, source_target_pairs={{0,8},{8,0},{16,24},{24,16},{1,9},{9,1},{17,25},{25,17},{2,10},{10... | collective-permute-start | bytes 1228808 | tf_op jit(solution)/shard_map/ppermute | solution.py:47
  93.9 1.5 %collective-permute-start.24 = (bf16[336,2560]{1,0:T(8,128)(2,1)S(1)}, bf16[336,2560]{1,0:T(8,128)(2,1)S(1)}, u32[]{:S(2)}, u32[]{:S(2)}) collective-permute-start(bf16[336,2560]{1,0:T(8,128)(2,1)S(1)} %fusion.2), channel_id=1, source_target_pairs={{0,4},{4,0},{1,5},{5,1},{2,6},{6,2},{3,7},{7,3},{8,12},{12,8},{9,1... | collective-permute-start | bytes 5160968 | tf_op jit(solution)/shard_map/ppermute | solution.py:47
  95.4 1.2 fusion.37
  96.6 1.7 %collective-permute-start.21 = (bf16[800,256]{1,0:T(8,128)(2,1)S(1)}, bf16[800,256]{1,0:T(8,128)(2,1)S(1)}, u32[]{:S(2)}, u32[]{:S(2)}) collective-permute-start(bf16[800,256]{1,0:T(8,128)(2,1)S(1)} %fusion.17), channel_id=1, source_target_pairs={{0,24},{8,16},{16,8},{24,0},{1,25},{9,17},{17,9},{25,1},{2,26},{10... | collective-permute-start | bytes 1228808 | tf_op jit(solution)/shard_map/ppermute | solution.py:47
  98.8 8.5 %collective-permute-done.18 = bf16[2,64,2560]{2,1,0:T(8,128)(2,1)S(1)} collective-permute-done((bf16[2,64,2560]{2,1,0:T(8,128)(2,1)S(1)}, bf16[2,64,2560]{2,1,0:T(8,128)(2,1)S(1)}, u32[]{:S(2)}, u32[]{:S(2)}) %collective-permute-start.18) | collective-permute-done | bytes 655392 | tf_op jit(solution)/shard_map/ppermute | solution.py:47
  107.4 1.5 %collective-permute-start.20 = (bf16[2,64,2560]{2,1,0:T(8,128)(2,1)S(1)}, bf16[2,64,2560]{2,1,0:T(8,128)(2,1)S(1)}, u32[]{:S(2)}, u32[]{:S(2)}) collective-permute-start(bf16[2,64,2560]{2,1,0:T(8,128)(2,1)S(1)} %fusion.5), channel_id=1, source_target_pairs={{0,8},{8,0},{16,24},{24,16},{1,9},{9,1},{17,25},{25,17},{2,10},{10... | collective-permute-start | bytes 1966088 | tf_op jit(solution)/shard_map/ppermute | solution.py:47
  108.9 10.8 %collective-permute-done.17 = bf16[2,64,2560]{2,1,0:T(8,128)(2,1)S(1)} collective-permute-done((bf16[2,64,2560]{2,1,0:T(8,128)(2,1)S(1)}, bf16[2,64,2560]{2,1,0:T(8,128)(2,1)S(1)}, u32[]{:S(2)}, u32[]{:S(2)}) %collective-permute-start.17) | collective-permute-done | bytes 655392 | tf_op jit(solution)/shard_map/ppermute | solution.py:47
  119.9 7.1 %collective-permute-done.20 = bf16[2,64,2560]{2,1,0:T(8,128)(2,1)S(1)} collective-permute-done((bf16[2,64,2560]{2,1,0:T(8,128)(2,1)S(1)}, bf16[2,64,2560]{2,1,0:T(8,128)(2,1)S(1)}, u32[]{:S(2)}, u32[]{:S(2)}) %collective-permute-start.20) | collective-permute-done | bytes 655392 | tf_op jit(solution)/shard_map/ppermute | solution.py:47
  127.8 4.5 %collective-permute-done.24 = bf16[336,2560]{1,0:T(8,128)(2,1)S(1)} collective-permute-done((bf16[336,2560]{1,0:T(8,128)(2,1)S(1)}, bf16[336,2560]{1,0:T(8,128)(2,1)S(1)}, u32[]{:S(2)}, u32[]{:S(2)}) %collective-permute-start.24) | collective-permute-done | bytes 1720352 | tf_op jit(solution)/shard_map/ppermute | solution.py:47
  132.3 3.2 %convert_add_fusion.1 = f32[400,2560]{1,0:T(8,128)} fusion(bf16[336,2560]{1,0:T(8,128)(2,1)S(1)} %collective-permute-done.24, bf16[64,2560]{1,0:T(8,128)(2,1)S(1)} %collective-permute-done.16, f32[400,2560]{1,0:T(8,128)S(1)} %fusion.37, bf16[400,512]{1,0:T(8,128)(2,1)S(1)} %get-tuple-element.126, bf16[512,2560]{1,0:T(8,128)(2,1)S(1)} %shard_map.89), kind=kOutput, calls=%fused_computation.7 | convolution fusion | flops 1055744000 | bytes 13271040 | tf_op jit(solution)/shard_map/dot_general | solution.py:174
  135.5 5.7 %shard_map.90 = (bf16[256,3200]{1,0:T(8,128)(2,1)}, bf16[256,3200]{1,0:T(8,128)(2,1)}) custom-call(s32[4]{0:T(128)S(1)} %pad_add_fusion.place, bf16[256,3200]{1,0:T(8,128)(2,1)S(1)} %copy-done, bf16[256,3200]{1,0:T(8,128)(2,1)S(1)} %copy-done.2, bf16[800,256]{1,0:T(8,128)(2,1)S(1)} %fusion.20.refs_0_, bf16[800,256]{1,0:T(8,128)(2,1)S(1)} %collective-permute-done.23.refs_1_, ...), custom_call_target="tpu_custom_call" | custom-call | flops 19660800 | bytes 8192000 | tf_op jit(solution)/shard_map/pallas_call | solution.py:52
  141.2 3.2 %collective-permute-done.22 = bf16[64,2560]{1,0:T(8,128)(2,1)S(1)} collective-permute-done((bf16[64,2560]{1,0:T(8,128)(2,1)S(1)}, bf16[64,2560]{1,0:T(8,128)(2,1)S(1)}, u32[]{:S(2)}, u32[]{:S(2)}) %collective-permute-start.22) | collective-permute-done | bytes 327712 | tf_op jit(solution)/shard_map/ppermute | solution.py:47
  144.4 0.8 fusion.29
  (44 shorter events, 5.8 us)
Async XLA Ops:
  0.6 12.5 %copy-start = (bf16[256,3200]{1,0:T(8,128)(2,1)S(1)}, bf16[256,3200]{1,0:T(8,128)(2,1)}, u32[]{:S(2)}) copy-start(bf16[256,3200]{1,0:T(8,128)(2,1)} %gate.3) | copy-start | bytes 4915204
  0.6 16.8 %collective-permute-start.2 = (bf16[64,2560]{1,0:T(8,128)(2,1)}, bf16[64,2560]{1,0:T(8,128)(2,1)S(1)}, u32[]{:S(2)}, u32[]{:S(2)}) collective-permute-start(bf16[64,2560]{1,0:T(8,128)(2,1)} %refs_0_.1), channel_id=1, source_target_pairs={{0,2},{2,0},{1,3},{3,1},{4,6},{6,4},{5,7},{7,5},{8,10},{10,8},{9,1... | collective-permute-start | bytes 983048 | tf_op jit(solution)/shard_map/ppermute | solution.py:47
  3.7 16.3 %collective-permute-start.1 = (bf16[64,2560]{1,0:T(8,128)(2,1)}, bf16[64,2560]{1,0:T(8,128)(2,1)S(1)}, u32[]{:S(2)}, u32[]{:S(2)}) collective-permute-start(bf16[64,2560]{1,0:T(8,128)(2,1)} %refs_0_.1), channel_id=1, source_target_pairs={{0,8},{8,0},{16,24},{24,16},{1,9},{9,1},{17,25},{25,17},{2,10},{10... | collective-permute-start | bytes 983048 | tf_op jit(solution)/shard_map/ppermute | solution.py:47
  5.2 17.1 %collective-permute-start = (bf16[64,2560]{1,0:T(8,128)(2,1)}, bf16[64,2560]{1,0:T(8,128)(2,1)S(1)}, u32[]{:S(2)}, u32[]{:S(2)}) collective-permute-start(bf16[64,2560]{1,0:T(8,128)(2,1)} %refs_0_.1), channel_id=1, source_target_pairs={{0,16},{8,24},{16,0},{24,8},{1,17},{9,25},{17,1},{25,9},{2,18},{10... | collective-permute-start | bytes 983048 | tf_op jit(solution)/shard_map/ppermute | solution.py:47
  7.8 14.5 %collective-permute-start.3 = (bf16[64,2560]{1,0:T(8,128)(2,1)}, bf16[64,2560]{1,0:T(8,128)(2,1)S(1)}, u32[]{:S(2)}, u32[]{:S(2)}) collective-permute-start(bf16[64,2560]{1,0:T(8,128)(2,1)} %refs_0_.1), channel_id=1, source_target_pairs={{0,1},{1,0},{2,3},{3,2},{4,5},{5,4},{6,7},{7,6},{8,9},{9,8},{10,11... | collective-permute-start | bytes 983048 | tf_op jit(solution)/shard_map/ppermute | solution.py:47
  8.8 1.6 %copy-start.3 = (bf16[400,2560]{1,0:T(8,128)(2,1)S(1)}, bf16[400,2560]{1,0:T(8,128)(2,1)}, u32[]{:S(2)}) copy-start(bf16[400,2560]{1,0:T(8,128)(2,1)} %codes.1) | copy-start | bytes 6144004
  11.5 32.8 %collective-permute-start.7 = (bf16[400,1536]{1,0:T(8,128)(2,1)S(1)}, bf16[400,1536]{1,0:T(8,128)(2,1)S(1)}, u32[]{:S(2)}, u32[]{:S(2)}) collective-permute-start(bf16[400,1536]{1,0:T(8,128)(2,1)S(1)} %get-tuple-element.78.own_a), channel_id=1, source_target_pairs={{0,4},{4,0},{1,5},{5,1},{2,6},{6,2},{3,7},{7,3},{8,12},{12,8},{9,1... | collective-permute-start | bytes 3686408 | tf_op jit(solution)/shard_map/ppermute | solution.py:47
  13.1 1.4 copy-start.1
  22.5 21.9 %collective-permute-start.8 = (bf16[3,64,2560]{2,1,0:T(8,128)(2,1)S(1)}, bf16[3,64,2560]{2,1,0:T(8,128)(2,1)S(1)}, u32[]{:S(2)}, u32[]{:S(2)}) collective-permute-start(bf16[3,64,2560]{2,1,0:T(8,128)(2,1)S(1)} %pad_maximum_fusion), channel_id=1, source_target_pairs={{0,1},{1,0},{2,3},{3,2},{4,5},{5,4},{6,7},{7,6},{8,9},{9,8},{10,11... | collective-permute-start | bytes 2949128 | tf_op jit(solution)/shard_map/ppermute | solution.py:47
  22.6 21.7 %collective-permute-start.5 = (bf16[2,64,2560]{2,1,0:T(8,128)(2,1)S(1)}, bf16[2,64,2560]{2,1,0:T(8,128)(2,1)S(1)}, u32[]{:S(2)}, u32[]{:S(2)}) collective-permute-start(bf16[2,64,2560]{2,1,0:T(8,128)(2,1)S(1)} %pad_maximum_fusion.2), channel_id=1, source_target_pairs={{0,2},{2,0},{1,3},{3,1},{4,6},{6,4},{5,7},{7,5},{8,10},{10,8},{9,1... | collective-permute-start | bytes 1966088 | tf_op jit(solution)/shard_map/ppermute | solution.py:47
  23.2 21.1 %collective-permute-start.6 = (bf16[800,256]{1,0:T(8,128)(2,1)S(1)}, bf16[800,256]{1,0:T(8,128)(2,1)S(1)}, u32[]{:S(2)}, u32[]{:S(2)}) collective-permute-start(bf16[800,256]{1,0:T(8,128)(2,1)S(1)} %get-tuple-element.77), channel_id=1, source_target_pairs={{0,16},{8,24},{16,0},{24,8},{1,17},{9,25},{17,1},{25,9},{2,18},{10... | collective-permute-start | bytes 1228808 | tf_op jit(solution)/shard_map/ppermute | solution.py:47
  23.5 16.2 %collective-permute-start.4 = (bf16[64,2560]{1,0:T(8,128)(2,1)S(1)}, bf16[64,2560]{1,0:T(8,128)(2,1)S(1)}, u32[]{:S(2)}, u32[]{:S(2)}) collective-permute-start(bf16[64,2560]{1,0:T(8,128)(2,1)S(1)} %collective-permute-done.refs_3_), channel_id=1, source_target_pairs={{0,8},{8,0},{16,24},{24,16},{1,9},{9,1},{17,25},{25,17},{2,10},{10... | collective-permute-start | bytes 983048 | tf_op jit(solution)/shard_map/ppermute | solution.py:47
  39.7 19.5 %collective-permute-start.12 = (bf16[400,1024]{1,0:T(8,128)(2,1)S(1)}, bf16[400,1024]{1,0:T(8,128)(2,1)S(1)}, u32[]{:S(2)}, u32[]{:S(2)}) collective-permute-start(bf16[400,1024]{1,0:T(8,128)(2,1)S(1)} %get-tuple-element.87.own_b), channel_id=1, source_target_pairs={{0,4},{4,0},{1,5},{5,1},{2,6},{6,2},{3,7},{7,3},{8,12},{12,8},{9,1... | collective-permute-start | bytes 2457608 | tf_op jit(solution)/shard_map/ppermute | solution.py:47
  44.4 23.8 %collective-permute-start.13 = (bf16[3,64,2560]{2,1,0:T(8,128)(2,1)S(1)}, bf16[3,64,2560]{2,1,0:T(8,128)(2,1)S(1)}, u32[]{:S(2)}, u32[]{:S(2)}) collective-permute-start(bf16[3,64,2560]{2,1,0:T(8,128)(2,1)S(1)} %pad_maximum_fusion.1), channel_id=1, source_target_pairs={{0,1},{1,0},{2,3},{3,2},{4,5},{5,4},{6,7},{7,6},{8,9},{9,8},{10,11... | collective-permute-start | bytes 2949128 | tf_op jit(solution)/shard_map/ppermute | solution.py:47
  44.5 14.7 %collective-permute-start.10 = (bf16[800,256]{1,0:T(8,128)(2,1)S(1)}, bf16[800,256]{1,0:T(8,128)(2,1)S(1)}, u32[]{:S(2)}, u32[]{:S(2)}) collective-permute-start(bf16[800,256]{1,0:T(8,128)(2,1)S(1)} %get-tuple-element.85), channel_id=1, source_target_pairs={{0,24},{8,16},{16,8},{24,0},{1,25},{9,17},{17,9},{25,1},{2,26},{10... | collective-permute-start | bytes 1228808 | tf_op jit(solution)/shard_map/ppermute | solution.py:47
  45.9 20.3 %collective-permute-start.11 = (bf16[800,256]{1,0:T(8,128)(2,1)S(1)}, bf16[800,256]{1,0:T(8,128)(2,1)S(1)}, u32[]{:S(2)}, u32[]{:S(2)}) collective-permute-start(bf16[800,256]{1,0:T(8,128)(2,1)S(1)} %get-tuple-element.86), channel_id=1, source_target_pairs={{0,8},{8,0},{16,24},{24,16},{1,9},{9,1},{17,25},{25,17},{2,10},{10... | collective-permute-start | bytes 1228808 | tf_op jit(solution)/shard_map/ppermute | solution.py:47
  45.9 13.3 %collective-permute-start.9 = (bf16[64,2560]{1,0:T(8,128)(2,1)S(1)}, bf16[64,2560]{1,0:T(8,128)(2,1)S(1)}, u32[]{:S(2)}, u32[]{:S(2)}) collective-permute-start(bf16[64,2560]{1,0:T(8,128)(2,1)S(1)} %collective-permute-done.4.refs_1_), channel_id=1, source_target_pairs={{0,2},{2,0},{1,3},{3,1},{4,6},{6,4},{5,7},{7,5},{8,10},{10,8},{9,1... | collective-permute-start | bytes 983048 | tf_op jit(solution)/shard_map/ppermute | solution.py:47
  66.2 2.0 %collective-permute-start.14 = (bf16[64,2560]{1,0:T(8,128)(2,1)S(1)}, bf16[64,2560]{1,0:T(8,128)(2,1)S(1)}, u32[]{:S(2)}, u32[]{:S(2)}) collective-permute-start(bf16[64,2560]{1,0:T(8,128)(2,1)S(1)} %collective-permute-done.9.refs_2_), channel_id=1, source_target_pairs={{0,1},{1,0},{2,3},{3,2},{4,5},{5,4},{6,7},{7,6},{8,9},{9,8},{10,11... | collective-permute-start | bytes 983048 | tf_op jit(solution)/shard_map/ppermute | solution.py:47
  68.2 1.0 copy-start.4
  71.1 25.5 %collective-permute-start.19 = (bf16[800,256]{1,0:T(8,128)(2,1)S(1)}, bf16[800,256]{1,0:T(8,128)(2,1)S(1)}, u32[]{:S(2)}, u32[]{:S(2)}) collective-permute-start(bf16[800,256]{1,0:T(8,128)(2,1)S(1)} %fusion.14), channel_id=1, source_target_pairs={{0,16},{8,24},{16,0},{24,8},{1,17},{9,25},{17,1},{25,9},{2,18},{10... | collective-permute-start | bytes 1228808 | tf_op jit(solution)/shard_map/ppermute | solution.py:47
  75.6 10.9 %collective-permute-start.15 = (bf16[512,2560]{1,0:T(8,128)(2,1)S(1)}, bf16[512,2560]{1,0:T(8,128)(2,1)S(1)}, u32[]{:S(2)}, u32[]{:S(2)}) collective-permute-start(bf16[512,2560]{1,0:T(8,128)(2,1)S(1)} %convolution_convert_fusion.1), channel_id=1, source_target_pairs={{0,1},{1,0},{2,3},{3,2},{4,5},{5,4},{6,7},{7,6},{8,9},{9,8},{10,11... | collective-permute-start | bytes 7864328 | tf_op jit(solution)/shard_map/ppermute | solution.py:47
  79.2 9.9 %collective-permute-start.16 = (bf16[64,2560]{1,0:T(8,128)(2,1)S(1)}, bf16[64,2560]{1,0:T(8,128)(2,1)S(1)}, u32[]{:S(2)}, u32[]{:S(2)}) collective-permute-start(bf16[64,2560]{1,0:T(8,128)(2,1)S(1)} %fusion.4), channel_id=1, source_target_pairs={{0,4},{4,0},{1,5},{5,1},{2,6},{6,2},{3,7},{7,3},{8,12},{12,8},{9,1... | collective-permute-start | bytes 983048 | tf_op jit(solution)/shard_map/ppermute | solution.py:47
  89.6 17.7 %collective-permute-start.18 = (bf16[2,64,2560]{2,1,0:T(8,128)(2,1)S(1)}, bf16[2,64,2560]{2,1,0:T(8,128)(2,1)S(1)}, u32[]{:S(2)}, u32[]{:S(2)}) collective-permute-start(bf16[2,64,2560]{2,1,0:T(8,128)(2,1)S(1)} %get-tuple-element.137), channel_id=1, source_target_pairs={{0,2},{2,0},{1,3},{3,1},{4,6},{6,4},{5,7},{7,5},{8,10},{10,8},{9,1... | collective-permute-start | bytes 1966088 | tf_op jit(solution)/shard_map/ppermute | solution.py:47
  92.4 43.1 %collective-permute-start.23 = (bf16[800,256]{1,0:T(8,128)(2,1)S(1)}, bf16[800,256]{1,0:T(8,128)(2,1)S(1)}, u32[]{:S(2)}, u32[]{:S(2)}) collective-permute-start(bf16[800,256]{1,0:T(8,128)(2,1)S(1)} %fusion.23), channel_id=1, source_target_pairs={{0,8},{8,0},{16,24},{24,16},{1,9},{9,1},{17,25},{25,17},{2,10},{10... | collective-permute-start | bytes 1228808 | tf_op jit(solution)/shard_map/ppermute | solution.py:47
  93.9 38.4 %collective-permute-start.24 = (bf16[336,2560]{1,0:T(8,128)(2,1)S(1)}, bf16[336,2560]{1,0:T(8,128)(2,1)S(1)}, u32[]{:S(2)}, u32[]{:S(2)}) collective-permute-start(bf16[336,2560]{1,0:T(8,128)(2,1)S(1)} %fusion.2), channel_id=1, source_target_pairs={{0,4},{4,0},{1,5},{5,1},{2,6},{6,2},{3,7},{7,3},{8,12},{12,8},{9,1... | collective-permute-start | bytes 5160968 | tf_op jit(solution)/shard_map/ppermute | solution.py:47
  96.6 30.6 %collective-permute-start.21 = (bf16[800,256]{1,0:T(8,128)(2,1)S(1)}, bf16[800,256]{1,0:T(8,128)(2,1)S(1)}, u32[]{:S(2)}, u32[]{:S(2)}) collective-permute-start(bf16[800,256]{1,0:T(8,128)(2,1)S(1)} %fusion.17), channel_id=1, source_target_pairs={{0,24},{8,16},{16,8},{24,0},{1,25},{9,17},{17,9},{25,1},{2,26},{10... | collective-permute-start | bytes 1228808 | tf_op jit(solution)/shard_map/ppermute | solution.py:47
  98.3 21.4 %collective-permute-start.17 = (bf16[2,64,2560]{2,1,0:T(8,128)(2,1)S(1)}, bf16[2,64,2560]{2,1,0:T(8,128)(2,1)S(1)}, u32[]{:S(2)}, u32[]{:S(2)}) collective-permute-start(bf16[2,64,2560]{2,1,0:T(8,128)(2,1)S(1)} %get-tuple-element.136), channel_id=1, source_target_pairs={{0,2},{2,0},{1,3},{3,1},{4,6},{6,4},{5,7},{7,5},{8,10},{10,8},{9,1... | collective-permute-start | bytes 1966088 | tf_op jit(solution)/shard_map/ppermute | solution.py:47
  107.4 19.5 %collective-permute-start.20 = (bf16[2,64,2560]{2,1,0:T(8,128)(2,1)S(1)}, bf16[2,64,2560]{2,1,0:T(8,128)(2,1)S(1)}, u32[]{:S(2)}, u32[]{:S(2)}) collective-permute-start(bf16[2,64,2560]{2,1,0:T(8,128)(2,1)S(1)} %fusion.5), channel_id=1, source_target_pairs={{0,8},{8,0},{16,24},{24,16},{1,9},{9,1},{17,25},{25,17},{2,10},{10... | collective-permute-start | bytes 1966088 | tf_op jit(solution)/shard_map/ppermute | solution.py:47
  127.2 17.2 %collective-permute-start.22 = (bf16[64,2560]{1,0:T(8,128)(2,1)S(1)}, bf16[64,2560]{1,0:T(8,128)(2,1)S(1)}, u32[]{:S(2)}, u32[]{:S(2)}) collective-permute-start(bf16[64,2560]{1,0:T(8,128)(2,1)S(1)} %fusion.33), channel_id=1, source_target_pairs={{0,16},{8,24},{16,0},{24,8},{1,17},{9,25},{17,1},{25,9},{2,18},{10... | collective-permute-start | bytes 983048 | tf_op jit(solution)/shard_map/ppermute | solution.py:47
  132.3 3.2 %copy-start.2 = (bf16[256,3200]{1,0:T(8,128)(2,1)S(1)}, bf16[256,3200]{1,0:T(8,128)(2,1)}, u32[]{:S(2)}) copy-start(bf16[256,3200]{1,0:T(8,128)(2,1)} %up.3) | copy-start | bytes 4915204

commit v2 on v0

--- a/solution.py
+++ b/solution.py
@@ -259,41 +259,41 @@
         (near, last, last_y, other_y, first_c, other_c, last_c),
         ((0, 0), (3, 1), (4, 2), (5, 1), (1, 0), (2, 0), (5, 2), (6, 0)),
     )
-    even, odd, send, keep = barrier((even, odd, send, keep))
-    flat = [even, odd]
-
     factor = float(total_tokens) ** (-0.5)
 
 
-    def grad_half(r):
-        return (matmul(by_units[r], flat[0]) + matmul(by_units[2 + r], flat[1])) * factor
+    def grad_half(r, low=0, high=owned):
+        first, second = by_units[r][low:high], by_units[2 + r][low:high]
+        return (matmul(first, flat[0]) + matmul(second, flat[1])) * factor
 
     def back_of(k):
         rows_of_k = flat[k % 2][k // 2 * group_rows : (k // 2 + 1) * group_rows]
         return matmul(weight, rows_of_k, 1, 1, bf16)
 
     over_c = exchange(matmul(send, weight, dtype=bf16), "c", 1)
-    back = [None, None, back_of(2), None]
-    back[2], flat = barrier((back[2], flat))
-    theirs = grad_half(1).astype(bf16)
-    theirs, keep, flat = barrier((theirs, keep, flat))
-    over_x = exchange(theirs, "x", 1)
     kept = matmul(keep, weight, dtype=bf16)
-    back = [back_of(0), back_of(1), back[2], back_of(3)]
-    back = [back[0]] + [exchange(back[k], "z", k) for k in range(1, nz)]
+    kept, flat = barrier((kept, [even, odd]))
+    far_back = back_of(2)
+    kept, far_back = barrier((kept, far_back))
     sums = (kept.astype(f32) + over_c.astype(f32)).reshape(2, nz, rows, width)
+    sums, flat = barrier((sums, flat))
     odd_y = exchange(sums[1, :2].astype(bf16), "y", 1)
     even_y = exchange(sums[1, 2:].astype(bf16), "y", 1)
+    over_x = exchange(grad_half(1).astype(bf16), "x", 1)
+    near_back = exchange(back_of(1), "z", 1)
+    odd_y, flat = barrier((odd_y, flat))
+    back = [back_of(0), near_back, exchange(far_back, "z", 2), exchange(back_of(3), "z", 3)]
     odd_sum = (sums[0, :2] + odd_y.astype(f32)).astype(bf16)
     odd_sum, back[2] = barrier((odd_sum, back[2]))
-    even_y, _ = barrier((even_y, odd_sum))
-    near_sum = exchange(odd_sum, "z", 1).astype(f32)
+    near_sum, even_y = barrier((exchange(odd_sum, "z", 1), even_y))
+    near_sum = near_sum.astype(f32)
     even_sum = sums[0, 2:] + even_y.astype(f32)
     ours, across = even_sum[0] + near_sum[0], (even_sum[1] + near_sum[1]).astype(bf16)
     across, back[3] = barrier((across, back[3]))
-    layer_out = (ours + exchange(across, "z", 2).astype(f32)).astype(bf16)
-
-    back, _ = barrier((back, across))
+    far_sum = exchange(across, "z", 2)
+
+    back, flat, _ = barrier((back, flat, across))
+    own_grad = grad_half(0)
     gate_grad, up_grad = call_kernel(
         functools.partial(grads_kernel, nz, units), place, (gate_pre, up_pre, *back),
         [wide] * 2 + [whole((units, group_rows))] * nz,
@@ -301,7 +301,9 @@
         (12 * act_bytes, 5 * act_bytes, act_bytes // 2),
     )
     over_x, _ = barrier((over_x, gate_grad))
-    weight_grad = grad_half(0) + over_x.astype(f32)
+    weight_grad = own_grad + over_x.astype(f32)
+    far_sum, weight_grad = barrier((far_sum, weight_grad))
+    layer_out = (ours + far_sum.astype(f32)).astype(bf16)
     return layer_out, gate_grad, up_grad, weight_grad
 
 

time: 141 us -> 142 us (level)
  matrix products: 16.1 us -> 18.1 us
  starting transfers between devices: 25.5 us -> 27.3 us
  other arithmetic: 4.36 us -> 2.59 us
    dot_general x10, matrix products: 16.1 us -> 18.1 us  [matmul(): lax.dot_general(lhs, rhs, dims, preferred_element_type=jnp.float32)]
    ppermute x24, starting transfers between devices: 25.5 us -> 27.3 us  [exchange(): return lax.ppermute(value, axis, [(i, i ^ offset) for i in range(size)])]
    add x1, other arithmetic: 2.5 us -> 0.74 us  [paired_body(): sums = (kept.astype(f32) + over_c.astype(f32)).reshape(2, nz, rows, width)]
  transfers between devices with their start and end apart: 24 -> 24, of which waited for: 12 -> 14; matrix products, arithmetic and copies ran while one was open for 12% -> 13% of each run, Pallas kernels for 9% -> 8%
where the time goes in v2:
time: 142 us
  waiting for transfers between devices  76.1 us (54%)
  starting transfers between devices  27.3 us (19%)
  matrix products  18.1 us (13%)
  Pallas kernels  13 us (9%)
  local copies, waits for them, and re-layouts  4.01 us (3%)
  other arithmetic  2.59 us (2%)
    ppermute x24, waiting for transfers between devices, exchange(): return lax.ppermute(value, axis, [(i, i ^ offset) for i in range(size)])  76.1 us
    ppermute x24, starting transfers between devices, exchange(): return lax.ppermute(value, axis, [(i, i ^ offset) for i in range(size)])  27.3 us
    dot_general x10, matrix products, matmul(): lax.dot_general(lhs, rhs, dims, preferred_element_type=jnp.float32)  18.1 us
    pallas_call x7, Pallas kernels, call_kernel(): pl.pallas_call(kernel, out_shape=out_shapes, grid_spec=pltpu.PrefetchScal...  13 us
    unnamed x11, local copies, waits for them, and re-layouts  3.91 us
  transfers between devices with their start and end apart: 24, of which 14 were waited for; matrix products, arithmetic and copies ran while one was open for 13% of the time, Pallas kernels for 8%

profile of v2, /device:TPU:0, one launch (start us, length us, event | category | flops | bytes accessed | tf_op | source)
XLA Modules:
  0.0 142.0 jit_solution(6565319313587202974)
XLA Ops:
  0.6 4.1 %collective-permute-start = (bf16[64,2560]{1,0:T(8,128)(2,1)}, bf16[64,2560]{1,0:T(8,128)(2,1)S(1)}, u32[]{:S(2)}, u32[]{:S(2)}) collective-permute-start(bf16[64,2560]{1,0:T(8,128)(2,1)} %refs_0_.1), channel_id=1, source_target_pairs={{0,16},{8,24},{16,0},{24,8},{1,17},{9,25},{17,1},{25,9},{2,18},{10... | collective-permute-start | bytes 983048 | tf_op jit(solution)/shard_map/ppermute | solution.py:47
  4.7 1.6 %collective-permute-start.1 = (bf16[64,2560]{1,0:T(8,128)(2,1)}, bf16[64,2560]{1,0:T(8,128)(2,1)S(1)}, u32[]{:S(2)}, u32[]{:S(2)}) collective-permute-start(bf16[64,2560]{1,0:T(8,128)(2,1)} %refs_0_.1), channel_id=1, source_target_pairs={{0,8},{8,0},{16,24},{24,16},{1,9},{9,1},{17,25},{25,17},{2,10},{10... | collective-permute-start | bytes 983048 | tf_op jit(solution)/shard_map/ppermute | solution.py:47
  6.3 1.5 %collective-permute-start.2 = (bf16[64,2560]{1,0:T(8,128)(2,1)}, bf16[64,2560]{1,0:T(8,128)(2,1)S(1)}, u32[]{:S(2)}, u32[]{:S(2)}) collective-permute-start(bf16[64,2560]{1,0:T(8,128)(2,1)} %refs_0_.1), channel_id=1, source_target_pairs={{0,2},{2,0},{1,3},{3,1},{4,6},{6,4},{5,7},{7,5},{8,10},{10,8},{9,1... | collective-permute-start | bytes 983048 | tf_op jit(solution)/shard_map/ppermute | solution.py:47
  7.8 0.9 copy.9.scales
  8.8 1.6 %copy-done.3 = bf16[400,2560]{1,0:T(8,128)(2,1)S(1)} copy-done((bf16[400,2560]{1,0:T(8,128)(2,1)S(1)}, bf16[400,2560]{1,0:T(8,128)(2,1)}, u32[]{:S(2)}) %copy-start.3) | copy-done | bytes 2048024
  10.4 1.1 shard_map.85
  11.5 1.6 %collective-permute-start.7 = (bf16[400,1536]{1,0:T(8,128)(2,1)S(1)}, bf16[400,1536]{1,0:T(8,128)(2,1)S(1)}, u32[]{:S(2)}, u32[]{:S(2)}) collective-permute-start(bf16[400,1536]{1,0:T(8,128)(2,1)S(1)} %get-tuple-element.74.own_a), channel_id=1, source_target_pairs={{0,4},{4,0},{1,5},{5,1},{2,6},{6,2},{3,7},{7,3},{8,12},{12,8},{9,1... | collective-permute-start | bytes 3686408 | tf_op jit(solution)/shard_map/ppermute | solution.py:47
  13.1 1.4 %copy-done.1 = bf16[256,3200]{1,0:T(8,128)(2,1)S(1)} copy-done((bf16[256,3200]{1,0:T(8,128)(2,1)S(1)}, bf16[256,3200]{1,0:T(8,128)(2,1)}, u32[]{:S(2)}) %copy-start.1) | copy-done | bytes 1638424
  14.5 2.8 %shard_map.84 = (bf16[800,256]{1,0:T(8,128)(2,1)S(1)}, bf16[800,256]{1,0:T(8,128)(2,1)S(1)}, bf16[800,256]{1,0:T(8,128)(2,1)S(1)}, bf16[800,256]{1,0:T(8,128)(2,1)S(1)}) custom-call(s32[4]{0:T(128)S(1)} %pad_add_fusion.place, bf16[256,3200]{1,0:T(8,128)(2,1)S(1)} %copy-done, bf16[256,3200]{1,0:T(8,128)(2,1)S(1)} %copy-done.1), custom_call_target="tpu_custom_call" | custom-call | flops 6553600 | bytes 4915200 | tf_op jit(solution)/shard_map/pallas_call | solution.py:52
  17.4 2.4 %collective-permute-done.refs_3_ = bf16[64,2560]{1,0:T(8,128)(2,1)S(1)} collective-permute-done((bf16[64,2560]{1,0:T(8,128)(2,1)}, bf16[64,2560]{1,0:T(8,128)(2,1)S(1)}, u32[]{:S(2)}, u32[]{:S(2)}) %collective-permute-start) | collective-permute-done | bytes 327712 | tf_op jit(solution)/shard_map/ppermute | solution.py:47
  20.0 1.5 %collective-permute-start.4 = (bf16[64,2560]{1,0:T(8,128)(2,1)S(1)}, bf16[64,2560]{1,0:T(8,128)(2,1)S(1)}, u32[]{:S(2)}, u32[]{:S(2)}) collective-permute-start(bf16[64,2560]{1,0:T(8,128)(2,1)S(1)} %collective-permute-done.refs_3_), channel_id=1, source_target_pairs={{0,8},{8,0},{16,24},{24,16},{1,9},{9,1},{17,25},{25,17},{2,10},{10... | collective-permute-start | bytes 983048 | tf_op jit(solution)/shard_map/ppermute | solution.py:47
  21.7 1.6 %collective-permute-start.5 = (bf16[2,64,2560]{2,1,0:T(8,128)(2,1)S(1)}, bf16[2,64,2560]{2,1,0:T(8,128)(2,1)S(1)}, u32[]{:S(2)}, u32[]{:S(2)}) collective-permute-start(bf16[2,64,2560]{2,1,0:T(8,128)(2,1)S(1)} %pad_maximum_fusion.2), channel_id=1, source_target_pairs={{0,2},{2,0},{1,3},{3,1},{4,6},{6,4},{5,7},{7,5},{8,10},{10,8},{9,1... | collective-permute-start | bytes 1966088 | tf_op jit(solution)/shard_map/ppermute | solution.py:47
  23.3 2.4 %collective-permute-start.6 = (bf16[800,256]{1,0:T(8,128)(2,1)S(1)}, bf16[800,256]{1,0:T(8,128)(2,1)S(1)}, u32[]{:S(2)}, u32[]{:S(2)}) collective-permute-start(bf16[800,256]{1,0:T(8,128)(2,1)S(1)} %get-tuple-element.73), channel_id=1, source_target_pairs={{0,16},{8,24},{16,0},{24,8},{1,17},{9,25},{17,1},{25,9},{2,18},{10... | collective-permute-start | bytes 1228808 | tf_op jit(solution)/shard_map/ppermute | solution.py:47
  25.7 7.2 %collective-permute-done.4.refs_1_ = bf16[64,2560]{1,0:T(8,128)(2,1)S(1)} collective-permute-done((bf16[64,2560]{1,0:T(8,128)(2,1)S(1)}, bf16[64,2560]{1,0:T(8,128)(2,1)S(1)}, u32[]{:S(2)}, u32[]{:S(2)}) %collective-permute-start.4) | collective-permute-done | bytes 327712 | tf_op jit(solution)/shard_map/ppermute | solution.py:47
  32.9 1.3 collective-permute-start.12
  34.2 10.4 %collective-permute-done.6.refs_1_ = bf16[800,256]{1,0:T(8,128)(2,1)S(1)} collective-permute-done((bf16[800,256]{1,0:T(8,128)(2,1)S(1)}, bf16[800,256]{1,0:T(8,128)(2,1)S(1)}, u32[]{:S(2)}, u32[]{:S(2)}) %collective-permute-start.6) | collective-permute-done | bytes 409632 | tf_op jit(solution)/shard_map/ppermute | solution.py:47
  44.6 1.9 %collective-permute-start.10 = (bf16[800,256]{1,0:T(8,128)(2,1)S(1)}, bf16[800,256]{1,0:T(8,128)(2,1)S(1)}, u32[]{:S(2)}, u32[]{:S(2)}) collective-permute-start(bf16[800,256]{1,0:T(8,128)(2,1)S(1)} %get-tuple-element.81), channel_id=1, source_target_pairs={{0,24},{8,16},{16,8},{24,0},{1,25},{9,17},{17,9},{25,1},{2,26},{10... | collective-permute-start | bytes 1228808 | tf_op jit(solution)/shard_map/ppermute | solution.py:47
  47.1 11.5 %collective-permute-done.12.other_b = bf16[400,1024]{1,0:T(8,128)(2,1)S(1)} collective-permute-done((bf16[400,1024]{1,0:T(8,128)(2,1)S(1)}, bf16[400,1024]{1,0:T(8,128)(2,1)S(1)}, u32[]{:S(2)}, u32[]{:S(2)}) %collective-permute-start.12) | collective-permute-done | bytes 819232 | tf_op jit(solution)/shard_map/ppermute | solution.py:47
  58.9 6.9 %collective-permute-done.11.refs_3_ = bf16[800,256]{1,0:T(8,128)(2,1)S(1)} collective-permute-done((bf16[800,256]{1,0:T(8,128)(2,1)S(1)}, bf16[800,256]{1,0:T(8,128)(2,1)S(1)}, u32[]{:S(2)}, u32[]{:S(2)}) %collective-permute-start.11) | collective-permute-done | bytes 409632 | tf_op jit(solution)/shard_map/ppermute | solution.py:47
  65.8 0.8 shard_map.87
  66.6 1.1 shard_map.86
  67.8 3.1 %convolution_convert_fusion = bf16[512,2560]{1,0:T(8,128)(2,1)S(1)} fusion(bf16[512,800]{1,0:T(8,128)(2,1)S(1)} %get-tuple-element.98, bf16[800,2560]{1,0:T(8,128)(2,1)S(1)} %shard_map.87), kind=kOutput, calls=%fused_computation.6 | convolution fusion | flops 2098462720 | bytes 7536640 | tf_op jit(solution)/shard_map/dot_general | solution.py:174
  71.7 3.1 %convolution_convert_fusion.1 = bf16[512,2560]{1,0:T(8,128)(2,1)S(1)} fusion(bf16[512,800]{1,0:T(8,128)(2,1)S(1)} %get-tuple-element.88, bf16[800,2560]{1,0:T(8,128)(2,1)S(1)} %shard_map.87), kind=kOutput, calls=%fused_computation.7 | convolution fusion | flops 2098462720 | bytes 7536640 | tf_op jit(solution)/shard_map/dot_general | solution.py:174
  74.8 2.9 %collective-permute-done.14.refs_6_ = bf16[64,2560]{1,0:T(8,128)(2,1)S(1)} collective-permute-done((bf16[64,2560]{1,0:T(8,128)(2,1)S(1)}, bf16[64,2560]{1,0:T(8,128)(2,1)S(1)}, u32[]{:S(2)}, u32[]{:S(2)}) %collective-permute-start.14) | collective-permute-done | bytes 327712 | tf_op jit(solution)/shard_map/ppermute | solution.py:47
  77.7 0.7 shard_map.89
  78.5 0.7 shard_map.88
  79.2 1.3 fusion.13
  80.4 0.9 collective-permute-start.17
  81.4 0.7 convert_add_fusion
  82.1 1.3 fusion.22
  83.4 1.8 %collective-permute-start.22 = (bf16[800,256]{1,0:T(8,128)(2,1)S(1)}, bf16[800,256]{1,0:T(8,128)(2,1)S(1)}, u32[]{:S(2)}, u32[]{:S(2)}) collective-permute-start(bf16[800,256]{1,0:T(8,128)(2,1)S(1)} %fusion.22), channel_id=1, source_target_pairs={{0,8},{8,0},{16,24},{24,16},{1,9},{9,1},{17,25},{25,17},{2,10},{10... | collective-permute-start | bytes 1228808 | tf_op jit(solution)/shard_map/ppermute | solution.py:47
  86.1 1.5 %collective-permute-start.19 = (bf16[2,64,2560]{2,1,0:T(8,128)(2,1)S(1)}, bf16[2,64,2560]{2,1,0:T(8,128)(2,1)S(1)}, u32[]{:S(2)}, u32[]{:S(2)}) collective-permute-start(bf16[2,64,2560]{2,1,0:T(8,128)(2,1)S(1)} %get-tuple-element.128), channel_id=1, source_target_pairs={{0,2},{2,0},{1,3},{3,1},{4,6},{6,4},{5,7},{7,5},{8,10},{10,8},{9,1... | collective-permute-start | bytes 1966088 | tf_op jit(solution)/shard_map/ppermute | solution.py:47
  87.6 1.2 fusion.31
  88.9 1.2 fusion.3
  90.1 1.6 %collective-permute-start.23 = (bf16[400,2560]{1,0:T(8,128)(2,1)S(1)}, bf16[400,2560]{1,0:T(8,128)(2,1)S(1)}, u32[]{:S(2)}, u32[]{:S(2)}) collective-permute-start(bf16[400,2560]{1,0:T(8,128)(2,1)S(1)} %fusion.3), channel_id=1, source_target_pairs={{0,4},{4,0},{1,5},{5,1},{2,6},{6,2},{3,7},{7,3},{8,12},{12,8},{9,1... | collective-permute-start | bytes 6144008 | tf_op jit(solution)/shard_map/ppermute | solution.py:47
  91.6 11.6 %collective-permute-done.16 = bf16[2,64,2560]{2,1,0:T(8,128)(2,1)S(1)} collective-permute-done((bf16[2,64,2560]{2,1,0:T(8,128)(2,1)S(1)}, bf16[2,64,2560]{2,1,0:T(8,128)(2,1)S(1)}, u32[]{:S(2)}, u32[]{:S(2)}) %collective-permute-start.16) | collective-permute-done | bytes 655392 | tf_op jit(solution)/shard_map/ppermute | solution.py:47
  103.8 1.3 fusion.19.refs_0_
  105.0 1.2 fusion.16
  106.3 1.9 %collective-permute-start.20 = (bf16[800,256]{1,0:T(8,128)(2,1)S(1)}, bf16[800,256]{1,0:T(8,128)(2,1)S(1)}, u32[]{:S(2)}, u32[]{:S(2)}) collective-permute-start(bf16[800,256]{1,0:T(8,128)(2,1)S(1)} %fusion.16), channel_id=1, source_target_pairs={{0,24},{8,16},{16,8},{24,0},{1,25},{9,17},{17,9},{25,1},{2,26},{10... | collective-permute-start | bytes 1228808 | tf_op jit(solution)/shard_map/ppermute | solution.py:47
  108.2 7.7 %collective-permute-done.19 = bf16[2,64,2560]{2,1,0:T(8,128)(2,1)S(1)} collective-permute-done((bf16[2,64,2560]{2,1,0:T(8,128)(2,1)S(1)}, bf16[2,64,2560]{2,1,0:T(8,128)(2,1)S(1)}, u32[]{:S(2)}, u32[]{:S(2)}) %collective-permute-start.19) | collective-permute-done | bytes 655392 | tf_op jit(solution)/shard_map/ppermute | solution.py:47
  115.9 4.9 %collective-permute-done.18 = bf16[2,64,2560]{2,1,0:T(8,128)(2,1)S(1)} collective-permute-done((bf16[2,64,2560]{2,1,0:T(8,128)(2,1)S(1)}, bf16[2,64,2560]{2,1,0:T(8,128)(2,1)S(1)}, u32[]{:S(2)}, u32[]{:S(2)}) %collective-permute-start.18) | collective-permute-done | bytes 655392 | tf_op jit(solution)/shard_map/ppermute | solution.py:47
  121.1 6.2 %collective-permute-done.20.refs_3_ = bf16[800,256]{1,0:T(8,128)(2,1)S(1)} collective-permute-done((bf16[800,256]{1,0:T(8,128)(2,1)S(1)}, bf16[800,256]{1,0:T(8,128)(2,1)S(1)}, u32[]{:S(2)}, u32[]{:S(2)}) %collective-permute-start.20) | collective-permute-done | bytes 409632 | tf_op jit(solution)/shard_map/ppermute | solution.py:47
  127.3 5.7 %shard_map.90 = (bf16[256,3200]{1,0:T(8,128)(2,1)}, bf16[256,3200]{1,0:T(8,128)(2,1)}) custom-call(s32[4]{0:T(128)S(1)} %pad_add_fusion.place, bf16[256,3200]{1,0:T(8,128)(2,1)S(1)} %copy-done, bf16[256,3200]{1,0:T(8,128)(2,1)S(1)} %copy-done.2, bf16[800,256]{1,0:T(8,128)(2,1)S(1)} %fusion.19.refs_0_, bf16[800,256]{1,0:T(8,128)(2,1)S(1)} %collective-permute-done.22.refs_1_, ...), custom_call_target="tpu_custom_call" | custom-call | flops 19660800 | bytes 8192000 | tf_op jit(solution)/shard_map/pallas_call | solution.py:52
  133.0 1.2 fusion.30
  134.2 1.5 %collective-permute-done.23 = bf16[400,2560]{1,0:T(8,128)(2,1)S(1)} collective-permute-done((bf16[400,2560]{1,0:T(8,128)(2,1)S(1)}, bf16[400,2560]{1,0:T(8,128)(2,1)S(1)}, u32[]{:S(2)}, u32[]{:S(2)}) %collective-permute-start.23) | collective-permute-done | bytes 2048032 | tf_op jit(solution)/shard_map/ppermute | solution.py:47
  135.7 3.2 %fusion.2 = f32[400,2560]{1,0:T(8,128)} fusion(f32[400,2560]{1,0:T(8,128)S(1)} %fusion.30, bf16[400,512]{1,0:T(8,128)(2,1)S(1)} %get-tuple-element.110, bf16[512,2560]{1,0:T(8,128)(2,1)S(1)} %shard_map.88, bf16[400,2560]{1,0:T(8,128)(2,1)S(1)} %collective-permute-done.23), kind=kOutput, calls=%fused_computation.5 | convolution fusion | flops 1052672000 | bytes 13271040 | tf_op jit(solution)/shard_map/dot_general | solution.py:174
  138.9 2.4 %collective-permute-done.21 = bf16[64,2560]{1,0:T(8,128)(2,1)S(1)} collective-permute-done((bf16[64,2560]{1,0:T(8,128)(2,1)S(1)}, bf16[64,2560]{1,0:T(8,128)(2,1)S(1)}, u32[]{:S(2)}, u32[]{:S(2)}) %collective-permute-start.21) | collective-permute-done | bytes 327712 | tf_op jit(solution)/shard_map/ppermute | solution.py:47
  141.2 0.8 fusion.28
  (40 shorter events, 3.9 us)
Async XLA Ops:
  0.6 12.5 %copy-start = (bf16[256,3200]{1,0:T(8,128)(2,1)S(1)}, bf16[256,3200]{1,0:T(8,128)(2,1)}, u32[]{:S(2)}) copy-start(bf16[256,3200]{1,0:T(8,128)(2,1)} %gate.3) | copy-start | bytes 4915204
  0.6 19.2 %collective-permute-start = (bf16[64,2560]{1,0:T(8,128)(2,1)}, bf16[64,2560]{1,0:T(8,128)(2,1)S(1)}, u32[]{:S(2)}, u32[]{:S(2)}) collective-permute-start(bf16[64,2560]{1,0:T(8,128)(2,1)} %refs_0_.1), channel_id=1, source_target_pairs={{0,16},{8,24},{16,0},{24,8},{1,17},{9,25},{17,1},{25,9},{2,18},{10... | collective-permute-start | bytes 983048 | tf_op jit(solution)/shard_map/ppermute | solution.py:47
  4.7 15.2 %collective-permute-start.1 = (bf16[64,2560]{1,0:T(8,128)(2,1)}, bf16[64,2560]{1,0:T(8,128)(2,1)S(1)}, u32[]{:S(2)}, u32[]{:S(2)}) collective-permute-start(bf16[64,2560]{1,0:T(8,128)(2,1)} %refs_0_.1), channel_id=1, source_target_pairs={{0,8},{8,0},{16,24},{24,16},{1,9},{9,1},{17,25},{25,17},{2,10},{10... | collective-permute-start | bytes 983048 | tf_op jit(solution)/shard_map/ppermute | solution.py:47
  6.3 13.7 %collective-permute-start.2 = (bf16[64,2560]{1,0:T(8,128)(2,1)}, bf16[64,2560]{1,0:T(8,128)(2,1)S(1)}, u32[]{:S(2)}, u32[]{:S(2)}) collective-permute-start(bf16[64,2560]{1,0:T(8,128)(2,1)} %refs_0_.1), channel_id=1, source_target_pairs={{0,2},{2,0},{1,3},{3,1},{4,6},{6,4},{5,7},{7,5},{8,10},{10,8},{9,1... | collective-permute-start | bytes 983048 | tf_op jit(solution)/shard_map/ppermute | solution.py:47
  7.8 12.1 %collective-permute-start.3 = (bf16[64,2560]{1,0:T(8,128)(2,1)}, bf16[64,2560]{1,0:T(8,128)(2,1)S(1)}, u32[]{:S(2)}, u32[]{:S(2)}) collective-permute-start(bf16[64,2560]{1,0:T(8,128)(2,1)} %refs_0_.1), channel_id=1, source_target_pairs={{0,1},{1,0},{2,3},{3,2},{4,5},{5,4},{6,7},{7,6},{8,9},{9,8},{10,11... | collective-permute-start | bytes 983048 | tf_op jit(solution)/shard_map/ppermute | solution.py:47
  8.8 1.6 %copy-start.3 = (bf16[400,2560]{1,0:T(8,128)(2,1)S(1)}, bf16[400,2560]{1,0:T(8,128)(2,1)}, u32[]{:S(2)}) copy-start(bf16[400,2560]{1,0:T(8,128)(2,1)} %codes.1) | copy-start | bytes 6144004
  11.5 33.1 %collective-permute-start.7 = (bf16[400,1536]{1,0:T(8,128)(2,1)S(1)}, bf16[400,1536]{1,0:T(8,128)(2,1)S(1)}, u32[]{:S(2)}, u32[]{:S(2)}) collective-permute-start(bf16[400,1536]{1,0:T(8,128)(2,1)S(1)} %get-tuple-element.74.own_a), channel_id=1, source_target_pairs={{0,4},{4,0},{1,5},{5,1},{2,6},{6,2},{3,7},{7,3},{8,12},{12,8},{9,1... | collective-permute-start | bytes 3686408 | tf_op jit(solution)/shard_map/ppermute | solution.py:47
  13.1 1.4 %copy-start.1 = (bf16[256,3200]{1,0:T(8,128)(2,1)S(1)}, bf16[256,3200]{1,0:T(8,128)(2,1)}, u32[]{:S(2)}) copy-start(bf16[256,3200]{1,0:T(8,128)(2,1)} %up.3) | copy-start | bytes 4915204
  20.0 12.9 %collective-permute-start.4 = (bf16[64,2560]{1,0:T(8,128)(2,1)S(1)}, bf16[64,2560]{1,0:T(8,128)(2,1)S(1)}, u32[]{:S(2)}, u32[]{:S(2)}) collective-permute-start(bf16[64,2560]{1,0:T(8,128)(2,1)S(1)} %collective-permute-done.refs_3_), channel_id=1, source_target_pairs={{0,8},{8,0},{16,24},{24,16},{1,9},{9,1},{17,25},{25,17},{2,10},{10... | collective-permute-start | bytes 983048 | tf_op jit(solution)/shard_map/ppermute | solution.py:47
  21.6 23.1 %collective-permute-start.8 = (bf16[3,64,2560]{2,1,0:T(8,128)(2,1)S(1)}, bf16[3,64,2560]{2,1,0:T(8,128)(2,1)S(1)}, u32[]{:S(2)}, u32[]{:S(2)}) collective-permute-start(bf16[3,64,2560]{2,1,0:T(8,128)(2,1)S(1)} %pad_maximum_fusion), channel_id=1, source_target_pairs={{0,1},{1,0},{2,3},{3,2},{4,5},{5,4},{6,7},{7,6},{8,9},{9,8},{10,11... | collective-permute-start | bytes 2949128 | tf_op jit(solution)/shard_map/ppermute | solution.py:47
  21.7 22.9 %collective-permute-start.5 = (bf16[2,64,2560]{2,1,0:T(8,128)(2,1)S(1)}, bf16[2,64,2560]{2,1,0:T(8,128)(2,1)S(1)}, u32[]{:S(2)}, u32[]{:S(2)}) collective-permute-start(bf16[2,64,2560]{2,1,0:T(8,128)(2,1)S(1)} %pad_maximum_fusion.2), channel_id=1, source_target_pairs={{0,2},{2,0},{1,3},{3,1},{4,6},{6,4},{5,7},{7,5},{8,10},{10,8},{9,1... | collective-permute-start | bytes 1966088 | tf_op jit(solution)/shard_map/ppermute | solution.py:47
  23.3 21.3 %collective-permute-start.6 = (bf16[800,256]{1,0:T(8,128)(2,1)S(1)}, bf16[800,256]{1,0:T(8,128)(2,1)S(1)}, u32[]{:S(2)}, u32[]{:S(2)}) collective-permute-start(bf16[800,256]{1,0:T(8,128)(2,1)S(1)} %get-tuple-element.73), channel_id=1, source_target_pairs={{0,16},{8,24},{16,0},{24,8},{1,17},{9,25},{17,1},{25,9},{2,18},{10... | collective-permute-start | bytes 1228808 | tf_op jit(solution)/shard_map/ppermute | solution.py:47
  32.9 25.7 %collective-permute-start.12 = (bf16[400,1024]{1,0:T(8,128)(2,1)S(1)}, bf16[400,1024]{1,0:T(8,128)(2,1)S(1)}, u32[]{:S(2)}, u32[]{:S(2)}) collective-permute-start(bf16[400,1024]{1,0:T(8,128)(2,1)S(1)} %get-tuple-element.83.own_b), channel_id=1, source_target_pairs={{0,4},{4,0},{1,5},{5,1},{2,6},{6,2},{3,7},{7,3},{8,12},{12,8},{9,1... | collective-permute-start | bytes 2457608 | tf_op jit(solution)/shard_map/ppermute | solution.py:47
  44.6 14.3 %collective-permute-start.10 = (bf16[800,256]{1,0:T(8,128)(2,1)S(1)}, bf16[800,256]{1,0:T(8,128)(2,1)S(1)}, u32[]{:S(2)}, u32[]{:S(2)}) collective-permute-start(bf16[800,256]{1,0:T(8,128)(2,1)S(1)} %get-tuple-element.81), channel_id=1, source_target_pairs={{0,24},{8,16},{16,8},{24,0},{1,25},{9,17},{17,9},{25,1},{2,26},{10... | collective-permute-start | bytes 1228808 | tf_op jit(solution)/shard_map/ppermute | solution.py:47
  46.6 19.3 %collective-permute-start.11 = (bf16[800,256]{1,0:T(8,128)(2,1)S(1)}, bf16[800,256]{1,0:T(8,128)(2,1)S(1)}, u32[]{:S(2)}, u32[]{:S(2)}) collective-permute-start(bf16[800,256]{1,0:T(8,128)(2,1)S(1)} %get-tuple-element.82), channel_id=1, source_target_pairs={{0,8},{8,0},{16,24},{24,16},{1,9},{9,1},{17,25},{25,17},{2,10},{10... | collective-permute-start | bytes 1228808 | tf_op jit(solution)/shard_map/ppermute | solution.py:47
  46.6 12.0 %collective-permute-start.9 = (bf16[64,2560]{1,0:T(8,128)(2,1)S(1)}, bf16[64,2560]{1,0:T(8,128)(2,1)S(1)}, u32[]{:S(2)}, u32[]{:S(2)}) collective-permute-start(bf16[64,2560]{1,0:T(8,128)(2,1)S(1)} %collective-permute-done.4.refs_1_), channel_id=1, source_target_pairs={{0,2},{2,0},{1,3},{3,1},{4,6},{6,4},{5,7},{7,5},{8,10},{10,8},{9,1... | collective-permute-start | bytes 983048 | tf_op jit(solution)/shard_map/ppermute | solution.py:47
  70.9 10.5 %collective-permute-start.15 = (bf16[512,2560]{1,0:T(8,128)(2,1)S(1)}, bf16[512,2560]{1,0:T(8,128)(2,1)S(1)}, u32[]{:S(2)}, u32[]{:S(2)}) collective-permute-start(bf16[512,2560]{1,0:T(8,128)(2,1)S(1)} %convolution_convert_fusion), channel_id=1, source_target_pairs={{0,1},{1,0},{2,3},{3,2},{4,5},{5,4},{6,7},{7,6},{8,9},{9,8},{10,11... | collective-permute-start | bytes 7864328 | tf_op jit(solution)/shard_map/ppermute | solution.py:47
  71.1 6.7 %collective-permute-start.13 = (bf16[3,64,2560]{2,1,0:T(8,128)(2,1)S(1)}, bf16[3,64,2560]{2,1,0:T(8,128)(2,1)S(1)}, u32[]{:S(2)}, u32[]{:S(2)}) collective-permute-start(bf16[3,64,2560]{2,1,0:T(8,128)(2,1)S(1)} %pad_maximum_fusion.1), channel_id=1, source_target_pairs={{0,1},{1,0},{2,3},{3,2},{4,5},{5,4},{6,7},{7,6},{8,9},{9,8},{10,11... | collective-permute-start | bytes 2949128 | tf_op jit(solution)/shard_map/ppermute | solution.py:47
  71.6 6.1 %collective-permute-start.14 = (bf16[64,2560]{1,0:T(8,128)(2,1)S(1)}, bf16[64,2560]{1,0:T(8,128)(2,1)S(1)}, u32[]{:S(2)}, u32[]{:S(2)}) collective-permute-start(bf16[64,2560]{1,0:T(8,128)(2,1)S(1)} %collective-permute-done.9.refs_2_), channel_id=1, source_target_pairs={{0,1},{1,0},{2,3},{3,2},{4,5},{5,4},{6,7},{7,6},{8,9},{9,8},{10,11... | collective-permute-start | bytes 983048 | tf_op jit(solution)/shard_map/ppermute | solution.py:47
  74.8 3.7 %copy-start.4 = (bf16[64,2560]{1,0:T(8,128)(2,1)S(1)}, bf16[64,2560]{1,0:T(8,128)(2,1)}, u32[]{:S(2)}) copy-start(bf16[64,2560]{1,0:T(8,128)(2,1)} %refs_0_.1) | copy-start | bytes 983044
  80.4 22.9 %collective-permute-start.17 = (bf16[800,256]{1,0:T(8,128)(2,1)S(1)}, bf16[800,256]{1,0:T(8,128)(2,1)S(1)}, u32[]{:S(2)}, u32[]{:S(2)}) collective-permute-start(bf16[800,256]{1,0:T(8,128)(2,1)S(1)} %fusion.13), channel_id=1, source_target_pairs={{0,16},{8,24},{16,0},{24,8},{1,17},{9,25},{17,1},{25,9},{2,18},{10... | collective-permute-start | bytes 1228808 | tf_op jit(solution)/shard_map/ppermute | solution.py:47
  83.4 44.0 %collective-permute-start.22 = (bf16[800,256]{1,0:T(8,128)(2,1)S(1)}, bf16[800,256]{1,0:T(8,128)(2,1)S(1)}, u32[]{:S(2)}, u32[]{:S(2)}) collective-permute-start(bf16[800,256]{1,0:T(8,128)(2,1)S(1)} %fusion.22), channel_id=1, source_target_pairs={{0,8},{8,0},{16,24},{24,16},{1,9},{9,1},{17,25},{25,17},{2,10},{10... | collective-permute-start | bytes 1228808 | tf_op jit(solution)/shard_map/ppermute | solution.py:47
  85.5 17.7 %collective-permute-start.16 = (bf16[2,64,2560]{2,1,0:T(8,128)(2,1)S(1)}, bf16[2,64,2560]{2,1,0:T(8,128)(2,1)S(1)}, u32[]{:S(2)}, u32[]{:S(2)}) collective-permute-start(bf16[2,64,2560]{2,1,0:T(8,128)(2,1)S(1)} %get-tuple-element.129), channel_id=1, source_target_pairs={{0,2},{2,0},{1,3},{3,1},{4,6},{6,4},{5,7},{7,5},{8,10},{10,8},{9,1... | collective-permute-start | bytes 1966088 | tf_op jit(solution)/shard_map/ppermute | solution.py:47
  86.1 29.8 %collective-permute-start.19 = (bf16[2,64,2560]{2,1,0:T(8,128)(2,1)S(1)}, bf16[2,64,2560]{2,1,0:T(8,128)(2,1)S(1)}, u32[]{:S(2)}, u32[]{:S(2)}) collective-permute-start(bf16[2,64,2560]{2,1,0:T(8,128)(2,1)S(1)} %get-tuple-element.128), channel_id=1, source_target_pairs={{0,2},{2,0},{1,3},{3,1},{4,6},{6,4},{5,7},{7,5},{8,10},{10,8},{9,1... | collective-permute-start | bytes 1966088 | tf_op jit(solution)/shard_map/ppermute | solution.py:47
  90.1 45.6 %collective-permute-start.23 = (bf16[400,2560]{1,0:T(8,128)(2,1)S(1)}, bf16[400,2560]{1,0:T(8,128)(2,1)S(1)}, u32[]{:S(2)}, u32[]{:S(2)}) collective-permute-start(bf16[400,2560]{1,0:T(8,128)(2,1)S(1)} %fusion.3), channel_id=1, source_target_pairs={{0,4},{4,0},{1,5},{5,1},{2,6},{6,2},{3,7},{7,3},{8,12},{12,8},{9,1... | collective-permute-start | bytes 6144008 | tf_op jit(solution)/shard_map/ppermute | solution.py:47
  103.4 17.4 %collective-permute-start.18 = (bf16[2,64,2560]{2,1,0:T(8,128)(2,1)S(1)}, bf16[2,64,2560]{2,1,0:T(8,128)(2,1)S(1)}, u32[]{:S(2)}, u32[]{:S(2)}) collective-permute-start(bf16[2,64,2560]{2,1,0:T(8,128)(2,1)S(1)} %fusion.4), channel_id=1, source_target_pairs={{0,8},{8,0},{16,24},{24,16},{1,9},{9,1},{17,25},{25,17},{2,10},{10... | collective-permute-start | bytes 1966088 | tf_op jit(solution)/shard_map/ppermute | solution.py:47
  106.3 21.0 %collective-permute-start.20 = (bf16[800,256]{1,0:T(8,128)(2,1)S(1)}, bf16[800,256]{1,0:T(8,128)(2,1)S(1)}, u32[]{:S(2)}, u32[]{:S(2)}) collective-permute-start(bf16[800,256]{1,0:T(8,128)(2,1)S(1)} %fusion.16), channel_id=1, source_target_pairs={{0,24},{8,16},{16,8},{24,0},{1,25},{9,17},{17,9},{25,1},{2,26},{10... | collective-permute-start | bytes 1228808 | tf_op jit(solution)/shard_map/ppermute | solution.py:47
  120.9 6.4 %copy-start.2 = (bf16[256,3200]{1,0:T(8,128)(2,1)S(1)}, bf16[256,3200]{1,0:T(8,128)(2,1)}, u32[]{:S(2)}) copy-start(bf16[256,3200]{1,0:T(8,128)(2,1)} %up.3) | copy-start | bytes 4915204
  127.3 13.9 %collective-permute-start.21 = (bf16[64,2560]{1,0:T(8,128)(2,1)S(1)}, bf16[64,2560]{1,0:T(8,128)(2,1)S(1)}, u32[]{:S(2)}, u32[]{:S(2)}) collective-permute-start(bf16[64,2560]{1,0:T(8,128)(2,1)S(1)} %fusion.29), channel_id=1, source_target_pairs={{0,16},{8,24},{16,0},{24,8},{1,17},{9,25},{17,1},{25,9},{2,18},{10... | collective-permute-start | bytes 983048 | tf_op jit(solution)/shard_map/ppermute | solution.py:47

commit v3 on v2

--- a/solution.py
+++ b/solution.py
@@ -270,37 +270,38 @@
         rows_of_k = flat[k % 2][k // 2 * group_rows : (k // 2 + 1) * group_rows]
         return matmul(weight, rows_of_k, 1, 1, bf16)
 
-    over_c = exchange(matmul(send, weight, dtype=bf16), "c", 1)
+    flat = [even, odd]
+    far_back = back_of(2)
+    far_back, send = barrier((far_back, send))
+    given = matmul(send, weight, dtype=bf16)
+    given, flat = barrier((given, flat))
+    over_c = exchange(given, "c", 1)
+    theirs = grad_half(1).astype(bf16)
+    theirs, keep, flat = barrier((theirs, keep, flat))
+    over_x = exchange(theirs, "x", 1)
     kept = matmul(keep, weight, dtype=bf16)
-    kept, flat = barrier((kept, [even, odd]))
-    far_back = back_of(2)
-    kept, far_back = barrier((kept, far_back))
     sums = (kept.astype(f32) + over_c.astype(f32)).reshape(2, nz, rows, width)
     sums, flat = barrier((sums, flat))
     odd_y = exchange(sums[1, :2].astype(bf16), "y", 1)
     even_y = exchange(sums[1, 2:].astype(bf16), "y", 1)
-    over_x = exchange(grad_half(1).astype(bf16), "x", 1)
-    near_back = exchange(back_of(1), "z", 1)
+    near_back, last_back = exchange(back_of(1), "z", 1), exchange(back_of(3), "z", 3)
     odd_y, flat = barrier((odd_y, flat))
-    back = [back_of(0), near_back, exchange(far_back, "z", 2), exchange(back_of(3), "z", 3)]
+    back = [back_of(0), near_back, exchange(far_back, "z", 2), last_back]
+    own_grad = grad_half(0)
     odd_sum = (sums[0, :2] + odd_y.astype(f32)).astype(bf16)
     odd_sum, back[2] = barrier((odd_sum, back[2]))
-    near_sum, even_y = barrier((exchange(odd_sum, "z", 1), even_y))
-    near_sum = near_sum.astype(f32)
-    even_sum = sums[0, 2:] + even_y.astype(f32)
-    ours, across = even_sum[0] + near_sum[0], (even_sum[1] + near_sum[1]).astype(bf16)
-    across, back[3] = barrier((across, back[3]))
-    far_sum = exchange(across, "z", 2)
-
-    back, flat, _ = barrier((back, flat, across))
-    own_grad = grad_half(0)
+    near_sum = exchange(odd_sum, "z", 1)
     gate_grad, up_grad = call_kernel(
         functools.partial(grads_kernel, nz, units), place, (gate_pre, up_pre, *back),
         [wide] * 2 + [whole((units, group_rows))] * nz,
         [struct((group_rows, local_hidden), bf16)] * 2, [wide] * 2, (steps,), act_scratch[::-1],
         (12 * act_bytes, 5 * act_bytes, act_bytes // 2),
     )
-    over_x, _ = barrier((over_x, gate_grad))
+    near_sum, even_y, gate_grad, own_grad = barrier((near_sum, even_y, gate_grad, own_grad))
+    near_sum = near_sum.astype(f32)
+    even_sum = sums[0, 2:] + even_y.astype(f32)
+    ours, across = even_sum[0] + near_sum[0], (even_sum[1] + near_sum[1]).astype(bf16)
+    far_sum = exchange(across, "z", 2)
     weight_grad = own_grad + over_x.astype(f32)
     far_sum, weight_grad = barrier((far_sum, weight_grad))
     layer_out = (ours + far_sum.astype(f32)).astype(bf16)

time: 142 us -> 147 us (1.035)
  waiting for transfers between devices: 76.1 us -> 79.8 us
  other arithmetic: 2.59 us -> 5.19 us
  matrix products: 18.1 us -> 16.1 us
    ppermute x24, waiting for transfers between devices: 76.1 us -> 79.8 us  [exchange(): return lax.ppermute(value, axis, [(i, i ^ offset) for i in range(size)])]
    add x0 -> x1, other arithmetic: none -> 2.56 us  [paired_body(): weight_grad = own_grad + over_x.astype(f32)]
    dot_general x10, matrix products: 18.1 us -> 16.1 us  [matmul(): lax.dot_general(lhs, rhs, dims, preferred_element_type=jnp.float32)]
  transfers between devices with their start and end apart: 24 -> 24, of which waited for: 14 -> 10; matrix products, arithmetic and copies ran while one was open for 13% -> 15% of each run, Pallas kernels for 8% -> 8%
where the time goes in v3:
time: 147 us
  waiting for transfers between devices  79.8 us (54%)
  starting transfers between devices  27.7 us (19%)
  matrix products  16.1 us (11%)
  Pallas kernels  13.2 us (9%)
  other arithmetic  5.19 us (4%)
  local copies, waits for them, and re-layouts  4 us (3%)
    ppermute x24, waiting for transfers between devices, exchange(): return lax.ppermute(value, axis, [(i, i ^ offset) for i in range(size)])  79.8 us
    ppermute x24, starting transfers between devices, exchange(): return lax.ppermute(value, axis, [(i, i ^ offset) for i in range(size)])  27.7 us
    dot_general x10, matrix products, matmul(): lax.dot_general(lhs, rhs, dims, preferred_element_type=jnp.float32)  16.1 us
    pallas_call x7, Pallas kernels, call_kernel(): pl.pallas_call(kernel, out_shape=out_shapes, grid_spec=pltpu.PrefetchScal...  13.2 us
    unnamed x11, local copies, waits for them, and re-layouts  3.9 us
  transfers between devices with their start and end apart: 24, of which 10 were waited for; matrix products, arithmetic and copies ran while one was open for 15% of the time, Pallas kernels for 8%

profile of v3, /device:TPU:0, one launch (start us, length us, event | category | flops | bytes accessed | tf_op | source)
XLA Modules:
  0.0 146.9 jit_solution(2482805864412840549)
XLA Ops:
  0.6 3.0 %collective-permute-start.2 = (bf16[64,2560]{1,0:T(8,128)(2,1)}, bf16[64,2560]{1,0:T(8,128)(2,1)S(1)}, u32[]{:S(2)}, u32[]{:S(2)}) collective-permute-start(bf16[64,2560]{1,0:T(8,128)(2,1)} %refs_0_.1), channel_id=1, source_target_pairs={{0,2},{2,0},{1,3},{3,1},{4,6},{6,4},{5,7},{7,5},{8,10},{10,8},{9,1... | collective-permute-start | bytes 983048 | tf_op jit(solution)/shard_map/ppermute | solution.py:47
  3.7 1.6 %collective-permute-start.1 = (bf16[64,2560]{1,0:T(8,128)(2,1)}, bf16[64,2560]{1,0:T(8,128)(2,1)S(1)}, u32[]{:S(2)}, u32[]{:S(2)}) collective-permute-start(bf16[64,2560]{1,0:T(8,128)(2,1)} %refs_0_.1), channel_id=1, source_target_pairs={{0,8},{8,0},{16,24},{24,16},{1,9},{9,1},{17,25},{25,17},{2,10},{10... | collective-permute-start | bytes 983048 | tf_op jit(solution)/shard_map/ppermute | solution.py:47
  5.2 2.6 %collective-permute-start = (bf16[64,2560]{1,0:T(8,128)(2,1)}, bf16[64,2560]{1,0:T(8,128)(2,1)S(1)}, u32[]{:S(2)}, u32[]{:S(2)}) collective-permute-start(bf16[64,2560]{1,0:T(8,128)(2,1)} %refs_0_.1), channel_id=1, source_target_pairs={{0,16},{8,24},{16,0},{24,8},{1,17},{9,25},{17,1},{25,9},{2,18},{10... | collective-permute-start | bytes 983048 | tf_op jit(solution)/shard_map/ppermute | solution.py:47
  7.8 0.9 copy.9.scales
  8.8 1.6 %copy-done.3 = bf16[400,2560]{1,0:T(8,128)(2,1)S(1)} copy-done((bf16[400,2560]{1,0:T(8,128)(2,1)S(1)}, bf16[400,2560]{1,0:T(8,128)(2,1)}, u32[]{:S(2)}) %copy-start.3) | copy-done | bytes 2048024
  10.4 1.1 shard_map.85
  11.5 1.6 %collective-permute-start.7 = (bf16[400,1536]{1,0:T(8,128)(2,1)S(1)}, bf16[400,1536]{1,0:T(8,128)(2,1)S(1)}, u32[]{:S(2)}, u32[]{:S(2)}) collective-permute-start(bf16[400,1536]{1,0:T(8,128)(2,1)S(1)} %get-tuple-element.71.own_a), channel_id=1, source_target_pairs={{0,4},{4,0},{1,5},{5,1},{2,6},{6,2},{3,7},{7,3},{8,12},{12,8},{9,1... | collective-permute-start | bytes 3686408 | tf_op jit(solution)/shard_map/ppermute | solution.py:47
  13.1 1.4 copy-done.1
  14.5 2.8 %shard_map.84 = (bf16[800,256]{1,0:T(8,128)(2,1)S(1)}, bf16[800,256]{1,0:T(8,128)(2,1)S(1)}, bf16[800,256]{1,0:T(8,128)(2,1)S(1)}, bf16[800,256]{1,0:T(8,128)(2,1)S(1)}) custom-call(s32[4]{0:T(128)S(1)} %pad_add_fusion.place, bf16[256,3200]{1,0:T(8,128)(2,1)S(1)} %copy-done, bf16[256,3200]{1,0:T(8,128)(2,1)S(1)} %copy-done.1), custom_call_target="tpu_custom_call" | custom-call | flops 6553600 | bytes 4915200 | tf_op jit(solution)/shard_map/pallas_call | solution.py:52
  17.4 2.5 %collective-permute-done.1.refs_0_ = bf16[64,2560]{1,0:T(8,128)(2,1)S(1)} collective-permute-done((bf16[64,2560]{1,0:T(8,128)(2,1)}, bf16[64,2560]{1,0:T(8,128)(2,1)S(1)}, u32[]{:S(2)}, u32[]{:S(2)}) %collective-permute-start.1) | collective-permute-done | bytes 327712 | tf_op jit(solution)/shard_map/ppermute | solution.py:47
  19.9 2.4 %collective-permute-done.refs_3_ = bf16[64,2560]{1,0:T(8,128)(2,1)S(1)} collective-permute-done((bf16[64,2560]{1,0:T(8,128)(2,1)}, bf16[64,2560]{1,0:T(8,128)(2,1)S(1)}, u32[]{:S(2)}, u32[]{:S(2)}) %collective-permute-start) | collective-permute-done | bytes 327712 | tf_op jit(solution)/shard_map/ppermute | solution.py:47
  23.5 2.7 %collective-permute-start.4 = (bf16[64,2560]{1,0:T(8,128)(2,1)S(1)}, bf16[64,2560]{1,0:T(8,128)(2,1)S(1)}, u32[]{:S(2)}, u32[]{:S(2)}) collective-permute-start(bf16[64,2560]{1,0:T(8,128)(2,1)S(1)} %collective-permute-done.refs_3_), channel_id=1, source_target_pairs={{0,8},{8,0},{16,24},{24,16},{1,9},{9,1},{17,25},{25,17},{2,10},{10... | collective-permute-start | bytes 983048 | tf_op jit(solution)/shard_map/ppermute | solution.py:47
  26.2 13.5 %collective-permute-done.4.refs_1_ = bf16[64,2560]{1,0:T(8,128)(2,1)S(1)} collective-permute-done((bf16[64,2560]{1,0:T(8,128)(2,1)S(1)}, bf16[64,2560]{1,0:T(8,128)(2,1)S(1)}, u32[]{:S(2)}, u32[]{:S(2)}) %collective-permute-start.4) | collective-permute-done | bytes 327712 | tf_op jit(solution)/shard_map/ppermute | solution.py:47
  39.7 4.6 %collective-permute-done.6.refs_1_ = bf16[800,256]{1,0:T(8,128)(2,1)S(1)} collective-permute-done((bf16[800,256]{1,0:T(8,128)(2,1)S(1)}, bf16[800,256]{1,0:T(8,128)(2,1)S(1)}, u32[]{:S(2)}, u32[]{:S(2)}) %collective-permute-start.6) | collective-permute-done | bytes 409632 | tf_op jit(solution)/shard_map/ppermute | solution.py:47
  44.5 1.5 %collective-permute-start.12 = (bf16[400,1024]{1,0:T(8,128)(2,1)S(1)}, bf16[400,1024]{1,0:T(8,128)(2,1)S(1)}, u32[]{:S(2)}, u32[]{:S(2)}) collective-permute-start(bf16[400,1024]{1,0:T(8,128)(2,1)S(1)} %get-tuple-element.80.own_b), channel_id=1, source_target_pairs={{0,4},{4,0},{1,5},{5,1},{2,6},{6,2},{3,7},{7,3},{8,12},{12,8},{9,1... | collective-permute-start | bytes 2457608 | tf_op jit(solution)/shard_map/ppermute | solution.py:47
  46.1 1.3 collective-permute-start.10
  47.4 1.5 %collective-permute-start.9 = (bf16[64,2560]{1,0:T(8,128)(2,1)S(1)}, bf16[64,2560]{1,0:T(8,128)(2,1)S(1)}, u32[]{:S(2)}, u32[]{:S(2)}) collective-permute-start(bf16[64,2560]{1,0:T(8,128)(2,1)S(1)} %collective-permute-done.4.refs_1_), channel_id=1, source_target_pairs={{0,2},{2,0},{1,3},{3,1},{4,6},{6,4},{5,7},{7,5},{8,10},{10,8},{9,1... | collective-permute-start | bytes 983048 | tf_op jit(solution)/shard_map/ppermute | solution.py:47
  48.9 16.2 %collective-permute-done.12.other_b = bf16[400,1024]{1,0:T(8,128)(2,1)S(1)} collective-permute-done((bf16[400,1024]{1,0:T(8,128)(2,1)S(1)}, bf16[400,1024]{1,0:T(8,128)(2,1)S(1)}, u32[]{:S(2)}, u32[]{:S(2)}) %collective-permute-start.12) | collective-permute-done | bytes 819232 | tf_op jit(solution)/shard_map/ppermute | solution.py:47
  65.2 2.3 %collective-permute-done.11.refs_3_ = bf16[800,256]{1,0:T(8,128)(2,1)S(1)} collective-permute-done((bf16[800,256]{1,0:T(8,128)(2,1)S(1)}, bf16[800,256]{1,0:T(8,128)(2,1)S(1)}, u32[]{:S(2)}, u32[]{:S(2)}) %collective-permute-start.11) | collective-permute-done | bytes 409632 | tf_op jit(solution)/shard_map/ppermute | solution.py:47
  67.4 0.8 shard_map.87
  68.2 1.1 shard_map.86
  69.4 0.7 shard_map.88
  70.1 1.2 fusion.21
  71.4 3.1 %convolution_convert_fusion.1 = bf16[512,2560]{1,0:T(8,128)(2,1)S(1)} fusion(bf16[512,800]{1,0:T(8,128)(2,1)S(1)} %get-tuple-element.92, bf16[800,2560]{1,0:T(8,128)(2,1)S(1)} %shard_map.87), kind=kOutput, calls=%fused_computation.6 | convolution fusion | flops 2098462720 | bytes 7536640 | tf_op jit(solution)/shard_map/dot_general | solution.py:174
  74.5 0.7 shard_map.89
  75.8 1.3 collective-permute-start.17
  77.1 1.2 fusion.29
  78.4 1.2 fusion.2
  79.6 0.6 collective-permute-start.23
  80.2 3.1 %convolution_convert_fusion = bf16[512,2560]{1,0:T(8,128)(2,1)S(1)} fusion(bf16[512,800]{1,0:T(8,128)(2,1)S(1)} %get-tuple-element.98, bf16[800,2560]{1,0:T(8,128)(2,1)S(1)} %shard_map.87), kind=kOutput, calls=%fused_computation.5 | convolution fusion | flops 2098462720 | bytes 7536640 | tf_op jit(solution)/shard_map/dot_general | solution.py:174
  83.3 0.7 convert_add_fusion
  84.5 1.6 %collective-permute-start.16 = (bf16[2,64,2560]{2,1,0:T(8,128)(2,1)S(1)}, bf16[2,64,2560]{2,1,0:T(8,128)(2,1)S(1)}, u32[]{:S(2)}, u32[]{:S(2)}) collective-permute-start(bf16[2,64,2560]{2,1,0:T(8,128)(2,1)S(1)} %get-tuple-element.123), channel_id=1, source_target_pairs={{0,2},{2,0},{1,3},{3,1},{4,6},{6,4},{5,7},{7,5},{8,10},{10,8},{9,1... | collective-permute-start | bytes 1966088 | tf_op jit(solution)/shard_map/ppermute | solution.py:47
  86.1 1.2 fusion.15
  87.3 1.5 %collective-permute-start.20 = (bf16[800,256]{1,0:T(8,128)(2,1)S(1)}, bf16[800,256]{1,0:T(8,128)(2,1)S(1)}, u32[]{:S(2)}, u32[]{:S(2)}) collective-permute-start(bf16[800,256]{1,0:T(8,128)(2,1)S(1)} %fusion.15), channel_id=1, source_target_pairs={{0,8},{8,0},{16,24},{24,16},{1,9},{9,1},{17,25},{25,17},{2,10},{10... | collective-permute-start | bytes 1228808 | tf_op jit(solution)/shard_map/ppermute | solution.py:47
  88.8 1.2 fusion.18
  90.0 1.7 %collective-permute-start.21 = (bf16[800,256]{1,0:T(8,128)(2,1)S(1)}, bf16[800,256]{1,0:T(8,128)(2,1)S(1)}, u32[]{:S(2)}, u32[]{:S(2)}) collective-permute-start(bf16[800,256]{1,0:T(8,128)(2,1)S(1)} %fusion.18), channel_id=1, source_target_pairs={{0,24},{8,16},{16,8},{24,0},{1,25},{9,17},{17,9},{25,1},{2,26},{10... | collective-permute-start | bytes 1228808 | tf_op jit(solution)/shard_map/ppermute | solution.py:47
  91.8 8.9 %collective-permute-done.16 = bf16[2,64,2560]{2,1,0:T(8,128)(2,1)S(1)} collective-permute-done((bf16[2,64,2560]{2,1,0:T(8,128)(2,1)S(1)}, bf16[2,64,2560]{2,1,0:T(8,128)(2,1)S(1)}, u32[]{:S(2)}, u32[]{:S(2)}) %collective-permute-start.16) | collective-permute-done | bytes 655392 | tf_op jit(solution)/shard_map/ppermute | solution.py:47
  100.7 1.5 %collective-permute-start.19 = (bf16[2,64,2560]{2,1,0:T(8,128)(2,1)S(1)}, bf16[2,64,2560]{2,1,0:T(8,128)(2,1)S(1)}, u32[]{:S(2)}, u32[]{:S(2)}) collective-permute-start(bf16[2,64,2560]{2,1,0:T(8,128)(2,1)S(1)} %get-tuple-element.122), channel_id=1, source_target_pairs={{0,2},{2,0},{1,3},{3,1},{4,6},{6,4},{5,7},{7,5},{8,10},{10,8},{9,1... | collective-permute-start | bytes 1966088 | tf_op jit(solution)/shard_map/ppermute | solution.py:47
  102.3 1.3 fusion.12.refs_0_
  103.6 1.4 collective-permute-start.18
  105.1 1.2 fusion.30
  106.3 8.1 %collective-permute-done.20.refs_1_ = bf16[800,256]{1,0:T(8,128)(2,1)S(1)} collective-permute-done((bf16[800,256]{1,0:T(8,128)(2,1)S(1)}, bf16[800,256]{1,0:T(8,128)(2,1)S(1)}, u32[]{:S(2)}, u32[]{:S(2)}) %collective-permute-start.20) | collective-permute-done | bytes 409632 | tf_op jit(solution)/shard_map/ppermute | solution.py:47
  114.4 5.8 %shard_map.90 = (bf16[256,3200]{1,0:T(8,128)(2,1)}, bf16[256,3200]{1,0:T(8,128)(2,1)}) custom-call(s32[4]{0:T(128)S(1)} %pad_add_fusion.place, bf16[256,3200]{1,0:T(8,128)(2,1)S(1)} %copy-done, bf16[256,3200]{1,0:T(8,128)(2,1)S(1)} %copy-done.2, bf16[800,256]{1,0:T(8,128)(2,1)S(1)} %fusion.12.refs_0_, bf16[800,256]{1,0:T(8,128)(2,1)S(1)} %collective-permute-done.20.refs_1_, ...), custom_call_target="tpu_custom_call" | custom-call | flops 19660800 | bytes 8192000 | tf_op jit(solution)/shard_map/pallas_call | solution.py:52
  120.2 1.2 fusion
  121.5 6.9 %collective-permute-done.18 = bf16[2,64,2560]{2,1,0:T(8,128)(2,1)S(1)} collective-permute-done((bf16[2,64,2560]{2,1,0:T(8,128)(2,1)S(1)}, bf16[2,64,2560]{2,1,0:T(8,128)(2,1)S(1)}, u32[]{:S(2)}, u32[]{:S(2)}) %collective-permute-start.18) | collective-permute-done | bytes 655392 | tf_op jit(solution)/shard_map/ppermute | solution.py:47
  129.2 2.6 %convert_add_fusion.1 = f32[400,2560]{1,0:T(8,128)} fusion(f32[400,2560]{1,0:T(8,128)S(1)} %fusion, bf16[400,2560]{1,0:T(8,128)(2,1)S(1)} %collective-permute-done.23), kind=kLoop, calls=%fused_computation.8 | loop fusion | flops 2048000 | bytes 10240000 | tf_op jit(solution)/shard_map/add | solution.py:305
  131.8 14.3 %collective-permute-done.22 = bf16[64,2560]{1,0:T(8,128)(2,1)S(1)} collective-permute-done((bf16[64,2560]{1,0:T(8,128)(2,1)S(1)}, bf16[64,2560]{1,0:T(8,128)(2,1)S(1)}, u32[]{:S(2)}, u32[]{:S(2)}) %collective-permute-start.22) | collective-permute-done | bytes 327712 | tf_op jit(solution)/shard_map/ppermute | solution.py:47
  146.0 0.8 fusion.27
  (41 shorter events, 3.4 us)
Async XLA Ops:
  0.6 12.5 %copy-start = (bf16[256,3200]{1,0:T(8,128)(2,1)S(1)}, bf16[256,3200]{1,0:T(8,128)(2,1)}, u32[]{:S(2)}) copy-start(bf16[256,3200]{1,0:T(8,128)(2,1)} %gate.3) | copy-start | bytes 4915204
  0.6 16.8 %collective-permute-start.2 = (bf16[64,2560]{1,0:T(8,128)(2,1)}, bf16[64,2560]{1,0:T(8,128)(2,1)S(1)}, u32[]{:S(2)}, u32[]{:S(2)}) collective-permute-start(bf16[64,2560]{1,0:T(8,128)(2,1)} %refs_0_.1), channel_id=1, source_target_pairs={{0,2},{2,0},{1,3},{3,1},{4,6},{6,4},{5,7},{7,5},{8,10},{10,8},{9,1... | collective-permute-start | bytes 983048 | tf_op jit(solution)/shard_map/ppermute | solution.py:47
  3.7 16.3 %collective-permute-start.1 = (bf16[64,2560]{1,0:T(8,128)(2,1)}, bf16[64,2560]{1,0:T(8,128)(2,1)S(1)}, u32[]{:S(2)}, u32[]{:S(2)}) collective-permute-start(bf16[64,2560]{1,0:T(8,128)(2,1)} %refs_0_.1), channel_id=1, source_target_pairs={{0,8},{8,0},{16,24},{24,16},{1,9},{9,1},{17,25},{25,17},{2,10},{10... | collective-permute-start | bytes 983048 | tf_op jit(solution)/shard_map/ppermute | solution.py:47
  5.2 17.1 %collective-permute-start = (bf16[64,2560]{1,0:T(8,128)(2,1)}, bf16[64,2560]{1,0:T(8,128)(2,1)S(1)}, u32[]{:S(2)}, u32[]{:S(2)}) collective-permute-start(bf16[64,2560]{1,0:T(8,128)(2,1)} %refs_0_.1), channel_id=1, source_target_pairs={{0,16},{8,24},{16,0},{24,8},{1,17},{9,25},{17,1},{25,9},{2,18},{10... | collective-permute-start | bytes 983048 | tf_op jit(solution)/shard_map/ppermute | solution.py:47
  7.8 14.5 %collective-permute-start.3 = (bf16[64,2560]{1,0:T(8,128)(2,1)}, bf16[64,2560]{1,0:T(8,128)(2,1)S(1)}, u32[]{:S(2)}, u32[]{:S(2)}) collective-permute-start(bf16[64,2560]{1,0:T(8,128)(2,1)} %refs_0_.1), channel_id=1, source_target_pairs={{0,1},{1,0},{2,3},{3,2},{4,5},{5,4},{6,7},{7,6},{8,9},{9,8},{10,11... | collective-permute-start | bytes 983048 | tf_op jit(solution)/shard_map/ppermute | solution.py:47
  8.8 1.6 %copy-start.3 = (bf16[400,2560]{1,0:T(8,128)(2,1)S(1)}, bf16[400,2560]{1,0:T(8,128)(2,1)}, u32[]{:S(2)}) copy-start(bf16[400,2560]{1,0:T(8,128)(2,1)} %codes.1) | copy-start | bytes 6144004
  11.5 32.8 %collective-permute-start.7 = (bf16[400,1536]{1,0:T(8,128)(2,1)S(1)}, bf16[400,1536]{1,0:T(8,128)(2,1)S(1)}, u32[]{:S(2)}, u32[]{:S(2)}) collective-permute-start(bf16[400,1536]{1,0:T(8,128)(2,1)S(1)} %get-tuple-element.71.own_a), channel_id=1, source_target_pairs={{0,4},{4,0},{1,5},{5,1},{2,6},{6,2},{3,7},{7,3},{8,12},{12,8},{9,1... | collective-permute-start | bytes 3686408 | tf_op jit(solution)/shard_map/ppermute | solution.py:47
  13.1 1.4 copy-start.1
  22.5 21.9 %collective-permute-start.8 = (bf16[3,64,2560]{2,1,0:T(8,128)(2,1)S(1)}, bf16[3,64,2560]{2,1,0:T(8,128)(2,1)S(1)}, u32[]{:S(2)}, u32[]{:S(2)}) collective-permute-start(bf16[3,64,2560]{2,1,0:T(8,128)(2,1)S(1)} %pad_maximum_fusion), channel_id=1, source_target_pairs={{0,1},{1,0},{2,3},{3,2},{4,5},{5,4},{6,7},{7,6},{8,9},{9,8},{10,11... | collective-permute-start | bytes 2949128 | tf_op jit(solution)/shard_map/ppermute | solution.py:47
  22.6 21.7 %collective-permute-start.5 = (bf16[2,64,2560]{2,1,0:T(8,128)(2,1)S(1)}, bf16[2,64,2560]{2,1,0:T(8,128)(2,1)S(1)}, u32[]{:S(2)}, u32[]{:S(2)}) collective-permute-start(bf16[2,64,2560]{2,1,0:T(8,128)(2,1)S(1)} %pad_maximum_fusion.2), channel_id=1, source_target_pairs={{0,2},{2,0},{1,3},{3,1},{4,6},{6,4},{5,7},{7,5},{8,10},{10,8},{9,1... | collective-permute-start | bytes 1966088 | tf_op jit(solution)/shard_map/ppermute | solution.py:47
  23.2 21.1 %collective-permute-start.6 = (bf16[800,256]{1,0:T(8,128)(2,1)S(1)}, bf16[800,256]{1,0:T(8,128)(2,1)S(1)}, u32[]{:S(2)}, u32[]{:S(2)}) collective-permute-start(bf16[800,256]{1,0:T(8,128)(2,1)S(1)} %get-tuple-element.70), channel_id=1, source_target_pairs={{0,16},{8,24},{16,0},{24,8},{1,17},{9,25},{17,1},{25,9},{2,18},{10... | collective-permute-start | bytes 1228808 | tf_op jit(solution)/shard_map/ppermute | solution.py:47
  23.5 16.2 %collective-permute-start.4 = (bf16[64,2560]{1,0:T(8,128)(2,1)S(1)}, bf16[64,2560]{1,0:T(8,128)(2,1)S(1)}, u32[]{:S(2)}, u32[]{:S(2)}) collective-permute-start(bf16[64,2560]{1,0:T(8,128)(2,1)S(1)} %collective-permute-done.refs_3_), channel_id=1, source_target_pairs={{0,8},{8,0},{16,24},{24,16},{1,9},{9,1},{17,25},{25,17},{2,10},{10... | collective-permute-start | bytes 983048 | tf_op jit(solution)/shard_map/ppermute | solution.py:47
  44.4 25.0 %collective-permute-start.13 = (bf16[3,64,2560]{2,1,0:T(8,128)(2,1)S(1)}, bf16[3,64,2560]{2,1,0:T(8,128)(2,1)S(1)}, u32[]{:S(2)}, u32[]{:S(2)}) collective-permute-start(bf16[3,64,2560]{2,1,0:T(8,128)(2,1)S(1)} %pad_maximum_fusion.1), channel_id=1, source_target_pairs={{0,1},{1,0},{2,3},{3,2},{4,5},{5,4},{6,7},{7,6},{8,9},{9,8},{10,11... | collective-permute-start | bytes 2949128 | tf_op jit(solution)/shard_map/ppermute | solution.py:47
  44.5 24.9 %copy-start.4 = (bf16[64,2560]{1,0:T(8,128)(2,1)S(1)}, bf16[64,2560]{1,0:T(8,128)(2,1)}, u32[]{:S(2)}) copy-start(bf16[64,2560]{1,0:T(8,128)(2,1)} %refs_0_.1) | copy-start | bytes 983044
  44.5 20.6 %collective-permute-start.12 = (bf16[400,1024]{1,0:T(8,128)(2,1)S(1)}, bf16[400,1024]{1,0:T(8,128)(2,1)S(1)}, u32[]{:S(2)}, u32[]{:S(2)}) collective-permute-start(bf16[400,1024]{1,0:T(8,128)(2,1)S(1)} %get-tuple-element.80.own_b), channel_id=1, source_target_pairs={{0,4},{4,0},{1,5},{5,1},{2,6},{6,2},{3,7},{7,3},{8,12},{12,8},{9,1... | collective-permute-start | bytes 2457608 | tf_op jit(solution)/shard_map/ppermute | solution.py:47
  46.1 19.1 %collective-permute-start.10 = (bf16[800,256]{1,0:T(8,128)(2,1)S(1)}, bf16[800,256]{1,0:T(8,128)(2,1)S(1)}, u32[]{:S(2)}, u32[]{:S(2)}) collective-permute-start(bf16[800,256]{1,0:T(8,128)(2,1)S(1)} %get-tuple-element.78), channel_id=1, source_target_pairs={{0,24},{8,16},{16,8},{24,0},{1,25},{9,17},{17,9},{25,1},{2,26},{10... | collective-permute-start | bytes 1228808 | tf_op jit(solution)/shard_map/ppermute | solution.py:47
  47.4 20.0 %collective-permute-start.11 = (bf16[800,256]{1,0:T(8,128)(2,1)S(1)}, bf16[800,256]{1,0:T(8,128)(2,1)S(1)}, u32[]{:S(2)}, u32[]{:S(2)}) collective-permute-start(bf16[800,256]{1,0:T(8,128)(2,1)S(1)} %get-tuple-element.79), channel_id=1, source_target_pairs={{0,8},{8,0},{16,24},{24,16},{1,9},{9,1},{17,25},{25,17},{2,10},{10... | collective-permute-start | bytes 1228808 | tf_op jit(solution)/shard_map/ppermute | solution.py:47
  47.4 17.7 %collective-permute-start.9 = (bf16[64,2560]{1,0:T(8,128)(2,1)S(1)}, bf16[64,2560]{1,0:T(8,128)(2,1)S(1)}, u32[]{:S(2)}, u32[]{:S(2)}) collective-permute-start(bf16[64,2560]{1,0:T(8,128)(2,1)S(1)} %collective-permute-done.4.refs_1_), channel_id=1, source_target_pairs={{0,2},{2,0},{1,3},{3,1},{4,6},{6,4},{5,7},{7,5},{8,10},{10,8},{9,1... | collective-permute-start | bytes 983048 | tf_op jit(solution)/shard_map/ppermute | solution.py:47
  67.4 7.1 %collective-permute-start.14 = (bf16[64,2560]{1,0:T(8,128)(2,1)S(1)}, bf16[64,2560]{1,0:T(8,128)(2,1)S(1)}, u32[]{:S(2)}, u32[]{:S(2)}) collective-permute-start(bf16[64,2560]{1,0:T(8,128)(2,1)S(1)} %collective-permute-done.9.refs_2_), channel_id=1, source_target_pairs={{0,1},{1,0},{2,3},{3,2},{4,5},{5,4},{6,7},{7,6},{8,9},{9,8},{10,11... | collective-permute-start | bytes 983048 | tf_op jit(solution)/shard_map/ppermute | solution.py:47
  75.2 8.1 %collective-permute-start.15 = (bf16[512,2560]{1,0:T(8,128)(2,1)S(1)}, bf16[512,2560]{1,0:T(8,128)(2,1)S(1)}, u32[]{:S(2)}, u32[]{:S(2)}) collective-permute-start(bf16[512,2560]{1,0:T(8,128)(2,1)S(1)} %convolution_convert_fusion.1), channel_id=1, source_target_pairs={{0,1},{1,0},{2,3},{3,2},{4,5},{5,4},{6,7},{7,6},{8,9},{9,8},{10,11... | collective-permute-start | bytes 7864328 | tf_op jit(solution)/shard_map/ppermute | solution.py:47
  75.8 27.8 %collective-permute-start.17 = (bf16[800,256]{1,0:T(8,128)(2,1)S(1)}, bf16[800,256]{1,0:T(8,128)(2,1)S(1)}, u32[]{:S(2)}, u32[]{:S(2)}) collective-permute-start(bf16[800,256]{1,0:T(8,128)(2,1)S(1)} %fusion.21), channel_id=1, source_target_pairs={{0,16},{8,24},{16,0},{24,8},{1,17},{9,25},{17,1},{25,9},{2,18},{10... | collective-permute-start | bytes 1228808 | tf_op jit(solution)/shard_map/ppermute | solution.py:47
  79.6 49.6 %collective-permute-start.23 = (bf16[400,2560]{1,0:T(8,128)(2,1)S(1)}, bf16[400,2560]{1,0:T(8,128)(2,1)S(1)}, u32[]{:S(2)}, u32[]{:S(2)}) collective-permute-start(bf16[400,2560]{1,0:T(8,128)(2,1)S(1)} %fusion.2), channel_id=1, source_target_pairs={{0,4},{4,0},{1,5},{5,1},{2,6},{6,2},{3,7},{7,3},{8,12},{12,8},{9,1... | collective-permute-start | bytes 6144008 | tf_op jit(solution)/shard_map/ppermute | solution.py:47
  84.5 16.2 %collective-permute-start.16 = (bf16[2,64,2560]{2,1,0:T(8,128)(2,1)S(1)}, bf16[2,64,2560]{2,1,0:T(8,128)(2,1)S(1)}, u32[]{:S(2)}, u32[]{:S(2)}) collective-permute-start(bf16[2,64,2560]{2,1,0:T(8,128)(2,1)S(1)} %get-tuple-element.123), channel_id=1, source_target_pairs={{0,2},{2,0},{1,3},{3,1},{4,6},{6,4},{5,7},{7,5},{8,10},{10,8},{9,1... | collective-permute-start | bytes 1966088 | tf_op jit(solution)/shard_map/ppermute | solution.py:47
  87.3 27.1 %collective-permute-start.20 = (bf16[800,256]{1,0:T(8,128)(2,1)S(1)}, bf16[800,256]{1,0:T(8,128)(2,1)S(1)}, u32[]{:S(2)}, u32[]{:S(2)}) collective-permute-start(bf16[800,256]{1,0:T(8,128)(2,1)S(1)} %fusion.15), channel_id=1, source_target_pairs={{0,8},{8,0},{16,24},{24,16},{1,9},{9,1},{17,25},{25,17},{2,10},{10... | collective-permute-start | bytes 1228808 | tf_op jit(solution)/shard_map/ppermute | solution.py:47
  90.0 24.4 %collective-permute-start.21 = (bf16[800,256]{1,0:T(8,128)(2,1)S(1)}, bf16[800,256]{1,0:T(8,128)(2,1)S(1)}, u32[]{:S(2)}, u32[]{:S(2)}) collective-permute-start(bf16[800,256]{1,0:T(8,128)(2,1)S(1)} %fusion.18), channel_id=1, source_target_pairs={{0,24},{8,16},{16,8},{24,0},{1,25},{9,17},{17,9},{25,1},{2,26},{10... | collective-permute-start | bytes 1228808 | tf_op jit(solution)/shard_map/ppermute | solution.py:47
  100.7 20.8 %collective-permute-start.19 = (bf16[2,64,2560]{2,1,0:T(8,128)(2,1)S(1)}, bf16[2,64,2560]{2,1,0:T(8,128)(2,1)S(1)}, u32[]{:S(2)}, u32[]{:S(2)}) collective-permute-start(bf16[2,64,2560]{2,1,0:T(8,128)(2,1)S(1)} %get-tuple-element.122), channel_id=1, source_target_pairs={{0,2},{2,0},{1,3},{3,1},{4,6},{6,4},{5,7},{7,5},{8,10},{10,8},{9,1... | collective-permute-start | bytes 1966088 | tf_op jit(solution)/shard_map/ppermute | solution.py:47
  103.6 24.7 %collective-permute-start.18 = (bf16[2,64,2560]{2,1,0:T(8,128)(2,1)S(1)}, bf16[2,64,2560]{2,1,0:T(8,128)(2,1)S(1)}, u32[]{:S(2)}, u32[]{:S(2)}) collective-permute-start(bf16[2,64,2560]{2,1,0:T(8,128)(2,1)S(1)} %fusion.5), channel_id=1, source_target_pairs={{0,8},{8,0},{16,24},{24,16},{1,9},{9,1},{17,25},{25,17},{2,10},{10... | collective-permute-start | bytes 1966088 | tf_op jit(solution)/shard_map/ppermute | solution.py:47
  105.1 9.3 %copy-start.2 = (bf16[256,3200]{1,0:T(8,128)(2,1)S(1)}, bf16[256,3200]{1,0:T(8,128)(2,1)}, u32[]{:S(2)}) copy-start(bf16[256,3200]{1,0:T(8,128)(2,1)} %up.3) | copy-start | bytes 4915204
  128.7 17.4 %collective-permute-start.22 = (bf16[64,2560]{1,0:T(8,128)(2,1)S(1)}, bf16[64,2560]{1,0:T(8,128)(2,1)S(1)}, u32[]{:S(2)}, u32[]{:S(2)}) collective-permute-start(bf16[64,2560]{1,0:T(8,128)(2,1)S(1)} %fusion.28), channel_id=1, source_target_pairs={{0,16},{8,24},{16,0},{24,8},{1,17},{9,25},{17,1},{25,9},{2,18},{10... | collective-permute-start | bytes 983048 | tf_op jit(solution)/shard_map/ppermute | solution.py:47

commit v4 on v2

--- a/solution.py
+++ b/solution.py
@@ -140,8 +140,8 @@
             rest[lane // 2 * 2 + first + r][:, lanes] = piece[r * half : (r + 1) * half, :]
 
 
-def grads_kernel(nz, units, place, gate, up, *refs):
-    pieces, (gate_grad, up_grad, columns, natural) = refs[:nz], refs[nz:]
+def grads_kernel(parts, units, place, gate, up, *refs):
+    pieces, (gate_grad, up_grad, columns, natural) = refs[: len(parts)], refs[len(parts) :]
     step = pl.program_id(0)
     group, span = gate.shape
     rows = group // 4
@@ -149,10 +149,10 @@
     @pl.when(step == 0)
     def _():
         half = units // 2
-        for k in range(nz):
-            for r in range(2):
-                start = (place[0] ^ k) * units + (place[1] ^ r) * half
-                columns[pl.ds(pl.multiple_of(start, 16), half), :] = pieces[k][
+        for piece, (k, first, count) in zip(pieces, parts):
+            for r in range(count):
+                start = (place[0] ^ k) * units + (place[1] ^ (first + r)) * half
+                columns[pl.ds(pl.multiple_of(start, 16), half), :] = piece[
                     r * half : (r + 1) * half, :
                 ]
 
@@ -251,6 +251,7 @@
             whole((half_tokens, width)), (1,), [], (0, 4 * half_tokens * width, 0),
         )
 
+    send, last_c = barrier((send, last_c))
     even = gather_tokens(
         (cotangent, own_y, own_c, far, other_y, first_c, other_c),
         ((0, 0), (1, 0), (2, 0), (5, 0), (3, 0), (4, 0), (5, 1), (6, 0)),
@@ -266,42 +267,47 @@
         first, second = by_units[r][low:high], by_units[2 + r][low:high]
         return (matmul(first, flat[0]) + matmul(second, flat[1])) * factor
 
-    def back_of(k):
+    def back_of(k, low=0, high=units):
         rows_of_k = flat[k % 2][k // 2 * group_rows : (k // 2 + 1) * group_rows]
-        return matmul(weight, rows_of_k, 1, 1, bf16)
-
-    over_c = exchange(matmul(send, weight, dtype=bf16), "c", 1)
+        return matmul(weight[low:high], rows_of_k, 1, 1, bf16)
+
+    given = matmul(send, weight, dtype=bf16)
+    given, even = barrier((given, even))
+    flat = [even, odd]
+    far_back = back_of(2)
+    far_back, flat = barrier((far_back, flat))
+    over_c = exchange(given, "c", 1)
+    theirs = grad_half(1).astype(bf16)
+    theirs, keep, flat = barrier((theirs, keep, flat))
+    over_x = exchange(theirs, "x", 1)
     kept = matmul(keep, weight, dtype=bf16)
-    kept, flat = barrier((kept, [even, odd]))
-    far_back = back_of(2)
-    kept, far_back = barrier((kept, far_back))
     sums = (kept.astype(f32) + over_c.astype(f32)).reshape(2, nz, rows, width)
     sums, flat = barrier((sums, flat))
     odd_y = exchange(sums[1, :2].astype(bf16), "y", 1)
     even_y = exchange(sums[1, 2:].astype(bf16), "y", 1)
-    over_x = exchange(grad_half(1).astype(bf16), "x", 1)
+    far_back = exchange(far_back, "z", 2)
     near_back = exchange(back_of(1), "z", 1)
+    last_back, far_back = barrier((back_of(3, 0, owned), far_back))
+    last_back = exchange(last_back, "z", 3)
     odd_y, flat = barrier((odd_y, flat))
-    back = [back_of(0), near_back, exchange(far_back, "z", 2), exchange(back_of(3), "z", 3)]
     odd_sum = (sums[0, :2] + odd_y.astype(f32)).astype(bf16)
-    odd_sum, back[2] = barrier((odd_sum, back[2]))
+    odd_sum, far_back, last_back = barrier((odd_sum, far_back, last_back))
     near_sum, even_y = barrier((exchange(odd_sum, "z", 1), even_y))
+    back = [back_of(0), near_back, far_back, last_back, exchange(back_of(3, owned, units), "z", 3)]
     near_sum = near_sum.astype(f32)
     even_sum = sums[0, 2:] + even_y.astype(f32)
     ours, across = even_sum[0] + near_sum[0], (even_sum[1] + near_sum[1]).astype(bf16)
-    across, back[3] = barrier((across, back[3]))
     far_sum = exchange(across, "z", 2)
-
     back, flat, _ = barrier((back, flat, across))
-    own_grad = grad_half(0)
+    back_parts = tuple((k, 0, 2) for k in range(3)) + ((3, 0, 1), (3, 1, 1))
     gate_grad, up_grad = call_kernel(
-        functools.partial(grads_kernel, nz, units), place, (gate_pre, up_pre, *back),
-        [wide] * 2 + [whole((units, group_rows))] * nz,
+        functools.partial(grads_kernel, back_parts, units), place, (gate_pre, up_pre, *back),
+        [wide] * 2 + [whole(value.shape) for value in back],
         [struct((group_rows, local_hidden), bf16)] * 2, [wide] * 2, (steps,), act_scratch[::-1],
         (12 * act_bytes, 5 * act_bytes, act_bytes // 2),
     )
     over_x, _ = barrier((over_x, gate_grad))
-    weight_grad = own_grad + over_x.astype(f32)
+    weight_grad = grad_half(0) + over_x.astype(f32)
     far_sum, weight_grad = barrier((far_sum, weight_grad))
     layer_out = (ours + far_sum.astype(f32)).astype(bf16)
     return layer_out, gate_grad, up_grad, weight_grad

time: 142 us -> 148 us (1.042)
  waiting for transfers between devices: 76.1 us -> 78.9 us
  starting transfers between devices: 27.3 us -> 28.9 us
    ppermute x24 -> x25, waiting for transfers between devices: 76.1 us -> 78.9 us  [exchange(): return lax.ppermute(value, axis, [(i, i ^ offset) for i in range(size)])]
    ppermute x24 -> x25, starting transfers between devices: 27.3 us -> 28.9 us  [exchange(): return lax.ppermute(value, axis, [(i, i ^ offset) for i in range(size)])]
    dot_general x10 -> x11, matrix products: 18.1 us -> 19.3 us  [matmul(): lax.dot_general(lhs, rhs, dims, preferred_element_type=jnp.float32)]
  transfers between devices with their start and end apart: 24 -> 25, of which waited for: 14 -> 13; matrix products, arithmetic and copies ran while one was open for 13% -> 15% of each run, Pallas kernels for 8% -> 8%
where the time goes in v4:
time: 148 us
  waiting for transfers between devices  78.9 us (53%)
  starting transfers between devices  28.9 us (20%)
  matrix products  19.3 us (13%)
  Pallas kernels  13 us (9%)
  local copies, waits for them, and re-layouts  4 us (3%)
  other arithmetic  2.69 us (2%)
    ppermute x25, waiting for transfers between devices, exchange(): return lax.ppermute(value, axis, [(i, i ^ offset) for i in range(size)])  78.9 us
    ppermute x25, starting transfers between devices, exchange(): return lax.ppermute(value, axis, [(i, i ^ offset) for i in range(size)])  28.9 us
    dot_general x11, matrix products, matmul(): lax.dot_general(lhs, rhs, dims, preferred_element_type=jnp.float32)  19.3 us
    pallas_call x7, Pallas kernels, call_kernel(): pl.pallas_call(kernel, out_shape=out_shapes, grid_spec=pltpu.PrefetchScal...  13 us
    unnamed x11, local copies, waits for them, and re-layouts  3.91 us
  transfers between devices with their start and end apart: 25, of which 13 were waited for; matrix products, arithmetic and copies ran while one was open for 15% of the time, Pallas kernels for 8%

profile of v4, /device:TPU:0, one launch (start us, length us, event | category | flops | bytes accessed | tf_op | source)
XLA Modules:
  0.0 147.6 jit_solution(10591693434696346298)
XLA Ops:
  0.6 3.0 %collective-permute-start.2 = (bf16[64,2560]{1,0:T(8,128)(2,1)}, bf16[64,2560]{1,0:T(8,128)(2,1)S(1)}, u32[]{:S(2)}, u32[]{:S(2)}) collective-permute-start(bf16[64,2560]{1,0:T(8,128)(2,1)} %refs_0_.1), channel_id=1, source_target_pairs={{0,2},{2,0},{1,3},{3,1},{4,6},{6,4},{5,7},{7,5},{8,10},{10,8},{9,1... | collective-permute-start | bytes 983048 | tf_op jit(solution)/shard_map/ppermute | solution.py:47
  3.7 1.6 %collective-permute-start.1 = (bf16[64,2560]{1,0:T(8,128)(2,1)}, bf16[64,2560]{1,0:T(8,128)(2,1)S(1)}, u32[]{:S(2)}, u32[]{:S(2)}) collective-permute-start(bf16[64,2560]{1,0:T(8,128)(2,1)} %refs_0_.1), channel_id=1, source_target_pairs={{0,8},{8,0},{16,24},{24,16},{1,9},{9,1},{17,25},{25,17},{2,10},{10... | collective-permute-start | bytes 983048 | tf_op jit(solution)/shard_map/ppermute | solution.py:47
  5.2 2.6 %collective-permute-start = (bf16[64,2560]{1,0:T(8,128)(2,1)}, bf16[64,2560]{1,0:T(8,128)(2,1)S(1)}, u32[]{:S(2)}, u32[]{:S(2)}) collective-permute-start(bf16[64,2560]{1,0:T(8,128)(2,1)} %refs_0_.1), channel_id=1, source_target_pairs={{0,16},{8,24},{16,0},{24,8},{1,17},{9,25},{17,1},{25,9},{2,18},{10... | collective-permute-start | bytes 983048 | tf_op jit(solution)/shard_map/ppermute | solution.py:47
  7.8 0.9 copy.9.scales
  8.8 1.6 %copy-done.3 = bf16[400,2560]{1,0:T(8,128)(2,1)S(1)} copy-done((bf16[400,2560]{1,0:T(8,128)(2,1)S(1)}, bf16[400,2560]{1,0:T(8,128)(2,1)}, u32[]{:S(2)}) %copy-start.3) | copy-done | bytes 2048024
  10.4 1.1 shard_map.85
  11.5 1.6 %collective-permute-start.7 = (bf16[400,1536]{1,0:T(8,128)(2,1)S(1)}, bf16[400,1536]{1,0:T(8,128)(2,1)S(1)}, u32[]{:S(2)}, u32[]{:S(2)}) collective-permute-start(bf16[400,1536]{1,0:T(8,128)(2,1)S(1)} %get-tuple-element.82.own_a), channel_id=1, source_target_pairs={{0,4},{4,0},{1,5},{5,1},{2,6},{6,2},{3,7},{7,3},{8,12},{12,8},{9,1... | collective-permute-start | bytes 3686408 | tf_op jit(solution)/shard_map/ppermute | solution.py:47
  13.1 1.4 copy-done.1
  14.5 2.8 %shard_map.84 = (bf16[800,256]{1,0:T(8,128)(2,1)S(1)}, bf16[800,256]{1,0:T(8,128)(2,1)S(1)}, bf16[800,256]{1,0:T(8,128)(2,1)S(1)}, bf16[800,256]{1,0:T(8,128)(2,1)S(1)}) custom-call(s32[4]{0:T(128)S(1)} %pad_add_fusion.place, bf16[256,3200]{1,0:T(8,128)(2,1)S(1)} %copy-done, bf16[256,3200]{1,0:T(8,128)(2,1)S(1)} %copy-done.1), custom_call_target="tpu_custom_call" | custom-call | flops 6553600 | bytes 4915200 | tf_op jit(solution)/shard_map/pallas_call | solution.py:52
  17.4 2.5 %collective-permute-done.1.refs_0_ = bf16[64,2560]{1,0:T(8,128)(2,1)S(1)} collective-permute-done((bf16[64,2560]{1,0:T(8,128)(2,1)}, bf16[64,2560]{1,0:T(8,128)(2,1)S(1)}, u32[]{:S(2)}, u32[]{:S(2)}) %collective-permute-start.1) | collective-permute-done | bytes 327712 | tf_op jit(solution)/shard_map/ppermute | solution.py:47
  19.9 2.4 %collective-permute-done.refs_3_ = bf16[64,2560]{1,0:T(8,128)(2,1)S(1)} collective-permute-done((bf16[64,2560]{1,0:T(8,128)(2,1)}, bf16[64,2560]{1,0:T(8,128)(2,1)S(1)}, u32[]{:S(2)}, u32[]{:S(2)}) %collective-permute-start) | collective-permute-done | bytes 327712 | tf_op jit(solution)/shard_map/ppermute | solution.py:47
  23.6 2.7 %collective-permute-start.6 = (bf16[800,256]{1,0:T(8,128)(2,1)S(1)}, bf16[800,256]{1,0:T(8,128)(2,1)S(1)}, u32[]{:S(2)}, u32[]{:S(2)}) collective-permute-start(bf16[800,256]{1,0:T(8,128)(2,1)S(1)} %get-tuple-element.81), channel_id=1, source_target_pairs={{0,16},{8,24},{16,0},{24,8},{1,17},{9,25},{17,1},{25,9},{2,18},{10... | collective-permute-start | bytes 1228808 | tf_op jit(solution)/shard_map/ppermute | solution.py:47
  26.3 6.1 %collective-permute-done.4.refs_1_ = bf16[64,2560]{1,0:T(8,128)(2,1)S(1)} collective-permute-done((bf16[64,2560]{1,0:T(8,128)(2,1)S(1)}, bf16[64,2560]{1,0:T(8,128)(2,1)S(1)}, u32[]{:S(2)}, u32[]{:S(2)}) %collective-permute-start.4) | collective-permute-done | bytes 327712 | tf_op jit(solution)/shard_map/ppermute | solution.py:47
  32.4 1.5 %collective-permute-start.12 = (bf16[400,1024]{1,0:T(8,128)(2,1)S(1)}, bf16[400,1024]{1,0:T(8,128)(2,1)S(1)}, u32[]{:S(2)}, u32[]{:S(2)}) collective-permute-start(bf16[400,1024]{1,0:T(8,128)(2,1)S(1)} %get-tuple-element.91.own_b), channel_id=1, source_target_pairs={{0,4},{4,0},{1,5},{5,1},{2,6},{6,2},{3,7},{7,3},{8,12},{12,8},{9,1... | collective-permute-start | bytes 2457608 | tf_op jit(solution)/shard_map/ppermute | solution.py:47
  33.9 11.0 %collective-permute-done.6.refs_1_ = bf16[800,256]{1,0:T(8,128)(2,1)S(1)} collective-permute-done((bf16[800,256]{1,0:T(8,128)(2,1)S(1)}, bf16[800,256]{1,0:T(8,128)(2,1)S(1)}, u32[]{:S(2)}, u32[]{:S(2)}) %collective-permute-start.6) | collective-permute-done | bytes 409632 | tf_op jit(solution)/shard_map/ppermute | solution.py:47
  45.0 2.1 %collective-permute-start.10 = (bf16[800,256]{1,0:T(8,128)(2,1)S(1)}, bf16[800,256]{1,0:T(8,128)(2,1)S(1)}, u32[]{:S(2)}, u32[]{:S(2)}) collective-permute-start(bf16[800,256]{1,0:T(8,128)(2,1)S(1)} %get-tuple-element.89), channel_id=1, source_target_pairs={{0,24},{8,16},{16,8},{24,0},{1,25},{9,17},{17,9},{25,1},{2,26},{10... | collective-permute-start | bytes 1228808 | tf_op jit(solution)/shard_map/ppermute | solution.py:47
  47.1 1.5 %collective-permute-start.9 = (bf16[64,2560]{1,0:T(8,128)(2,1)S(1)}, bf16[64,2560]{1,0:T(8,128)(2,1)S(1)}, u32[]{:S(2)}, u32[]{:S(2)}) collective-permute-start(bf16[64,2560]{1,0:T(8,128)(2,1)S(1)} %collective-permute-done.4.refs_1_), channel_id=1, source_target_pairs={{0,2},{2,0},{1,3},{3,1},{4,6},{6,4},{5,7},{7,5},{8,10},{10,8},{9,1... | collective-permute-start | bytes 983048 | tf_op jit(solution)/shard_map/ppermute | solution.py:47
  48.8 9.8 %collective-permute-done.12.other_b = bf16[400,1024]{1,0:T(8,128)(2,1)S(1)} collective-permute-done((bf16[400,1024]{1,0:T(8,128)(2,1)S(1)}, bf16[400,1024]{1,0:T(8,128)(2,1)S(1)}, u32[]{:S(2)}, u32[]{:S(2)}) %collective-permute-start.12) | collective-permute-done | bytes 819232 | tf_op jit(solution)/shard_map/ppermute | solution.py:47
  59.2 7.1 %collective-permute-done.11.refs_3_ = bf16[800,256]{1,0:T(8,128)(2,1)S(1)} collective-permute-done((bf16[800,256]{1,0:T(8,128)(2,1)S(1)}, bf16[800,256]{1,0:T(8,128)(2,1)S(1)}, u32[]{:S(2)}, u32[]{:S(2)}) %collective-permute-start.11) | collective-permute-done | bytes 409632 | tf_op jit(solution)/shard_map/ppermute | solution.py:47
  66.4 0.8 shard_map.87
  67.2 1.1 shard_map.86
  68.3 4.2 %convolution_convert_fusion.1 = bf16[512,2560]{1,0:T(8,128)(2,1)} fusion(bf16[512,800]{1,0:T(8,128)(2,1)S(1)} %get-tuple-element.101, bf16[800,2560]{1,0:T(8,128)(2,1)S(1)} %shard_map.87), kind=kOutput, calls=%fused_computation.7 | convolution fusion | flops 2098462720 | bytes 7536640 | tf_op jit(solution)/shard_map/dot_general | solution.py:174
  72.5 0.7 shard_map.88
  74.5 1.3 fusion.17
  75.8 0.7 collective-permute-start.17
  76.5 1.2 fusion.41
  77.7 1.2 fusion.3
  79.0 1.6 %collective-permute-start.24 = (bf16[400,2560]{1,0:T(8,128)(2,1)S(1)}, bf16[400,2560]{1,0:T(8,128)(2,1)S(1)}, u32[]{:S(2)}, u32[]{:S(2)}) collective-permute-start(bf16[400,2560]{1,0:T(8,128)(2,1)S(1)} %fusion.3), channel_id=1, source_target_pairs={{0,4},{4,0},{1,5},{5,1},{2,6},{6,2},{3,7},{7,3},{8,12},{12,8},{9,1... | collective-permute-start | bytes 6144008 | tf_op jit(solution)/shard_map/ppermute | solution.py:47
  80.5 3.1 %convolution_convert_fusion = bf16[512,2560]{1,0:T(8,128)(2,1)S(1)} fusion(bf16[512,800]{1,0:T(8,128)(2,1)S(1)} %get-tuple-element.111, bf16[800,2560]{1,0:T(8,128)(2,1)S(1)} %shard_map.87), kind=kOutput, calls=%fused_computation.6 | convolution fusion | flops 2098462720 | bytes 7536640 | tf_op jit(solution)/shard_map/dot_general | solution.py:174
  83.6 0.7 convert_add_fusion
  84.8 1.6 %collective-permute-start.16 = (bf16[2,64,2560]{2,1,0:T(8,128)(2,1)S(1)}, bf16[2,64,2560]{2,1,0:T(8,128)(2,1)S(1)}, u32[]{:S(2)}, u32[]{:S(2)}) collective-permute-start(bf16[2,64,2560]{2,1,0:T(8,128)(2,1)S(1)} %get-tuple-element.145), channel_id=1, source_target_pairs={{0,2},{2,0},{1,3},{3,1},{4,6},{6,4},{5,7},{7,5},{8,10},{10,8},{9,1... | collective-permute-start | bytes 1966088 | tf_op jit(solution)/shard_map/ppermute | solution.py:47
  86.4 0.7 fusion.26
  87.1 9.6 %collective-permute-done.17.refs_2_ = bf16[800,256]{1,0:T(8,128)(2,1)S(1)} collective-permute-done((bf16[800,256]{1,0:T(8,128)(2,1)S(1)}, bf16[800,256]{1,0:T(8,128)(2,1)S(1)}, u32[]{:S(2)}, u32[]{:S(2)}) %collective-permute-start.17) | collective-permute-done | bytes 409632 | tf_op jit(solution)/shard_map/ppermute | solution.py:47
  96.7 1.8 %collective-permute-start.18 = (bf16[400,256]{1,0:T(8,128)(2,1)S(1)}, bf16[400,256]{1,0:T(8,128)(2,1)S(1)}, u32[]{:S(2)}, u32[]{:S(2)}) collective-permute-start(bf16[400,256]{1,0:T(8,128)(2,1)S(1)} %fusion.26), channel_id=1, source_target_pairs={{0,24},{8,16},{16,8},{24,0},{1,25},{9,17},{17,9},{25,1},{2,26},{10... | collective-permute-start | bytes 614408 | tf_op jit(solution)/shard_map/ppermute | solution.py:47
  98.5 1.2 fusion.23
  99.8 1.6 %collective-permute-start.20 = (bf16[2,64,2560]{2,1,0:T(8,128)(2,1)S(1)}, bf16[2,64,2560]{2,1,0:T(8,128)(2,1)S(1)}, u32[]{:S(2)}, u32[]{:S(2)}) collective-permute-start(bf16[2,64,2560]{2,1,0:T(8,128)(2,1)S(1)} %get-tuple-element.144), channel_id=1, source_target_pairs={{0,2},{2,0},{1,3},{3,1},{4,6},{6,4},{5,7},{7,5},{8,10},{10,8},{9,1... | collective-permute-start | bytes 1966088 | tf_op jit(solution)/shard_map/ppermute | solution.py:47
  101.5 4.9 %collective-permute-done.18.refs_3_ = bf16[400,256]{1,0:T(8,128)(2,1)S(1)} collective-permute-done((bf16[400,256]{1,0:T(8,128)(2,1)S(1)}, bf16[400,256]{1,0:T(8,128)(2,1)S(1)}, u32[]{:S(2)}, u32[]{:S(2)}) %collective-permute-start.18) | collective-permute-done | bytes 204832 | tf_op jit(solution)/shard_map/ppermute | solution.py:47
  107.0 0.7 fusion.31
  107.8 2.1 %collective-permute-start.23 = (bf16[400,256]{1,0:T(8,128)(2,1)S(1)}, bf16[400,256]{1,0:T(8,128)(2,1)S(1)}, u32[]{:S(2)}, u32[]{:S(2)}) collective-permute-start(bf16[400,256]{1,0:T(8,128)(2,1)S(1)} %fusion.31), channel_id=1, source_target_pairs={{0,24},{8,16},{16,8},{24,0},{1,25},{9,17},{17,9},{25,1},{2,26},{10... | collective-permute-start | bytes 614408 | tf_op jit(solution)/shard_map/ppermute | solution.py:47
  109.9 1.2 fusion.20.refs_0_
  111.1 5.1 %collective-permute-done.20 = bf16[2,64,2560]{2,1,0:T(8,128)(2,1)S(1)} collective-permute-done((bf16[2,64,2560]{2,1,0:T(8,128)(2,1)S(1)}, bf16[2,64,2560]{2,1,0:T(8,128)(2,1)S(1)}, u32[]{:S(2)}, u32[]{:S(2)}) %collective-permute-start.20) | collective-permute-done | bytes 655392 | tf_op jit(solution)/shard_map/ppermute | solution.py:47
  116.2 13.1 %collective-permute-done.19 = bf16[2,64,2560]{2,1,0:T(8,128)(2,1)S(1)} collective-permute-done((bf16[2,64,2560]{2,1,0:T(8,128)(2,1)S(1)}, bf16[2,64,2560]{2,1,0:T(8,128)(2,1)S(1)}, u32[]{:S(2)}, u32[]{:S(2)}) %collective-permute-start.19) | collective-permute-done | bytes 655392 | tf_op jit(solution)/shard_map/ppermute | solution.py:47
  130.3 2.8 %collective-permute-done.23.refs_4_ = bf16[400,256]{1,0:T(8,128)(2,1)S(1)} collective-permute-done((bf16[400,256]{1,0:T(8,128)(2,1)S(1)}, bf16[400,256]{1,0:T(8,128)(2,1)S(1)}, u32[]{:S(2)}, u32[]{:S(2)}) %collective-permute-start.23) | collective-permute-done | bytes 204832 | tf_op jit(solution)/shard_map/ppermute | solution.py:47
  133.0 5.6 %shard_map.90 = (bf16[256,3200]{1,0:T(8,128)(2,1)}, bf16[256,3200]{1,0:T(8,128)(2,1)}) custom-call(s32[4]{0:T(128)S(1)} %pad_add_fusion.place, bf16[256,3200]{1,0:T(8,128)(2,1)S(1)} %copy-done, bf16[256,3200]{1,0:T(8,128)(2,1)S(1)} %copy-done.2, bf16[800,256]{1,0:T(8,128)(2,1)S(1)} %fusion.20.refs_0_, bf16[800,256]{1,0:T(8,128)(2,1)S(1)} %collective-permute-done.22.refs_1_, ...), custom_call_target="tpu_custom_call" | custom-call | flops 19660800 | bytes 8192000 | tf_op jit(solution)/shard_map/pallas_call | solution.py:52
  138.7 1.2 fusion.42
  139.9 3.2 %fusion.2 = f32[400,2560]{1,0:T(8,128)} fusion(f32[400,2560]{1,0:T(8,128)S(1)} %fusion.42, bf16[400,512]{1,0:T(8,128)(2,1)S(1)} %get-tuple-element.125, bf16[512,2560]{1,0:T(8,128)(2,1)S(1)} %shard_map.88, bf16[400,2560]{1,0:T(8,128)(2,1)S(1)} %collective-permute-done.24), kind=kOutput, calls=%fused_computation.5 | convolution fusion | flops 1052672000 | bytes 13271040 | tf_op jit(solution)/shard_map/dot_general | solution.py:174
  143.2 3.6 %collective-permute-done.21 = bf16[64,2560]{1,0:T(8,128)(2,1)S(1)} collective-permute-done((bf16[64,2560]{1,0:T(8,128)(2,1)S(1)}, bf16[64,2560]{1,0:T(8,128)(2,1)S(1)}, u32[]{:S(2)}, u32[]{:S(2)}) %collective-permute-start.21) | collective-permute-done | bytes 327712 | tf_op jit(solution)/shard_map/ppermute | solution.py:47
  146.8 0.8 fusion.39
  (43 shorter events, 5.5 us)
Async XLA Ops:
  0.6 12.5 %copy-start = (bf16[256,3200]{1,0:T(8,128)(2,1)S(1)}, bf16[256,3200]{1,0:T(8,128)(2,1)}, u32[]{:S(2)}) copy-start(bf16[256,3200]{1,0:T(8,128)(2,1)} %gate.3) | copy-start | bytes 4915204
  0.6 16.8 %collective-permute-start.2 = (bf16[64,2560]{1,0:T(8,128)(2,1)}, bf16[64,2560]{1,0:T(8,128)(2,1)S(1)}, u32[]{:S(2)}, u32[]{:S(2)}) collective-permute-start(bf16[64,2560]{1,0:T(8,128)(2,1)} %refs_0_.1), channel_id=1, source_target_pairs={{0,2},{2,0},{1,3},{3,1},{4,6},{6,4},{5,7},{7,5},{8,10},{10,8},{9,1... | collective-permute-start | bytes 983048 | tf_op jit(solution)/shard_map/ppermute | solution.py:47
  3.7 16.3 %collective-permute-start.1 = (bf16[64,2560]{1,0:T(8,128)(2,1)}, bf16[64,2560]{1,0:T(8,128)(2,1)S(1)}, u32[]{:S(2)}, u32[]{:S(2)}) collective-permute-start(bf16[64,2560]{1,0:T(8,128)(2,1)} %refs_0_.1), channel_id=1, source_target_pairs={{0,8},{8,0},{16,24},{24,16},{1,9},{9,1},{17,25},{25,17},{2,10},{10... | collective-permute-start | bytes 983048 | tf_op jit(solution)/shard_map/ppermute | solution.py:47
  5.2 17.1 %collective-permute-start = (bf16[64,2560]{1,0:T(8,128)(2,1)}, bf16[64,2560]{1,0:T(8,128)(2,1)S(1)}, u32[]{:S(2)}, u32[]{:S(2)}) collective-permute-start(bf16[64,2560]{1,0:T(8,128)(2,1)} %refs_0_.1), channel_id=1, source_target_pairs={{0,16},{8,24},{16,0},{24,8},{1,17},{9,25},{17,1},{25,9},{2,18},{10... | collective-permute-start | bytes 983048 | tf_op jit(solution)/shard_map/ppermute | solution.py:47
  7.8 14.5 %collective-permute-start.3 = (bf16[64,2560]{1,0:T(8,128)(2,1)}, bf16[64,2560]{1,0:T(8,128)(2,1)S(1)}, u32[]{:S(2)}, u32[]{:S(2)}) collective-permute-start(bf16[64,2560]{1,0:T(8,128)(2,1)} %refs_0_.1), channel_id=1, source_target_pairs={{0,1},{1,0},{2,3},{3,2},{4,5},{5,4},{6,7},{7,6},{8,9},{9,8},{10,11... | collective-permute-start | bytes 983048 | tf_op jit(solution)/shard_map/ppermute | solution.py:47
  8.8 1.6 %copy-start.3 = (bf16[400,2560]{1,0:T(8,128)(2,1)S(1)}, bf16[400,2560]{1,0:T(8,128)(2,1)}, u32[]{:S(2)}) copy-start(bf16[400,2560]{1,0:T(8,128)(2,1)} %codes.1) | copy-start | bytes 6144004
  11.5 33.4 %collective-permute-start.7 = (bf16[400,1536]{1,0:T(8,128)(2,1)S(1)}, bf16[400,1536]{1,0:T(8,128)(2,1)S(1)}, u32[]{:S(2)}, u32[]{:S(2)}) collective-permute-start(bf16[400,1536]{1,0:T(8,128)(2,1)S(1)} %get-tuple-element.82.own_a), channel_id=1, source_target_pairs={{0,4},{4,0},{1,5},{5,1},{2,6},{6,2},{3,7},{7,3},{8,12},{12,8},{9,1... | collective-permute-start | bytes 3686408 | tf_op jit(solution)/shard_map/ppermute | solution.py:47
  13.1 1.4 copy-start.1
  22.3 10.1 %collective-permute-start.4 = (bf16[64,2560]{1,0:T(8,128)(2,1)S(1)}, bf16[64,2560]{1,0:T(8,128)(2,1)S(1)}, u32[]{:S(2)}, u32[]{:S(2)}) collective-permute-start(bf16[64,2560]{1,0:T(8,128)(2,1)S(1)} %collective-permute-done.refs_3_), channel_id=1, source_target_pairs={{0,8},{8,0},{16,24},{24,16},{1,9},{9,1},{17,25},{25,17},{2,10},{10... | collective-permute-start | bytes 983048 | tf_op jit(solution)/shard_map/ppermute | solution.py:47
  22.9 22.1 %collective-permute-start.8 = (bf16[3,64,2560]{2,1,0:T(8,128)(2,1)S(1)}, bf16[3,64,2560]{2,1,0:T(8,128)(2,1)S(1)}, u32[]{:S(2)}, u32[]{:S(2)}) collective-permute-start(bf16[3,64,2560]{2,1,0:T(8,128)(2,1)S(1)} %pad_maximum_fusion), channel_id=1, source_target_pairs={{0,1},{1,0},{2,3},{3,2},{4,5},{5,4},{6,7},{7,6},{8,9},{9,8},{10,11... | collective-permute-start | bytes 2949128 | tf_op jit(solution)/shard_map/ppermute | solution.py:47
  23.0 21.9 %collective-permute-start.5 = (bf16[2,64,2560]{2,1,0:T(8,128)(2,1)S(1)}, bf16[2,64,2560]{2,1,0:T(8,128)(2,1)S(1)}, u32[]{:S(2)}, u32[]{:S(2)}) collective-permute-start(bf16[2,64,2560]{2,1,0:T(8,128)(2,1)S(1)} %pad_maximum_fusion.2), channel_id=1, source_target_pairs={{0,2},{2,0},{1,3},{3,1},{4,6},{6,4},{5,7},{7,5},{8,10},{10,8},{9,1... | collective-permute-start | bytes 1966088 | tf_op jit(solution)/shard_map/ppermute | solution.py:47
  23.6 21.3 %collective-permute-start.6 = (bf16[800,256]{1,0:T(8,128)(2,1)S(1)}, bf16[800,256]{1,0:T(8,128)(2,1)S(1)}, u32[]{:S(2)}, u32[]{:S(2)}) collective-permute-start(bf16[800,256]{1,0:T(8,128)(2,1)S(1)} %get-tuple-element.81), channel_id=1, source_target_pairs={{0,16},{8,24},{16,0},{24,8},{1,17},{9,25},{17,1},{25,9},{2,18},{10... | collective-permute-start | bytes 1228808 | tf_op jit(solution)/shard_map/ppermute | solution.py:47
  32.4 26.2 %collective-permute-start.12 = (bf16[400,1024]{1,0:T(8,128)(2,1)S(1)}, bf16[400,1024]{1,0:T(8,128)(2,1)S(1)}, u32[]{:S(2)}, u32[]{:S(2)}) collective-permute-start(bf16[400,1024]{1,0:T(8,128)(2,1)S(1)} %get-tuple-element.91.own_b), channel_id=1, source_target_pairs={{0,4},{4,0},{1,5},{5,1},{2,6},{6,2},{3,7},{7,3},{8,12},{12,8},{9,1... | collective-permute-start | bytes 2457608 | tf_op jit(solution)/shard_map/ppermute | solution.py:47
  45.0 14.3 %collective-permute-start.10 = (bf16[800,256]{1,0:T(8,128)(2,1)S(1)}, bf16[800,256]{1,0:T(8,128)(2,1)S(1)}, u32[]{:S(2)}, u32[]{:S(2)}) collective-permute-start(bf16[800,256]{1,0:T(8,128)(2,1)S(1)} %get-tuple-element.89), channel_id=1, source_target_pairs={{0,24},{8,16},{16,8},{24,0},{1,25},{9,17},{17,9},{25,1},{2,26},{10... | collective-permute-start | bytes 1228808 | tf_op jit(solution)/shard_map/ppermute | solution.py:47
  47.1 19.3 %collective-permute-start.11 = (bf16[800,256]{1,0:T(8,128)(2,1)S(1)}, bf16[800,256]{1,0:T(8,128)(2,1)S(1)}, u32[]{:S(2)}, u32[]{:S(2)}) collective-permute-start(bf16[800,256]{1,0:T(8,128)(2,1)S(1)} %get-tuple-element.90), channel_id=1, source_target_pairs={{0,8},{8,0},{16,24},{24,16},{1,9},{9,1},{17,25},{25,17},{2,10},{10... | collective-permute-start | bytes 1228808 | tf_op jit(solution)/shard_map/ppermute | solution.py:47
  47.1 11.5 %collective-permute-start.9 = (bf16[64,2560]{1,0:T(8,128)(2,1)S(1)}, bf16[64,2560]{1,0:T(8,128)(2,1)S(1)}, u32[]{:S(2)}, u32[]{:S(2)}) collective-permute-start(bf16[64,2560]{1,0:T(8,128)(2,1)S(1)} %collective-permute-done.4.refs_1_), channel_id=1, source_target_pairs={{0,2},{2,0},{1,3},{3,1},{4,6},{6,4},{5,7},{7,5},{8,10},{10,8},{9,1... | collective-permute-start | bytes 983048 | tf_op jit(solution)/shard_map/ppermute | solution.py:47
  48.7 23.8 %collective-permute-start.14 = (bf16[3,64,2560]{2,1,0:T(8,128)(2,1)S(1)}, bf16[3,64,2560]{2,1,0:T(8,128)(2,1)S(1)}, u32[]{:S(2)}, u32[]{:S(2)}) collective-permute-start(bf16[3,64,2560]{2,1,0:T(8,128)(2,1)S(1)} %pad_maximum_fusion.1), channel_id=1, source_target_pairs={{0,1},{1,0},{2,3},{3,2},{4,5},{5,4},{6,7},{7,6},{8,9},{9,8},{10,11... | collective-permute-start | bytes 2949128 | tf_op jit(solution)/shard_map/ppermute | solution.py:47
  66.4 2.0 %collective-permute-start.13 = (bf16[64,2560]{1,0:T(8,128)(2,1)S(1)}, bf16[64,2560]{1,0:T(8,128)(2,1)S(1)}, u32[]{:S(2)}, u32[]{:S(2)}) collective-permute-start(bf16[64,2560]{1,0:T(8,128)(2,1)S(1)} %collective-permute-done.9.refs_2_), channel_id=1, source_target_pairs={{0,1},{1,0},{2,3},{3,2},{4,5},{5,4},{6,7},{7,6},{8,9},{9,8},{10,11... | collective-permute-start | bytes 983048 | tf_op jit(solution)/shard_map/ppermute | solution.py:47
  68.3 4.2 %copy-start.4 = (bf16[64,2560]{1,0:T(8,128)(2,1)S(1)}, bf16[64,2560]{1,0:T(8,128)(2,1)}, u32[]{:S(2)}) copy-start(bf16[64,2560]{1,0:T(8,128)(2,1)} %refs_0_.1) | copy-start | bytes 983044
  73.2 10.4 %collective-permute-start.15 = (bf16[512,2560]{1,0:T(8,128)(2,1)}, bf16[512,2560]{1,0:T(8,128)(2,1)S(1)}, u32[]{:S(2)}, u32[]{:S(2)}) collective-permute-start(bf16[512,2560]{1,0:T(8,128)(2,1)} %convolution_convert_fusion.1), channel_id=1, source_target_pairs={{0,1},{1,0},{2,3},{3,2},{4,5},{5,4},{6,7},{7,6},{8,9},{9,8},{10,11... | collective-permute-start | bytes 7864328 | tf_op jit(solution)/shard_map/ppermute | solution.py:47
  75.8 20.9 %collective-permute-start.17 = (bf16[800,256]{1,0:T(8,128)(2,1)S(1)}, bf16[800,256]{1,0:T(8,128)(2,1)S(1)}, u32[]{:S(2)}, u32[]{:S(2)}) collective-permute-start(bf16[800,256]{1,0:T(8,128)(2,1)S(1)} %fusion.17), channel_id=1, source_target_pairs={{0,16},{8,24},{16,0},{24,8},{1,17},{9,25},{17,1},{25,9},{2,18},{10... | collective-permute-start | bytes 1228808 | tf_op jit(solution)/shard_map/ppermute | solution.py:47
  79.0 59.7 %collective-permute-start.24 = (bf16[400,2560]{1,0:T(8,128)(2,1)S(1)}, bf16[400,2560]{1,0:T(8,128)(2,1)S(1)}, u32[]{:S(2)}, u32[]{:S(2)}) collective-permute-start(bf16[400,2560]{1,0:T(8,128)(2,1)S(1)} %fusion.3), channel_id=1, source_target_pairs={{0,4},{4,0},{1,5},{5,1},{2,6},{6,2},{3,7},{7,3},{8,12},{12,8},{9,1... | collective-permute-start | bytes 6144008 | tf_op jit(solution)/shard_map/ppermute | solution.py:47
  84.8 16.6 %collective-permute-start.16 = (bf16[2,64,2560]{2,1,0:T(8,128)(2,1)S(1)}, bf16[2,64,2560]{2,1,0:T(8,128)(2,1)S(1)}, u32[]{:S(2)}, u32[]{:S(2)}) collective-permute-start(bf16[2,64,2560]{2,1,0:T(8,128)(2,1)S(1)} %get-tuple-element.145), channel_id=1, source_target_pairs={{0,2},{2,0},{1,3},{3,1},{4,6},{6,4},{5,7},{7,5},{8,10},{10,8},{9,1... | collective-permute-start | bytes 1966088 | tf_op jit(solution)/shard_map/ppermute | solution.py:47
  96.7 9.8 %collective-permute-start.18 = (bf16[400,256]{1,0:T(8,128)(2,1)S(1)}, bf16[400,256]{1,0:T(8,128)(2,1)S(1)}, u32[]{:S(2)}, u32[]{:S(2)}) collective-permute-start(bf16[400,256]{1,0:T(8,128)(2,1)S(1)} %fusion.26), channel_id=1, source_target_pairs={{0,24},{8,16},{16,8},{24,0},{1,25},{9,17},{17,9},{25,1},{2,26},{10... | collective-permute-start | bytes 614408 | tf_op jit(solution)/shard_map/ppermute | solution.py:47
  99.7 30.6 %collective-permute-start.22 = (bf16[800,256]{1,0:T(8,128)(2,1)S(1)}, bf16[800,256]{1,0:T(8,128)(2,1)S(1)}, u32[]{:S(2)}, u32[]{:S(2)}) collective-permute-start(bf16[800,256]{1,0:T(8,128)(2,1)S(1)} %fusion.23), channel_id=1, source_target_pairs={{0,8},{8,0},{16,24},{24,16},{1,9},{9,1},{17,25},{25,17},{2,10},{10... | collective-permute-start | bytes 1228808 | tf_op jit(solution)/shard_map/ppermute | solution.py:47
  99.8 16.5 %collective-permute-start.20 = (bf16[2,64,2560]{2,1,0:T(8,128)(2,1)S(1)}, bf16[2,64,2560]{2,1,0:T(8,128)(2,1)S(1)}, u32[]{:S(2)}, u32[]{:S(2)}) collective-permute-start(bf16[2,64,2560]{2,1,0:T(8,128)(2,1)S(1)} %get-tuple-element.144), channel_id=1, source_target_pairs={{0,2},{2,0},{1,3},{3,1},{4,6},{6,4},{5,7},{7,5},{8,10},{10,8},{9,1... | collective-permute-start | bytes 1966088 | tf_op jit(solution)/shard_map/ppermute | solution.py:47
  106.5 22.9 %collective-permute-start.19 = (bf16[2,64,2560]{2,1,0:T(8,128)(2,1)S(1)}, bf16[2,64,2560]{2,1,0:T(8,128)(2,1)S(1)}, u32[]{:S(2)}, u32[]{:S(2)}) collective-permute-start(bf16[2,64,2560]{2,1,0:T(8,128)(2,1)S(1)} %fusion.8), channel_id=1, source_target_pairs={{0,8},{8,0},{16,24},{24,16},{1,9},{9,1},{17,25},{25,17},{2,10},{10... | collective-permute-start | bytes 1966088 | tf_op jit(solution)/shard_map/ppermute | solution.py:47
  107.8 25.3 %collective-permute-start.23 = (bf16[400,256]{1,0:T(8,128)(2,1)S(1)}, bf16[400,256]{1,0:T(8,128)(2,1)S(1)}, u32[]{:S(2)}, u32[]{:S(2)}) collective-permute-start(bf16[400,256]{1,0:T(8,128)(2,1)S(1)} %fusion.31), channel_id=1, source_target_pairs={{0,24},{8,16},{16,8},{24,0},{1,25},{9,17},{17,9},{25,1},{2,26},{10... | collective-permute-start | bytes 614408 | tf_op jit(solution)/shard_map/ppermute | solution.py:47
  129.5 3.6 %copy-start.2 = (bf16[256,3200]{1,0:T(8,128)(2,1)S(1)}, bf16[256,3200]{1,0:T(8,128)(2,1)}, u32[]{:S(2)}) copy-start(bf16[256,3200]{1,0:T(8,128)(2,1)} %up.3) | copy-start | bytes 4915204
  129.7 17.1 %collective-permute-start.21 = (bf16[64,2560]{1,0:T(8,128)(2,1)S(1)}, bf16[64,2560]{1,0:T(8,128)(2,1)S(1)}, u32[]{:S(2)}, u32[]{:S(2)}) collective-permute-start(bf16[64,2560]{1,0:T(8,128)(2,1)S(1)} %fusion.40), channel_id=1, source_target_pairs={{0,16},{8,24},{16,0},{24,8},{1,17},{9,25},{17,1},{25,9},{2,18},{10... | collective-permute-start | bytes 983048 | tf_op jit(solution)/shard_map/ppermute | solution.py:47

commit v5 on v0

--- a/solution.py
+++ b/solution.py
@@ -225,9 +225,6 @@
     last_y = exchange(last, "y", 1)
     columns += [exchange(sent[i], "z", parts[i][0]) for i in range(2, len(parts))]
     other_c = exchange(jnp.stack([other_y[0], other_y[1], last]), "c", 1)
-    last_y, columns, other_b = barrier((last_y, columns, other_b))
-    last_c = exchange(last_y, "c", 1)
-
     weight = call_kernel(
         join_kernel, place, (own_a, own_b, other_a, other_b),
         [whole(shape) for shape in sides] * 2,
@@ -236,6 +233,21 @@
     )
 
     half_tokens = nz * group_rows // 2
+
+    def gather_tokens(arrays, picks):
+        return call_kernel(
+            functools.partial(tokens_kernel, picks), place, arrays,
+            [whole(array.shape) for array in arrays], struct((half_tokens, width), bf16),
+            whole((half_tokens, width)), (1,), [], (0, 4 * half_tokens * width, 0),
+        )
+
+    even = gather_tokens(
+        (cotangent, own_y, own_c, far, other_y, first_c, other_c),
+        ((0, 0), (1, 0), (2, 0), (5, 0), (3, 0), (4, 0), (5, 1), (6, 0)),
+    )
+    far_back = matmul(weight, even[group_rows:], 1, 1, bf16)
+    last_y, columns, far_back, even = barrier((last_y, columns, far_back, even))
+    last_c = exchange(last_y, "c", 1)
     by_rows, by_lanes = (1, 3, 0, 2), (0, 2, 1, 3)
     keep, send, *by_units = call_kernel(
         functools.partial(columns_kernel, parts, by_rows, by_lanes), place, columns, piece_specs,
@@ -244,26 +256,14 @@
         (0, 12 * units * half_tokens, 0),
     )
 
-    def gather_tokens(arrays, picks):
-        return call_kernel(
-            functools.partial(tokens_kernel, picks), place, arrays,
-            [whole(array.shape) for array in arrays], struct((half_tokens, width), bf16),
-            whole((half_tokens, width)), (1,), [], (0, 4 * half_tokens * width, 0),
-        )
-
-    even = gather_tokens(
-        (cotangent, own_y, own_c, far, other_y, first_c, other_c),
-        ((0, 0), (1, 0), (2, 0), (5, 0), (3, 0), (4, 0), (5, 1), (6, 0)),
-    )
+    send, keep, last_c = barrier((send, keep, last_c))
     odd = gather_tokens(
         (near, last, last_y, other_y, first_c, other_c, last_c),
         ((0, 0), (3, 1), (4, 2), (5, 1), (1, 0), (2, 0), (5, 2), (6, 0)),
     )
-    even, odd, send, keep = barrier((even, odd, send, keep))
     flat = [even, odd]
 
     factor = float(total_tokens) ** (-0.5)
-
 
     def grad_half(r):
         return (matmul(by_units[r], flat[0]) + matmul(by_units[2 + r], flat[1])) * factor
@@ -272,28 +272,31 @@
         rows_of_k = flat[k % 2][k // 2 * group_rows : (k // 2 + 1) * group_rows]
         return matmul(weight, rows_of_k, 1, 1, bf16)
 
-    over_c = exchange(matmul(send, weight, dtype=bf16), "c", 1)
-    back = [None, None, back_of(2), None]
-    back[2], flat = barrier((back[2], flat))
+    given = matmul(send, weight, dtype=bf16)
+    given, flat = barrier((given, flat))
+    over_c = exchange(given, "c", 1)
     theirs = grad_half(1).astype(bf16)
-    theirs, keep, flat = barrier((theirs, keep, flat))
+    near_back, far_back = barrier((back_of(1), far_back))
+    theirs, keep, flat, near_back = barrier((theirs, keep, flat, near_back))
     over_x = exchange(theirs, "x", 1)
     kept = matmul(keep, weight, dtype=bf16)
-    back = [back_of(0), back_of(1), back[2], back_of(3)]
-    back = [back[0]] + [exchange(back[k], "z", k) for k in range(1, nz)]
+    near_back, far_back = exchange(near_back, "z", 1), exchange(far_back, "z", 2)
     sums = (kept.astype(f32) + over_c.astype(f32)).reshape(2, nz, rows, width)
     odd_y = exchange(sums[1, :2].astype(bf16), "y", 1)
     even_y = exchange(sums[1, 2:].astype(bf16), "y", 1)
+    odd_y, flat, near_back = barrier((odd_y, flat, near_back))
     odd_sum = (sums[0, :2] + odd_y.astype(f32)).astype(bf16)
-    odd_sum, back[2] = barrier((odd_sum, back[2]))
-    even_y, _ = barrier((even_y, odd_sum))
-    near_sum = exchange(odd_sum, "z", 1).astype(f32)
+    odd_sum, far_back = barrier((odd_sum, far_back))
+    own_grad = grad_half(0)
+    near_sum, even_y, own_grad = barrier((exchange(odd_sum, "z", 1), even_y, own_grad))
+    back = [near_back, far_back, exchange(back_of(3), "z", 3)]
+    near_sum = near_sum.astype(f32)
     even_sum = sums[0, 2:] + even_y.astype(f32)
     ours, across = even_sum[0] + near_sum[0], (even_sum[1] + near_sum[1]).astype(bf16)
-    across, back[3] = barrier((across, back[3]))
-    layer_out = (ours + exchange(across, "z", 2).astype(f32)).astype(bf16)
-
-    back, _ = barrier((back, across))
+    far_sum = exchange(across, "z", 2)
+
+    back, flat, _ = barrier((back, flat, across))
+    back = [back_of(0)] + back
     gate_grad, up_grad = call_kernel(
         functools.partial(grads_kernel, nz, units), place, (gate_pre, up_pre, *back),
         [wide] * 2 + [whole((units, group_rows))] * nz,
@@ -301,7 +304,9 @@
         (12 * act_bytes, 5 * act_bytes, act_bytes // 2),
     )
     over_x, _ = barrier((over_x, gate_grad))
-    weight_grad = grad_half(0) + over_x.astype(f32)
+    weight_grad = own_grad + over_x.astype(f32)
+    far_sum, weight_grad = barrier((far_sum, weight_grad))
+    layer_out = (ours + far_sum.astype(f32)).astype(bf16)
     return layer_out, gate_grad, up_grad, weight_grad
 
 

time: 141 us -> 150 us (1.064)
  waiting for transfers between devices: 77.3 us -> 82.8 us
    ppermute x24, waiting for transfers between devices: 77.3 us -> 82.8 us  [exchange(): return lax.ppermute(value, axis, [(i, i ^ offset) for i in range(size)])]
    add x1 -> x2, other arithmetic: 2.5 us -> 3.23 us  [the longest x1 2.5 us: paired_body(): weight_grad = own_grad + over_x.astype(f32)]
  transfers between devices with their start and end apart: 24 -> 24, of which waited for: 12 -> 12; matrix products, arithmetic and copies ran while one was open for 12% -> 12% of each run, Pallas kernels for 9% -> 8%
where the time goes in v5:
time: 150 us; the launch traced here: 149 us
  waiting for transfers between devices  82.8 us (55%)
  starting transfers between devices  26.1 us (17%)
  matrix products  17.4 us (12%)
  Pallas kernels  13 us (9%)
  other arithmetic  5.21 us (3%)
  local copies, waits for them, and re-layouts  4 us (3%)
    ppermute x24, waiting for transfers between devices, exchange(): return lax.ppermute(value, axis, [(i, i ^ offset) for i in range(size)])  82.8 us
    ppermute x24, starting transfers between devices, exchange(): return lax.ppermute(value, axis, [(i, i ^ offset) for i in range(size)])  26.1 us
    dot_general x10, matrix products, matmul(): lax.dot_general(lhs, rhs, dims, preferred_element_type=jnp.float32)  17.4 us
    pallas_call x7, Pallas kernels, call_kernel(): pl.pallas_call(kernel, out_shape=out_shapes, grid_spec=pltpu.PrefetchScal...  13 us
    unnamed x11, local copies, waits for them, and re-layouts  3.91 us
  transfers between devices with their start and end apart: 24, of which 12 were waited for; matrix products, arithmetic and copies ran while one was open for 12% of the time, Pallas kernels for 8%

profile of v5, /device:TPU:0, one launch (start us, length us, event | category | flops | bytes accessed | tf_op | source)
XLA Modules:
  0.0 149.5 jit_solution(16462049277790351132)
XLA Ops:
  0.6 3.0 %collective-permute-start.2 = (bf16[64,2560]{1,0:T(8,128)(2,1)}, bf16[64,2560]{1,0:T(8,128)(2,1)S(1)}, u32[]{:S(2)}, u32[]{:S(2)}) collective-permute-start(bf16[64,2560]{1,0:T(8,128)(2,1)} %refs_0_.1), channel_id=1, source_target_pairs={{0,2},{2,0},{1,3},{3,1},{4,6},{6,4},{5,7},{7,5},{8,10},{10,8},{9,1... | collective-permute-start | bytes 983048 | tf_op jit(solution)/shard_map/ppermute | solution.py:47
  3.7 1.6 %collective-permute-start.1 = (bf16[64,2560]{1,0:T(8,128)(2,1)}, bf16[64,2560]{1,0:T(8,128)(2,1)S(1)}, u32[]{:S(2)}, u32[]{:S(2)}) collective-permute-start(bf16[64,2560]{1,0:T(8,128)(2,1)} %refs_0_.1), channel_id=1, source_target_pairs={{0,8},{8,0},{16,24},{24,16},{1,9},{9,1},{17,25},{25,17},{2,10},{10... | collective-permute-start | bytes 983048 | tf_op jit(solution)/shard_map/ppermute | solution.py:47
  5.2 2.6 %collective-permute-start = (bf16[64,2560]{1,0:T(8,128)(2,1)}, bf16[64,2560]{1,0:T(8,128)(2,1)S(1)}, u32[]{:S(2)}, u32[]{:S(2)}) collective-permute-start(bf16[64,2560]{1,0:T(8,128)(2,1)} %refs_0_.1), channel_id=1, source_target_pairs={{0,16},{8,24},{16,0},{24,8},{1,17},{9,25},{17,1},{25,9},{2,18},{10... | collective-permute-start | bytes 983048 | tf_op jit(solution)/shard_map/ppermute | solution.py:47
  7.8 0.9 copy.9.scales
  8.8 1.6 %copy-done.3 = bf16[400,2560]{1,0:T(8,128)(2,1)S(1)} copy-done((bf16[400,2560]{1,0:T(8,128)(2,1)S(1)}, bf16[400,2560]{1,0:T(8,128)(2,1)}, u32[]{:S(2)}) %copy-start.3) | copy-done | bytes 2048024
  10.4 1.1 shard_map.85
  11.5 1.6 %collective-permute-start.7 = (bf16[400,1536]{1,0:T(8,128)(2,1)S(1)}, bf16[400,1536]{1,0:T(8,128)(2,1)S(1)}, u32[]{:S(2)}, u32[]{:S(2)}) collective-permute-start(bf16[400,1536]{1,0:T(8,128)(2,1)S(1)} %get-tuple-element.78.own_a), channel_id=1, source_target_pairs={{0,4},{4,0},{1,5},{5,1},{2,6},{6,2},{3,7},{7,3},{8,12},{12,8},{9,1... | collective-permute-start | bytes 3686408 | tf_op jit(solution)/shard_map/ppermute | solution.py:47
  13.1 1.4 copy-done.1
  14.5 2.8 %shard_map.84 = (bf16[800,256]{1,0:T(8,128)(2,1)S(1)}, bf16[800,256]{1,0:T(8,128)(2,1)S(1)}, bf16[800,256]{1,0:T(8,128)(2,1)S(1)}, bf16[800,256]{1,0:T(8,128)(2,1)S(1)}) custom-call(s32[4]{0:T(128)S(1)} %pad_add_fusion.place, bf16[256,3200]{1,0:T(8,128)(2,1)S(1)} %copy-done, bf16[256,3200]{1,0:T(8,128)(2,1)S(1)} %copy-done.1), custom_call_target="tpu_custom_call" | custom-call | flops 6553600 | bytes 4915200 | tf_op jit(solution)/shard_map/pallas_call | solution.py:52
  17.4 2.5 %collective-permute-done.1.refs_0_ = bf16[64,2560]{1,0:T(8,128)(2,1)S(1)} collective-permute-done((bf16[64,2560]{1,0:T(8,128)(2,1)}, bf16[64,2560]{1,0:T(8,128)(2,1)S(1)}, u32[]{:S(2)}, u32[]{:S(2)}) %collective-permute-start.1) | collective-permute-done | bytes 327712 | tf_op jit(solution)/shard_map/ppermute | solution.py:47
  19.9 2.4 %collective-permute-done.refs_3_ = bf16[64,2560]{1,0:T(8,128)(2,1)S(1)} collective-permute-done((bf16[64,2560]{1,0:T(8,128)(2,1)}, bf16[64,2560]{1,0:T(8,128)(2,1)S(1)}, u32[]{:S(2)}, u32[]{:S(2)}) %collective-permute-start) | collective-permute-done | bytes 327712 | tf_op jit(solution)/shard_map/ppermute | solution.py:47
  23.5 2.7 %collective-permute-start.4 = (bf16[64,2560]{1,0:T(8,128)(2,1)S(1)}, bf16[64,2560]{1,0:T(8,128)(2,1)S(1)}, u32[]{:S(2)}, u32[]{:S(2)}) collective-permute-start(bf16[64,2560]{1,0:T(8,128)(2,1)S(1)} %collective-permute-done.refs_3_), channel_id=1, source_target_pairs={{0,8},{8,0},{16,24},{24,16},{1,9},{9,1},{17,25},{25,17},{2,10},{10... | collective-permute-start | bytes 983048 | tf_op jit(solution)/shard_map/ppermute | solution.py:47
  26.2 13.5 %collective-permute-done.4.refs_1_ = bf16[64,2560]{1,0:T(8,128)(2,1)S(1)} collective-permute-done((bf16[64,2560]{1,0:T(8,128)(2,1)S(1)}, bf16[64,2560]{1,0:T(8,128)(2,1)S(1)}, u32[]{:S(2)}, u32[]{:S(2)}) %collective-permute-start.4) | collective-permute-done | bytes 327712 | tf_op jit(solution)/shard_map/ppermute | solution.py:47
  39.7 4.6 %collective-permute-done.6.refs_1_ = bf16[800,256]{1,0:T(8,128)(2,1)S(1)} collective-permute-done((bf16[800,256]{1,0:T(8,128)(2,1)S(1)}, bf16[800,256]{1,0:T(8,128)(2,1)S(1)}, u32[]{:S(2)}, u32[]{:S(2)}) %collective-permute-start.6) | collective-permute-done | bytes 409632 | tf_op jit(solution)/shard_map/ppermute | solution.py:47
  44.5 1.5 %collective-permute-start.12 = (bf16[400,1024]{1,0:T(8,128)(2,1)S(1)}, bf16[400,1024]{1,0:T(8,128)(2,1)S(1)}, u32[]{:S(2)}, u32[]{:S(2)}) collective-permute-start(bf16[400,1024]{1,0:T(8,128)(2,1)S(1)} %get-tuple-element.87.own_b), channel_id=1, source_target_pairs={{0,4},{4,0},{1,5},{5,1},{2,6},{6,2},{3,7},{7,3},{8,12},{12,8},{9,1... | collective-permute-start | bytes 2457608 | tf_op jit(solution)/shard_map/ppermute | solution.py:47
  46.1 1.5 %collective-permute-start.9 = (bf16[64,2560]{1,0:T(8,128)(2,1)S(1)}, bf16[64,2560]{1,0:T(8,128)(2,1)S(1)}, u32[]{:S(2)}, u32[]{:S(2)}) collective-permute-start(bf16[64,2560]{1,0:T(8,128)(2,1)S(1)} %collective-permute-done.4.refs_1_), channel_id=1, source_target_pairs={{0,2},{2,0},{1,3},{3,1},{4,6},{6,4},{5,7},{7,5},{8,10},{10,8},{9,1... | collective-permute-start | bytes 983048 | tf_op jit(solution)/shard_map/ppermute | solution.py:47
  47.6 1.3 collective-permute-start.10
  48.9 16.2 %collective-permute-done.12.other_b = bf16[400,1024]{1,0:T(8,128)(2,1)S(1)} collective-permute-done((bf16[400,1024]{1,0:T(8,128)(2,1)S(1)}, bf16[400,1024]{1,0:T(8,128)(2,1)S(1)}, u32[]{:S(2)}, u32[]{:S(2)}) %collective-permute-start.12) | collective-permute-done | bytes 819232 | tf_op jit(solution)/shard_map/ppermute | solution.py:47
  65.1 0.8 shard_map.86
  66.0 0.7 shard_map.87
  66.7 1.3 fusion.23
  68.0 0.7 collective-permute-done.11.refs_3_
  68.7 1.1 shard_map.88
  70.3 4.1 %convolution_convert_fusion.1 = bf16[512,2560]{1,0:T(8,128)(2,1)} fusion(bf16[512,800]{1,0:T(8,128)(2,1)S(1)} %get-tuple-element.100, bf16[800,2560]{1,0:T(8,128)(2,1)S(1)} %shard_map.86), kind=kOutput, calls=%fused_computation.6 | convolution fusion | flops 2098462720 | bytes 7536640 | tf_op jit(solution)/shard_map/dot_general | solution.py:174
  74.4 0.7 shard_map.89
  75.4 1.2 fusion.14
  76.6 1.2 fusion.31
  77.8 1.2 fusion.2
  79.1 3.3 %convolution_convert_fusion = bf16[512,2560]{1,0:T(8,128)(2,1)S(1)} fusion(bf16[512,800]{1,0:T(8,128)(2,1)S(1)} %get-tuple-element.109, bf16[800,2560]{1,0:T(8,128)(2,1)S(1)} %shard_map.86), kind=kOutput, calls=%fused_computation.5 | convolution fusion | flops 2098462720 | bytes 7536640 | tf_op jit(solution)/shard_map/dot_general | solution.py:174
  82.4 0.7 convert_add_fusion
  83.5 1.0 collective-permute-start.16
  84.5 2.3 %collective-permute-start.18 = (bf16[800,256]{1,0:T(8,128)(2,1)S(1)}, bf16[800,256]{1,0:T(8,128)(2,1)S(1)}, u32[]{:S(2)}, u32[]{:S(2)}) collective-permute-start(bf16[800,256]{1,0:T(8,128)(2,1)S(1)} %fusion.23), channel_id=1, source_target_pairs={{0,16},{8,24},{16,0},{24,8},{1,17},{9,25},{17,1},{25,9},{2,18},{10... | collective-permute-start | bytes 1228808 | tf_op jit(solution)/shard_map/ppermute | solution.py:47
  86.9 1.1 collective-permute-start.22
  87.9 1.0 collective-permute-start.20
  88.9 15.4 %collective-permute-done.17.refs_1_ = bf16[800,256]{1,0:T(8,128)(2,1)S(1)} collective-permute-done((bf16[800,256]{1,0:T(8,128)(2,1)S(1)}, bf16[800,256]{1,0:T(8,128)(2,1)S(1)}, u32[]{:S(2)}, u32[]{:S(2)}) %collective-permute-start.17) | collective-permute-done | bytes 409632 | tf_op jit(solution)/shard_map/ppermute | solution.py:47
  104.4 1.3 collective-permute-done.18.refs_2_
  105.7 1.3 fusion.17
  107.0 2.2 %collective-permute-start.23 = (bf16[800,256]{1,0:T(8,128)(2,1)S(1)}, bf16[800,256]{1,0:T(8,128)(2,1)S(1)}, u32[]{:S(2)}, u32[]{:S(2)}) collective-permute-start(bf16[800,256]{1,0:T(8,128)(2,1)S(1)} %fusion.17), channel_id=1, source_target_pairs={{0,24},{8,16},{16,8},{24,0},{1,25},{9,17},{17,9},{25,1},{2,26},{10... | collective-permute-start | bytes 1228808 | tf_op jit(solution)/shard_map/ppermute | solution.py:47
  109.2 1.2 fusion.32
  110.4 1.3 fusion
  111.7 2.9 %collective-permute-done.20 = bf16[2,64,2560]{2,1,0:T(8,128)(2,1)S(1)} collective-permute-done((bf16[2,64,2560]{2,1,0:T(8,128)(2,1)S(1)}, bf16[2,64,2560]{2,1,0:T(8,128)(2,1)S(1)}, u32[]{:S(2)}, u32[]{:S(2)}) %collective-permute-start.20) | collective-permute-done | bytes 655392 | tf_op jit(solution)/shard_map/ppermute | solution.py:47
  114.7 16.8 %collective-permute-done.19 = bf16[2,64,2560]{2,1,0:T(8,128)(2,1)S(1)} collective-permute-done((bf16[2,64,2560]{2,1,0:T(8,128)(2,1)S(1)}, bf16[2,64,2560]{2,1,0:T(8,128)(2,1)S(1)}, u32[]{:S(2)}, u32[]{:S(2)}) %collective-permute-start.19) | collective-permute-done | bytes 655392 | tf_op jit(solution)/shard_map/ppermute | solution.py:47
  131.9 1.4 collective-permute-start.21
  133.3 1.3 fusion.20.refs_0_
  134.6 5.7 %shard_map.90 = (bf16[256,3200]{1,0:T(8,128)(2,1)}, bf16[256,3200]{1,0:T(8,128)(2,1)}) custom-call(s32[4]{0:T(128)S(1)} %pad_add_fusion.place, bf16[256,3200]{1,0:T(8,128)(2,1)S(1)} %copy-done, bf16[256,3200]{1,0:T(8,128)(2,1)S(1)} %copy-done.2, bf16[800,256]{1,0:T(8,128)(2,1)S(1)} %fusion.20.refs_0_, bf16[800,256]{1,0:T(8,128)(2,1)S(1)} %collective-permute-done.17.refs_1_, ...), custom_call_target="tpu_custom_call" | custom-call | flops 19660800 | bytes 8192000 | tf_op jit(solution)/shard_map/pallas_call | solution.py:52
  140.2 2.5 %convert_add_fusion.1 = f32[400,2560]{1,0:T(8,128)} fusion(f32[400,2560]{1,0:T(8,128)S(1)} %fusion, bf16[400,2560]{1,0:T(8,128)(2,1)S(1)} %collective-permute-done.22), kind=kLoop, calls=%fused_computation.8 | loop fusion | flops 2048000 | bytes 10240000 | tf_op jit(solution)/shard_map/add | solution.py:307
  142.7 6.0 %collective-permute-done.21 = bf16[64,2560]{1,0:T(8,128)(2,1)S(1)} collective-permute-done((bf16[64,2560]{1,0:T(8,128)(2,1)S(1)}, bf16[64,2560]{1,0:T(8,128)(2,1)S(1)}, u32[]{:S(2)}, u32[]{:S(2)}) %collective-permute-start.21) | collective-permute-done | bytes 327712 | tf_op jit(solution)/shard_map/ppermute | solution.py:47
  148.7 0.8 fusion.29
  (41 shorter events, 3.0 us)
Async XLA Ops:
  0.6 12.5 %copy-start = (bf16[256,3200]{1,0:T(8,128)(2,1)S(1)}, bf16[256,3200]{1,0:T(8,128)(2,1)}, u32[]{:S(2)}) copy-start(bf16[256,3200]{1,0:T(8,128)(2,1)} %gate.3) | copy-start | bytes 4915204
  0.6 16.8 %collective-permute-start.2 = (bf16[64,2560]{1,0:T(8,128)(2,1)}, bf16[64,2560]{1,0:T(8,128)(2,1)S(1)}, u32[]{:S(2)}, u32[]{:S(2)}) collective-permute-start(bf16[64,2560]{1,0:T(8,128)(2,1)} %refs_0_.1), channel_id=1, source_target_pairs={{0,2},{2,0},{1,3},{3,1},{4,6},{6,4},{5,7},{7,5},{8,10},{10,8},{9,1... | collective-permute-start | bytes 983048 | tf_op jit(solution)/shard_map/ppermute | solution.py:47
  3.7 16.3 %collective-permute-start.1 = (bf16[64,2560]{1,0:T(8,128)(2,1)}, bf16[64,2560]{1,0:T(8,128)(2,1)S(1)}, u32[]{:S(2)}, u32[]{:S(2)}) collective-permute-start(bf16[64,2560]{1,0:T(8,128)(2,1)} %refs_0_.1), channel_id=1, source_target_pairs={{0,8},{8,0},{16,24},{24,16},{1,9},{9,1},{17,25},{25,17},{2,10},{10... | collective-permute-start | bytes 983048 | tf_op jit(solution)/shard_map/ppermute | solution.py:47
  5.2 17.1 %collective-permute-start = (bf16[64,2560]{1,0:T(8,128)(2,1)}, bf16[64,2560]{1,0:T(8,128)(2,1)S(1)}, u32[]{:S(2)}, u32[]{:S(2)}) collective-permute-start(bf16[64,2560]{1,0:T(8,128)(2,1)} %refs_0_.1), channel_id=1, source_target_pairs={{0,16},{8,24},{16,0},{24,8},{1,17},{9,25},{17,1},{25,9},{2,18},{10... | collective-permute-start | bytes 983048 | tf_op jit(solution)/shard_map/ppermute | solution.py:47
  7.8 14.5 %collective-permute-start.3 = (bf16[64,2560]{1,0:T(8,128)(2,1)}, bf16[64,2560]{1,0:T(8,128)(2,1)S(1)}, u32[]{:S(2)}, u32[]{:S(2)}) collective-permute-start(bf16[64,2560]{1,0:T(8,128)(2,1)} %refs_0_.1), channel_id=1, source_target_pairs={{0,1},{1,0},{2,3},{3,2},{4,5},{5,4},{6,7},{7,6},{8,9},{9,8},{10,11... | collective-permute-start | bytes 983048 | tf_op jit(solution)/shard_map/ppermute | solution.py:47
  8.8 1.6 %copy-start.3 = (bf16[400,2560]{1,0:T(8,128)(2,1)S(1)}, bf16[400,2560]{1,0:T(8,128)(2,1)}, u32[]{:S(2)}) copy-start(bf16[400,2560]{1,0:T(8,128)(2,1)} %codes.1) | copy-start | bytes 6144004
  11.5 32.8 %collective-permute-start.7 = (bf16[400,1536]{1,0:T(8,128)(2,1)S(1)}, bf16[400,1536]{1,0:T(8,128)(2,1)S(1)}, u32[]{:S(2)}, u32[]{:S(2)}) collective-permute-start(bf16[400,1536]{1,0:T(8,128)(2,1)S(1)} %get-tuple-element.78.own_a), channel_id=1, source_target_pairs={{0,4},{4,0},{1,5},{5,1},{2,6},{6,2},{3,7},{7,3},{8,12},{12,8},{9,1... | collective-permute-start | bytes 3686408 | tf_op jit(solution)/shard_map/ppermute | solution.py:47
  13.1 1.4 copy-start.1
  22.5 21.9 %collective-permute-start.8 = (bf16[3,64,2560]{2,1,0:T(8,128)(2,1)S(1)}, bf16[3,64,2560]{2,1,0:T(8,128)(2,1)S(1)}, u32[]{:S(2)}, u32[]{:S(2)}) collective-permute-start(bf16[3,64,2560]{2,1,0:T(8,128)(2,1)S(1)} %pad_maximum_fusion), channel_id=1, source_target_pairs={{0,1},{1,0},{2,3},{3,2},{4,5},{5,4},{6,7},{7,6},{8,9},{9,8},{10,11... | collective-permute-start | bytes 2949128 | tf_op jit(solution)/shard_map/ppermute | solution.py:47
  22.6 21.7 %collective-permute-start.5 = (bf16[2,64,2560]{2,1,0:T(8,128)(2,1)S(1)}, bf16[2,64,2560]{2,1,0:T(8,128)(2,1)S(1)}, u32[]{:S(2)}, u32[]{:S(2)}) collective-permute-start(bf16[2,64,2560]{2,1,0:T(8,128)(2,1)S(1)} %pad_maximum_fusion.2), channel_id=1, source_target_pairs={{0,2},{2,0},{1,3},{3,1},{4,6},{6,4},{5,7},{7,5},{8,10},{10,8},{9,1... | collective-permute-start | bytes 1966088 | tf_op jit(solution)/shard_map/ppermute | solution.py:47
  23.2 21.1 %collective-permute-start.6 = (bf16[800,256]{1,0:T(8,128)(2,1)S(1)}, bf16[800,256]{1,0:T(8,128)(2,1)S(1)}, u32[]{:S(2)}, u32[]{:S(2)}) collective-permute-start(bf16[800,256]{1,0:T(8,128)(2,1)S(1)} %get-tuple-element.77), channel_id=1, source_target_pairs={{0,16},{8,24},{16,0},{24,8},{1,17},{9,25},{17,1},{25,9},{2,18},{10... | collective-permute-start | bytes 1228808 | tf_op jit(solution)/shard_map/ppermute | solution.py:47
  23.5 16.2 %collective-permute-start.4 = (bf16[64,2560]{1,0:T(8,128)(2,1)S(1)}, bf16[64,2560]{1,0:T(8,128)(2,1)S(1)}, u32[]{:S(2)}, u32[]{:S(2)}) collective-permute-start(bf16[64,2560]{1,0:T(8,128)(2,1)S(1)} %collective-permute-done.refs_3_), channel_id=1, source_target_pairs={{0,8},{8,0},{16,24},{24,16},{1,9},{9,1},{17,25},{25,17},{2,10},{10... | collective-permute-start | bytes 983048 | tf_op jit(solution)/shard_map/ppermute | solution.py:47
  44.4 21.6 %collective-permute-start.13 = (bf16[3,64,2560]{2,1,0:T(8,128)(2,1)S(1)}, bf16[3,64,2560]{2,1,0:T(8,128)(2,1)S(1)}, u32[]{:S(2)}, u32[]{:S(2)}) collective-permute-start(bf16[3,64,2560]{2,1,0:T(8,128)(2,1)S(1)} %pad_maximum_fusion.1), channel_id=1, source_target_pairs={{0,1},{1,0},{2,3},{3,2},{4,5},{5,4},{6,7},{7,6},{8,9},{9,8},{10,11... | collective-permute-start | bytes 2949128 | tf_op jit(solution)/shard_map/ppermute | solution.py:47
  44.5 21.5 %copy-start.4 = (bf16[64,2560]{1,0:T(8,128)(2,1)S(1)}, bf16[64,2560]{1,0:T(8,128)(2,1)}, u32[]{:S(2)}) copy-start(bf16[64,2560]{1,0:T(8,128)(2,1)} %refs_0_.1) | copy-start | bytes 983044
  44.5 20.6 %collective-permute-start.12 = (bf16[400,1024]{1,0:T(8,128)(2,1)S(1)}, bf16[400,1024]{1,0:T(8,128)(2,1)S(1)}, u32[]{:S(2)}, u32[]{:S(2)}) collective-permute-start(bf16[400,1024]{1,0:T(8,128)(2,1)S(1)} %get-tuple-element.87.own_b), channel_id=1, source_target_pairs={{0,4},{4,0},{1,5},{5,1},{2,6},{6,2},{3,7},{7,3},{8,12},{12,8},{9,1... | collective-permute-start | bytes 2457608 | tf_op jit(solution)/shard_map/ppermute | solution.py:47
  46.1 21.9 %collective-permute-start.9 = (bf16[64,2560]{1,0:T(8,128)(2,1)S(1)}, bf16[64,2560]{1,0:T(8,128)(2,1)S(1)}, u32[]{:S(2)}, u32[]{:S(2)}) collective-permute-start(bf16[64,2560]{1,0:T(8,128)(2,1)S(1)} %collective-permute-done.4.refs_1_), channel_id=1, source_target_pairs={{0,2},{2,0},{1,3},{3,1},{4,6},{6,4},{5,7},{7,5},{8,10},{10,8},{9,1... | collective-permute-start | bytes 983048 | tf_op jit(solution)/shard_map/ppermute | solution.py:47
  47.6 20.4 %collective-permute-start.10 = (bf16[800,256]{1,0:T(8,128)(2,1)S(1)}, bf16[800,256]{1,0:T(8,128)(2,1)S(1)}, u32[]{:S(2)}, u32[]{:S(2)}) collective-permute-start(bf16[800,256]{1,0:T(8,128)(2,1)S(1)} %get-tuple-element.85), channel_id=1, source_target_pairs={{0,24},{8,16},{16,8},{24,0},{1,25},{9,17},{17,9},{25,1},{2,26},{10... | collective-permute-start | bytes 1228808 | tf_op jit(solution)/shard_map/ppermute | solution.py:47
  48.9 19.7 %collective-permute-start.11 = (bf16[800,256]{1,0:T(8,128)(2,1)S(1)}, bf16[800,256]{1,0:T(8,128)(2,1)S(1)}, u32[]{:S(2)}, u32[]{:S(2)}) collective-permute-start(bf16[800,256]{1,0:T(8,128)(2,1)S(1)} %get-tuple-element.86), channel_id=1, source_target_pairs={{0,8},{8,0},{16,24},{24,16},{1,9},{9,1},{17,25},{25,17},{2,10},{10... | collective-permute-start | bytes 1228808 | tf_op jit(solution)/shard_map/ppermute | solution.py:47
  68.7 1.6 %collective-permute-start.14 = (bf16[64,2560]{1,0:T(8,128)(2,1)S(1)}, bf16[64,2560]{1,0:T(8,128)(2,1)S(1)}, u32[]{:S(2)}, u32[]{:S(2)}) collective-permute-start(bf16[64,2560]{1,0:T(8,128)(2,1)S(1)} %collective-permute-done.9.refs_2_), channel_id=1, source_target_pairs={{0,1},{1,0},{2,3},{3,2},{4,5},{5,4},{6,7},{7,6},{8,9},{9,8},{10,11... | collective-permute-start | bytes 983048 | tf_op jit(solution)/shard_map/ppermute | solution.py:47
  75.2 7.2 %collective-permute-start.15 = (bf16[512,2560]{1,0:T(8,128)(2,1)}, bf16[512,2560]{1,0:T(8,128)(2,1)S(1)}, u32[]{:S(2)}, u32[]{:S(2)}) collective-permute-start(bf16[512,2560]{1,0:T(8,128)(2,1)} %convolution_convert_fusion.1), channel_id=1, source_target_pairs={{0,1},{1,0},{2,3},{3,2},{4,5},{5,4},{6,7},{7,6},{8,9},{9,8},{10,11... | collective-permute-start | bytes 7864328 | tf_op jit(solution)/shard_map/ppermute | solution.py:47
  83.5 20.8 %collective-permute-start.16 = (bf16[2,64,2560]{2,1,0:T(8,128)(2,1)S(1)}, bf16[2,64,2560]{2,1,0:T(8,128)(2,1)S(1)}, u32[]{:S(2)}, u32[]{:S(2)}) collective-permute-start(bf16[2,64,2560]{2,1,0:T(8,128)(2,1)S(1)} %get-tuple-element.137), channel_id=1, source_target_pairs={{0,2},{2,0},{1,3},{3,1},{4,6},{6,4},{5,7},{7,5},{8,10},{10,8},{9,1... | collective-permute-start | bytes 1966088 | tf_op jit(solution)/shard_map/ppermute | solution.py:47
  84.5 19.8 %collective-permute-start.17 = (bf16[800,256]{1,0:T(8,128)(2,1)S(1)}, bf16[800,256]{1,0:T(8,128)(2,1)S(1)}, u32[]{:S(2)}, u32[]{:S(2)}) collective-permute-start(bf16[800,256]{1,0:T(8,128)(2,1)S(1)} %fusion.14), channel_id=1, source_target_pairs={{0,8},{8,0},{16,24},{24,16},{1,9},{9,1},{17,25},{25,17},{2,10},{10... | collective-permute-start | bytes 1228808 | tf_op jit(solution)/shard_map/ppermute | solution.py:47
  84.5 21.2 %collective-permute-start.18 = (bf16[800,256]{1,0:T(8,128)(2,1)S(1)}, bf16[800,256]{1,0:T(8,128)(2,1)S(1)}, u32[]{:S(2)}, u32[]{:S(2)}) collective-permute-start(bf16[800,256]{1,0:T(8,128)(2,1)S(1)} %fusion.23), channel_id=1, source_target_pairs={{0,16},{8,24},{16,0},{24,8},{1,17},{9,25},{17,1},{25,9},{2,18},{10... | collective-permute-start | bytes 1228808 | tf_op jit(solution)/shard_map/ppermute | solution.py:47
  86.9 53.3 %collective-permute-start.22 = (bf16[400,2560]{1,0:T(8,128)(2,1)S(1)}, bf16[400,2560]{1,0:T(8,128)(2,1)S(1)}, u32[]{:S(2)}, u32[]{:S(2)}) collective-permute-start(bf16[400,2560]{1,0:T(8,128)(2,1)S(1)} %fusion.2), channel_id=1, source_target_pairs={{0,4},{4,0},{1,5},{5,1},{2,6},{6,2},{3,7},{7,3},{8,12},{12,8},{9,1... | collective-permute-start | bytes 6144008 | tf_op jit(solution)/shard_map/ppermute | solution.py:47
  87.9 26.7 %collective-permute-start.20 = (bf16[2,64,2560]{2,1,0:T(8,128)(2,1)S(1)}, bf16[2,64,2560]{2,1,0:T(8,128)(2,1)S(1)}, u32[]{:S(2)}, u32[]{:S(2)}) collective-permute-start(bf16[2,64,2560]{2,1,0:T(8,128)(2,1)S(1)} %get-tuple-element.136), channel_id=1, source_target_pairs={{0,2},{2,0},{1,3},{3,1},{4,6},{6,4},{5,7},{7,5},{8,10},{10,8},{9,1... | collective-permute-start | bytes 1966088 | tf_op jit(solution)/shard_map/ppermute | solution.py:47
  107.0 26.3 %collective-permute-start.23 = (bf16[800,256]{1,0:T(8,128)(2,1)S(1)}, bf16[800,256]{1,0:T(8,128)(2,1)S(1)}, u32[]{:S(2)}, u32[]{:S(2)}) collective-permute-start(bf16[800,256]{1,0:T(8,128)(2,1)S(1)} %fusion.17), channel_id=1, source_target_pairs={{0,24},{8,16},{16,8},{24,0},{1,25},{9,17},{17,9},{25,1},{2,26},{10... | collective-permute-start | bytes 1228808 | tf_op jit(solution)/shard_map/ppermute | solution.py:47
  109.2 22.3 %collective-permute-start.19 = (bf16[2,64,2560]{2,1,0:T(8,128)(2,1)S(1)}, bf16[2,64,2560]{2,1,0:T(8,128)(2,1)S(1)}, u32[]{:S(2)}, u32[]{:S(2)}) collective-permute-start(bf16[2,64,2560]{2,1,0:T(8,128)(2,1)S(1)} %fusion.4), channel_id=1, source_target_pairs={{0,8},{8,0},{16,24},{24,16},{1,9},{9,1},{17,25},{25,17},{2,10},{10... | collective-permute-start | bytes 1966088 | tf_op jit(solution)/shard_map/ppermute | solution.py:47
  131.9 2.7 %copy-start.2 = (bf16[256,3200]{1,0:T(8,128)(2,1)S(1)}, bf16[256,3200]{1,0:T(8,128)(2,1)}, u32[]{:S(2)}) copy-start(bf16[256,3200]{1,0:T(8,128)(2,1)} %up.3) | copy-start | bytes 4915204
  131.9 16.8 %collective-permute-start.21 = (bf16[64,2560]{1,0:T(8,128)(2,1)S(1)}, bf16[64,2560]{1,0:T(8,128)(2,1)S(1)}, u32[]{:S(2)}, u32[]{:S(2)}) collective-permute-start(bf16[64,2560]{1,0:T(8,128)(2,1)S(1)} %fusion.30), channel_id=1, source_target_pairs={{0,16},{8,24},{16,0},{24,8},{1,17},{9,25},{17,1},{25,9},{2,18},{10... | collective-permute-start | bytes 983048 | tf_op jit(solution)/shard_map/ppermute | solution.py:47

commit v6 on v5

--- a/solution.py
+++ b/solution.py
@@ -276,27 +276,26 @@
     given, flat = barrier((given, flat))
     over_c = exchange(given, "c", 1)
     theirs = grad_half(1).astype(bf16)
-    near_back, far_back = barrier((back_of(1), far_back))
-    theirs, keep, flat, near_back = barrier((theirs, keep, flat, near_back))
+    theirs, keep, flat = barrier((theirs, keep, flat))
     over_x = exchange(theirs, "x", 1)
     kept = matmul(keep, weight, dtype=bf16)
-    near_back, far_back = exchange(near_back, "z", 1), exchange(far_back, "z", 2)
+    back = [None, back_of(1), far_back, back_of(3)]
+    back = [None] + [exchange(back[k], "z", k) for k in range(1, nz)]
     sums = (kept.astype(f32) + over_c.astype(f32)).reshape(2, nz, rows, width)
     odd_y = exchange(sums[1, :2].astype(bf16), "y", 1)
     even_y = exchange(sums[1, 2:].astype(bf16), "y", 1)
-    odd_y, flat, near_back = barrier((odd_y, flat, near_back))
+    odd_y, flat = barrier((odd_y, flat))
+    back[0] = back_of(0)
     odd_sum = (sums[0, :2] + odd_y.astype(f32)).astype(bf16)
-    odd_sum, far_back = barrier((odd_sum, far_back))
-    own_grad = grad_half(0)
-    near_sum, even_y, own_grad = barrier((exchange(odd_sum, "z", 1), even_y, own_grad))
-    back = [near_back, far_back, exchange(back_of(3), "z", 3)]
-    near_sum = near_sum.astype(f32)
+    odd_sum, back[2] = barrier((odd_sum, back[2]))
+    even_y, _ = barrier((even_y, odd_sum))
+    near_sum = exchange(odd_sum, "z", 1).astype(f32)
     even_sum = sums[0, 2:] + even_y.astype(f32)
     ours, across = even_sum[0] + near_sum[0], (even_sum[1] + near_sum[1]).astype(bf16)
-    far_sum = exchange(across, "z", 2)
-
-    back, flat, _ = barrier((back, flat, across))
-    back = [back_of(0)] + back
+    across, back[3] = barrier((across, back[3]))
+    layer_out = (ours + exchange(across, "z", 2).astype(f32)).astype(bf16)
+
+    back, _ = barrier((back, across))
     gate_grad, up_grad = call_kernel(
         functools.partial(grads_kernel, nz, units), place, (gate_pre, up_pre, *back),
         [wide] * 2 + [whole((units, group_rows))] * nz,
@@ -304,9 +303,7 @@
         (12 * act_bytes, 5 * act_bytes, act_bytes // 2),
     )
     over_x, _ = barrier((over_x, gate_grad))
-    weight_grad = own_grad + over_x.astype(f32)
-    far_sum, weight_grad = barrier((far_sum, weight_grad))
-    layer_out = (ours + far_sum.astype(f32)).astype(bf16)
+    weight_grad = grad_half(0) + over_x.astype(f32)
     return layer_out, gate_grad, up_grad, weight_grad
 
 

time: 150 us -> 144 us (0.960)
  waiting for transfers between devices: 82.8 us -> 78.5 us
  other arithmetic: 5.21 us -> 2.71 us
    ppermute x24, waiting for transfers between devices: 82.8 us -> 78.5 us  [exchange(): return lax.ppermute(value, axis, [(i, i ^ offset) for i in range(size)])]
    add x1 -> x0, other arithmetic: 2.5 us -> none  [paired_body(): weight_grad = own_grad + over_x.astype(f32)]
  transfers between devices with their start and end apart: 24 -> 24, of which waited for: 12 -> 13; matrix products, arithmetic and copies ran while one was open for 12% -> 12% of each run, Pallas kernels for 8% -> 9%
where the time goes in v6:
time: 144 us
  waiting for transfers between devices  78.5 us (55%)
  starting transfers between devices  26.1 us (18%)
  matrix products  18.2 us (13%)
  Pallas kernels  13 us (9%)
  local copies, waits for them, and re-layouts  3.99 us (3%)
  other arithmetic  2.71 us (2%)
    ppermute x24, waiting for transfers between devices, exchange(): return lax.ppermute(value, axis, [(i, i ^ offset) for i in range(size)])  78.5 us
    ppermute x24, starting transfers between devices, exchange(): return lax.ppermute(value, axis, [(i, i ^ offset) for i in range(size)])  26.1 us
    dot_general x10, matrix products, matmul(): lax.dot_general(lhs, rhs, dims, preferred_element_type=jnp.float32)  18.2 us
    pallas_call x7, Pallas kernels, call_kernel(): pl.pallas_call(kernel, out_shape=out_shapes, grid_spec=pltpu.PrefetchScal...  13 us
    unnamed x11, local copies, waits for them, and re-layouts  3.91 us
  transfers between devices with their start and end apart: 24, of which 13 were waited for; matrix products, arithmetic and copies ran while one was open for 12% of the time, Pallas kernels for 9%

profile of v6, /device:TPU:0, one launch (start us, length us, event | category | flops | bytes accessed | tf_op | source)
XLA Modules:
  0.0 143.5 jit_solution(10328177866528096411)
XLA Ops:
  0.6 4.1 %collective-permute-start = (bf16[64,2560]{1,0:T(8,128)(2,1)}, bf16[64,2560]{1,0:T(8,128)(2,1)S(1)}, u32[]{:S(2)}, u32[]{:S(2)}) collective-permute-start(bf16[64,2560]{1,0:T(8,128)(2,1)} %refs_0_.1), channel_id=1, source_target_pairs={{0,16},{8,24},{16,0},{24,8},{1,17},{9,25},{17,1},{25,9},{2,18},{10... | collective-permute-start | bytes 983048 | tf_op jit(solution)/shard_map/ppermute | solution.py:47
  4.7 1.6 %collective-permute-start.1 = (bf16[64,2560]{1,0:T(8,128)(2,1)}, bf16[64,2560]{1,0:T(8,128)(2,1)S(1)}, u32[]{:S(2)}, u32[]{:S(2)}) collective-permute-start(bf16[64,2560]{1,0:T(8,128)(2,1)} %refs_0_.1), channel_id=1, source_target_pairs={{0,8},{8,0},{16,24},{24,16},{1,9},{9,1},{17,25},{25,17},{2,10},{10... | collective-permute-start | bytes 983048 | tf_op jit(solution)/shard_map/ppermute | solution.py:47
  6.3 1.5 %collective-permute-start.2 = (bf16[64,2560]{1,0:T(8,128)(2,1)}, bf16[64,2560]{1,0:T(8,128)(2,1)S(1)}, u32[]{:S(2)}, u32[]{:S(2)}) collective-permute-start(bf16[64,2560]{1,0:T(8,128)(2,1)} %refs_0_.1), channel_id=1, source_target_pairs={{0,2},{2,0},{1,3},{3,1},{4,6},{6,4},{5,7},{7,5},{8,10},{10,8},{9,1... | collective-permute-start | bytes 983048 | tf_op jit(solution)/shard_map/ppermute | solution.py:47
  7.8 0.9 copy.9.scales
  8.8 1.6 %copy-done.3 = bf16[400,2560]{1,0:T(8,128)(2,1)S(1)} copy-done((bf16[400,2560]{1,0:T(8,128)(2,1)S(1)}, bf16[400,2560]{1,0:T(8,128)(2,1)}, u32[]{:S(2)}) %copy-start.3) | copy-done | bytes 2048024
  10.4 1.1 shard_map.85
  11.5 1.6 %collective-permute-start.7 = (bf16[400,1536]{1,0:T(8,128)(2,1)S(1)}, bf16[400,1536]{1,0:T(8,128)(2,1)S(1)}, u32[]{:S(2)}, u32[]{:S(2)}) collective-permute-start(bf16[400,1536]{1,0:T(8,128)(2,1)S(1)} %get-tuple-element.72.own_a), channel_id=1, source_target_pairs={{0,4},{4,0},{1,5},{5,1},{2,6},{6,2},{3,7},{7,3},{8,12},{12,8},{9,1... | collective-permute-start | bytes 3686408 | tf_op jit(solution)/shard_map/ppermute | solution.py:47
  13.1 1.4 copy-done.1
  14.5 2.8 %shard_map.84 = (bf16[800,256]{1,0:T(8,128)(2,1)S(1)}, bf16[800,256]{1,0:T(8,128)(2,1)S(1)}, bf16[800,256]{1,0:T(8,128)(2,1)S(1)}, bf16[800,256]{1,0:T(8,128)(2,1)S(1)}) custom-call(s32[4]{0:T(128)S(1)} %pad_add_fusion.place, bf16[256,3200]{1,0:T(8,128)(2,1)S(1)} %copy-done, bf16[256,3200]{1,0:T(8,128)(2,1)S(1)} %copy-done.1), custom_call_target="tpu_custom_call" | custom-call | flops 6553600 | bytes 4915200 | tf_op jit(solution)/shard_map/pallas_call | solution.py:52
  17.4 2.4 %collective-permute-done.refs_3_ = bf16[64,2560]{1,0:T(8,128)(2,1)S(1)} collective-permute-done((bf16[64,2560]{1,0:T(8,128)(2,1)}, bf16[64,2560]{1,0:T(8,128)(2,1)S(1)}, u32[]{:S(2)}, u32[]{:S(2)}) %collective-permute-start) | collective-permute-done | bytes 327712 | tf_op jit(solution)/shard_map/ppermute | solution.py:47
  20.3 1.6 %collective-permute-start.5 = (bf16[2,64,2560]{2,1,0:T(8,128)(2,1)S(1)}, bf16[2,64,2560]{2,1,0:T(8,128)(2,1)S(1)}, u32[]{:S(2)}, u32[]{:S(2)}) collective-permute-start(bf16[2,64,2560]{2,1,0:T(8,128)(2,1)S(1)} %pad_maximum_fusion.2), channel_id=1, source_target_pairs={{0,2},{2,0},{1,3},{3,1},{4,6},{6,4},{5,7},{7,5},{8,10},{10,8},{9,1... | collective-permute-start | bytes 1966088 | tf_op jit(solution)/shard_map/ppermute | solution.py:47
  21.9 1.3 collective-permute-start.6
  23.2 2.4 %collective-permute-start.4 = (bf16[64,2560]{1,0:T(8,128)(2,1)S(1)}, bf16[64,2560]{1,0:T(8,128)(2,1)S(1)}, u32[]{:S(2)}, u32[]{:S(2)}) collective-permute-start(bf16[64,2560]{1,0:T(8,128)(2,1)S(1)} %collective-permute-done.refs_3_), channel_id=1, source_target_pairs={{0,8},{8,0},{16,24},{24,16},{1,9},{9,1},{17,25},{25,17},{2,10},{10... | collective-permute-start | bytes 983048 | tf_op jit(solution)/shard_map/ppermute | solution.py:47
  25.7 13.7 %collective-permute-done.4.refs_1_ = bf16[64,2560]{1,0:T(8,128)(2,1)S(1)} collective-permute-done((bf16[64,2560]{1,0:T(8,128)(2,1)S(1)}, bf16[64,2560]{1,0:T(8,128)(2,1)S(1)}, u32[]{:S(2)}, u32[]{:S(2)}) %collective-permute-start.4) | collective-permute-done | bytes 327712 | tf_op jit(solution)/shard_map/ppermute | solution.py:47
  39.4 3.8 %collective-permute-done.6.refs_1_ = bf16[800,256]{1,0:T(8,128)(2,1)S(1)} collective-permute-done((bf16[800,256]{1,0:T(8,128)(2,1)S(1)}, bf16[800,256]{1,0:T(8,128)(2,1)S(1)}, u32[]{:S(2)}, u32[]{:S(2)}) %collective-permute-start.6) | collective-permute-done | bytes 409632 | tf_op jit(solution)/shard_map/ppermute | solution.py:47
  43.3 1.6 %collective-permute-start.12 = (bf16[400,1024]{1,0:T(8,128)(2,1)S(1)}, bf16[400,1024]{1,0:T(8,128)(2,1)S(1)}, u32[]{:S(2)}, u32[]{:S(2)}) collective-permute-start(bf16[400,1024]{1,0:T(8,128)(2,1)S(1)} %get-tuple-element.81.own_b), channel_id=1, source_target_pairs={{0,4},{4,0},{1,5},{5,1},{2,6},{6,2},{3,7},{7,3},{8,12},{12,8},{9,1... | collective-permute-start | bytes 2457608 | tf_op jit(solution)/shard_map/ppermute | solution.py:47
  45.4 2.2 %collective-permute-start.10 = (bf16[800,256]{1,0:T(8,128)(2,1)S(1)}, bf16[800,256]{1,0:T(8,128)(2,1)S(1)}, u32[]{:S(2)}, u32[]{:S(2)}) collective-permute-start(bf16[800,256]{1,0:T(8,128)(2,1)S(1)} %get-tuple-element.79), channel_id=1, source_target_pairs={{0,24},{8,16},{16,8},{24,0},{1,25},{9,17},{17,9},{25,1},{2,26},{10... | collective-permute-start | bytes 1228808 | tf_op jit(solution)/shard_map/ppermute | solution.py:47
  47.6 16.4 %collective-permute-done.12.other_b = bf16[400,1024]{1,0:T(8,128)(2,1)S(1)} collective-permute-done((bf16[400,1024]{1,0:T(8,128)(2,1)S(1)}, bf16[400,1024]{1,0:T(8,128)(2,1)S(1)}, u32[]{:S(2)}, u32[]{:S(2)}) %collective-permute-start.12) | collective-permute-done | bytes 819232 | tf_op jit(solution)/shard_map/ppermute | solution.py:47
  64.0 0.8 shard_map.86
  64.8 0.7 shard_map.87
  65.5 1.2 fusion.24
  66.8 0.5 collective-permute-done.11.refs_3_
  67.4 1.1 shard_map.88
  69.0 3.1 %convolution_convert_fusion.1 = bf16[512,2560]{1,0:T(8,128)(2,1)S(1)} fusion(bf16[512,800]{1,0:T(8,128)(2,1)S(1)} %get-tuple-element.94, bf16[800,2560]{1,0:T(8,128)(2,1)S(1)} %shard_map.86), kind=kOutput, calls=%fused_computation.7 | convolution fusion | flops 2098462720 | bytes 7536640 | tf_op jit(solution)/shard_map/dot_general | solution.py:174
  72.1 0.7 shard_map.89
  73.0 0.6 collective-permute-start.18
  73.6 1.2 fusion.32
  74.8 1.2 fusion.3
  76.0 3.1 %convolution_convert_fusion = bf16[512,2560]{1,0:T(8,128)(2,1)S(1)} fusion(bf16[512,800]{1,0:T(8,128)(2,1)S(1)} %get-tuple-element.101, bf16[800,2560]{1,0:T(8,128)(2,1)S(1)} %shard_map.86), kind=kOutput, calls=%fused_computation.6 | convolution fusion | flops 2098462720 | bytes 7536640 | tf_op jit(solution)/shard_map/dot_general | solution.py:174
  79.1 0.7 convert_add_fusion
  80.3 1.6 %collective-permute-start.17 = (bf16[2,64,2560]{2,1,0:T(8,128)(2,1)S(1)}, bf16[2,64,2560]{2,1,0:T(8,128)(2,1)S(1)}, u32[]{:S(2)}, u32[]{:S(2)}) collective-permute-start(bf16[2,64,2560]{2,1,0:T(8,128)(2,1)S(1)} %get-tuple-element.125), channel_id=1, source_target_pairs={{0,2},{2,0},{1,3},{3,1},{4,6},{6,4},{5,7},{7,5},{8,10},{10,8},{9,1... | collective-permute-start | bytes 1966088 | tf_op jit(solution)/shard_map/ppermute | solution.py:47
  81.9 1.3 fusion.15
  83.1 2.2 %collective-permute-start.20 = (bf16[800,256]{1,0:T(8,128)(2,1)S(1)}, bf16[800,256]{1,0:T(8,128)(2,1)S(1)}, u32[]{:S(2)}, u32[]{:S(2)}) collective-permute-start(bf16[800,256]{1,0:T(8,128)(2,1)S(1)} %fusion.15), channel_id=1, source_target_pairs={{0,24},{8,16},{16,8},{24,0},{1,25},{9,17},{17,9},{25,1},{2,26},{10... | collective-permute-start | bytes 1228808 | tf_op jit(solution)/shard_map/ppermute | solution.py:47
  85.4 1.3 fusion.21
  86.6 0.8 collective-permute-start.22
  87.5 0.5 collective-permute-start.23
  88.0 9.1 %collective-permute-done.17 = bf16[2,64,2560]{2,1,0:T(8,128)(2,1)S(1)} collective-permute-done((bf16[2,64,2560]{2,1,0:T(8,128)(2,1)S(1)}, bf16[2,64,2560]{2,1,0:T(8,128)(2,1)S(1)}, u32[]{:S(2)}, u32[]{:S(2)}) %collective-permute-start.17) | collective-permute-done | bytes 655392 | tf_op jit(solution)/shard_map/ppermute | solution.py:47
  97.1 1.5 %collective-permute-start.16 = (bf16[2,64,2560]{2,1,0:T(8,128)(2,1)S(1)}, bf16[2,64,2560]{2,1,0:T(8,128)(2,1)S(1)}, u32[]{:S(2)}, u32[]{:S(2)}) collective-permute-start(bf16[2,64,2560]{2,1,0:T(8,128)(2,1)S(1)} %get-tuple-element.124), channel_id=1, source_target_pairs={{0,2},{2,0},{1,3},{3,1},{4,6},{6,4},{5,7},{7,5},{8,10},{10,8},{9,1... | collective-permute-start | bytes 1966088 | tf_op jit(solution)/shard_map/ppermute | solution.py:47
  98.7 4.4 %collective-permute-done.18.refs_2_ = bf16[800,256]{1,0:T(8,128)(2,1)S(1)} collective-permute-done((bf16[800,256]{1,0:T(8,128)(2,1)S(1)}, bf16[800,256]{1,0:T(8,128)(2,1)S(1)}, u32[]{:S(2)}, u32[]{:S(2)}) %collective-permute-start.18) | collective-permute-done | bytes 409632 | tf_op jit(solution)/shard_map/ppermute | solution.py:47
  103.1 1.2 fusion.33
  104.3 8.6 %collective-permute-done.16 = bf16[2,64,2560]{2,1,0:T(8,128)(2,1)S(1)} collective-permute-done((bf16[2,64,2560]{2,1,0:T(8,128)(2,1)S(1)}, bf16[2,64,2560]{2,1,0:T(8,128)(2,1)S(1)}, u32[]{:S(2)}, u32[]{:S(2)}) %collective-permute-start.16) | collective-permute-done | bytes 655392 | tf_op jit(solution)/shard_map/ppermute | solution.py:47
  112.9 1.3 fusion.18.refs_0_
  114.4 11.4 %collective-permute-done.19 = bf16[2,64,2560]{2,1,0:T(8,128)(2,1)S(1)} collective-permute-done((bf16[2,64,2560]{2,1,0:T(8,128)(2,1)S(1)}, bf16[2,64,2560]{2,1,0:T(8,128)(2,1)S(1)}, u32[]{:S(2)}, u32[]{:S(2)}) %collective-permute-start.19) | collective-permute-done | bytes 655392 | tf_op jit(solution)/shard_map/ppermute | solution.py:47
  126.1 5.7 %shard_map.90 = (bf16[256,3200]{1,0:T(8,128)(2,1)}, bf16[256,3200]{1,0:T(8,128)(2,1)}) custom-call(s32[4]{0:T(128)S(1)} %pad_add_fusion.place, bf16[256,3200]{1,0:T(8,128)(2,1)S(1)} %copy-done, bf16[256,3200]{1,0:T(8,128)(2,1)S(1)} %copy-done.2, bf16[800,256]{1,0:T(8,128)(2,1)S(1)} %fusion.18.refs_0_, bf16[800,256]{1,0:T(8,128)(2,1)S(1)} %collective-permute-done.22.refs_1_, ...), custom_call_target="tpu_custom_call" | custom-call | flops 19660800 | bytes 8192000 | tf_op jit(solution)/shard_map/pallas_call | solution.py:52
  131.8 1.4 collective-permute-done.23
  133.2 3.3 %fusion.2 = f32[400,2560]{1,0:T(8,128)} fusion(f32[400,2560]{1,0:T(8,128)S(1)} %fusion.33, bf16[400,512]{1,0:T(8,128)(2,1)S(1)} %get-tuple-element.119, bf16[512,2560]{1,0:T(8,128)(2,1)S(1)} %shard_map.87, bf16[400,2560]{1,0:T(8,128)(2,1)S(1)} %collective-permute-done.23), kind=kOutput, calls=%fused_computation.5 | convolution fusion | flops 1052672000 | bytes 13271040 | tf_op jit(solution)/shard_map/dot_general | solution.py:174
  136.5 6.2 %collective-permute-done.21 = bf16[64,2560]{1,0:T(8,128)(2,1)S(1)} collective-permute-done((bf16[64,2560]{1,0:T(8,128)(2,1)S(1)}, bf16[64,2560]{1,0:T(8,128)(2,1)S(1)}, u32[]{:S(2)}, u32[]{:S(2)}) %collective-permute-start.21) | collective-permute-done | bytes 327712 | tf_op jit(solution)/shard_map/ppermute | solution.py:47
  142.7 0.8 fusion.30
  (40 shorter events, 2.9 us)
Async XLA Ops:
  0.6 12.5 %copy-start = (bf16[256,3200]{1,0:T(8,128)(2,1)S(1)}, bf16[256,3200]{1,0:T(8,128)(2,1)}, u32[]{:S(2)}) copy-start(bf16[256,3200]{1,0:T(8,128)(2,1)} %gate.3) | copy-start | bytes 4915204
  0.6 19.2 %collective-permute-start = (bf16[64,2560]{1,0:T(8,128)(2,1)}, bf16[64,2560]{1,0:T(8,128)(2,1)S(1)}, u32[]{:S(2)}, u32[]{:S(2)}) collective-permute-start(bf16[64,2560]{1,0:T(8,128)(2,1)} %refs_0_.1), channel_id=1, source_target_pairs={{0,16},{8,24},{16,0},{24,8},{1,17},{9,25},{17,1},{25,9},{2,18},{10... | collective-permute-start | bytes 983048 | tf_op jit(solution)/shard_map/ppermute | solution.py:47
  4.7 15.2 %collective-permute-start.1 = (bf16[64,2560]{1,0:T(8,128)(2,1)}, bf16[64,2560]{1,0:T(8,128)(2,1)S(1)}, u32[]{:S(2)}, u32[]{:S(2)}) collective-permute-start(bf16[64,2560]{1,0:T(8,128)(2,1)} %refs_0_.1), channel_id=1, source_target_pairs={{0,8},{8,0},{16,24},{24,16},{1,9},{9,1},{17,25},{25,17},{2,10},{10... | collective-permute-start | bytes 983048 | tf_op jit(solution)/shard_map/ppermute | solution.py:47
  6.3 13.7 %collective-permute-start.2 = (bf16[64,2560]{1,0:T(8,128)(2,1)}, bf16[64,2560]{1,0:T(8,128)(2,1)S(1)}, u32[]{:S(2)}, u32[]{:S(2)}) collective-permute-start(bf16[64,2560]{1,0:T(8,128)(2,1)} %refs_0_.1), channel_id=1, source_target_pairs={{0,2},{2,0},{1,3},{3,1},{4,6},{6,4},{5,7},{7,5},{8,10},{10,8},{9,1... | collective-permute-start | bytes 983048 | tf_op jit(solution)/shard_map/ppermute | solution.py:47
  7.8 12.1 %collective-permute-start.3 = (bf16[64,2560]{1,0:T(8,128)(2,1)}, bf16[64,2560]{1,0:T(8,128)(2,1)S(1)}, u32[]{:S(2)}, u32[]{:S(2)}) collective-permute-start(bf16[64,2560]{1,0:T(8,128)(2,1)} %refs_0_.1), channel_id=1, source_target_pairs={{0,1},{1,0},{2,3},{3,2},{4,5},{5,4},{6,7},{7,6},{8,9},{9,8},{10,11... | collective-permute-start | bytes 983048 | tf_op jit(solution)/shard_map/ppermute | solution.py:47
  8.8 1.6 %copy-start.3 = (bf16[400,2560]{1,0:T(8,128)(2,1)S(1)}, bf16[400,2560]{1,0:T(8,128)(2,1)}, u32[]{:S(2)}) copy-start(bf16[400,2560]{1,0:T(8,128)(2,1)} %codes.1) | copy-start | bytes 6144004
  11.5 31.6 %collective-permute-start.7 = (bf16[400,1536]{1,0:T(8,128)(2,1)S(1)}, bf16[400,1536]{1,0:T(8,128)(2,1)S(1)}, u32[]{:S(2)}, u32[]{:S(2)}) collective-permute-start(bf16[400,1536]{1,0:T(8,128)(2,1)S(1)} %get-tuple-element.72.own_a), channel_id=1, source_target_pairs={{0,4},{4,0},{1,5},{5,1},{2,6},{6,2},{3,7},{7,3},{8,12},{12,8},{9,1... | collective-permute-start | bytes 3686408 | tf_op jit(solution)/shard_map/ppermute | solution.py:47
  13.1 1.4 copy-start.1
  20.1 23.1 %collective-permute-start.8 = (bf16[3,64,2560]{2,1,0:T(8,128)(2,1)S(1)}, bf16[3,64,2560]{2,1,0:T(8,128)(2,1)S(1)}, u32[]{:S(2)}, u32[]{:S(2)}) collective-permute-start(bf16[3,64,2560]{2,1,0:T(8,128)(2,1)S(1)} %pad_maximum_fusion), channel_id=1, source_target_pairs={{0,1},{1,0},{2,3},{3,2},{4,5},{5,4},{6,7},{7,6},{8,9},{9,8},{10,11... | collective-permute-start | bytes 2949128 | tf_op jit(solution)/shard_map/ppermute | solution.py:47
  20.3 22.9 %collective-permute-start.5 = (bf16[2,64,2560]{2,1,0:T(8,128)(2,1)S(1)}, bf16[2,64,2560]{2,1,0:T(8,128)(2,1)S(1)}, u32[]{:S(2)}, u32[]{:S(2)}) collective-permute-start(bf16[2,64,2560]{2,1,0:T(8,128)(2,1)S(1)} %pad_maximum_fusion.2), channel_id=1, source_target_pairs={{0,2},{2,0},{1,3},{3,1},{4,6},{6,4},{5,7},{7,5},{8,10},{10,8},{9,1... | collective-permute-start | bytes 1966088 | tf_op jit(solution)/shard_map/ppermute | solution.py:47
  21.9 21.3 %collective-permute-start.6 = (bf16[800,256]{1,0:T(8,128)(2,1)S(1)}, bf16[800,256]{1,0:T(8,128)(2,1)S(1)}, u32[]{:S(2)}, u32[]{:S(2)}) collective-permute-start(bf16[800,256]{1,0:T(8,128)(2,1)S(1)} %get-tuple-element.71), channel_id=1, source_target_pairs={{0,16},{8,24},{16,0},{24,8},{1,17},{9,25},{17,1},{25,9},{2,18},{10... | collective-permute-start | bytes 1228808 | tf_op jit(solution)/shard_map/ppermute | solution.py:47
  23.2 16.2 %collective-permute-start.4 = (bf16[64,2560]{1,0:T(8,128)(2,1)S(1)}, bf16[64,2560]{1,0:T(8,128)(2,1)S(1)}, u32[]{:S(2)}, u32[]{:S(2)}) collective-permute-start(bf16[64,2560]{1,0:T(8,128)(2,1)S(1)} %collective-permute-done.refs_3_), channel_id=1, source_target_pairs={{0,8},{8,0},{16,24},{24,16},{1,9},{9,1},{17,25},{25,17},{2,10},{10... | collective-permute-start | bytes 983048 | tf_op jit(solution)/shard_map/ppermute | solution.py:47
  43.3 21.6 %collective-permute-start.13 = (bf16[3,64,2560]{2,1,0:T(8,128)(2,1)S(1)}, bf16[3,64,2560]{2,1,0:T(8,128)(2,1)S(1)}, u32[]{:S(2)}, u32[]{:S(2)}) collective-permute-start(bf16[3,64,2560]{2,1,0:T(8,128)(2,1)S(1)} %pad_maximum_fusion.1), channel_id=1, source_target_pairs={{0,1},{1,0},{2,3},{3,2},{4,5},{5,4},{6,7},{7,6},{8,9},{9,8},{10,11... | collective-permute-start | bytes 2949128 | tf_op jit(solution)/shard_map/ppermute | solution.py:47
  43.3 21.5 %copy-start.4 = (bf16[64,2560]{1,0:T(8,128)(2,1)S(1)}, bf16[64,2560]{1,0:T(8,128)(2,1)}, u32[]{:S(2)}) copy-start(bf16[64,2560]{1,0:T(8,128)(2,1)} %refs_0_.1) | copy-start | bytes 983044
  43.3 20.6 %collective-permute-start.12 = (bf16[400,1024]{1,0:T(8,128)(2,1)S(1)}, bf16[400,1024]{1,0:T(8,128)(2,1)S(1)}, u32[]{:S(2)}, u32[]{:S(2)}) collective-permute-start(bf16[400,1024]{1,0:T(8,128)(2,1)S(1)} %get-tuple-element.81.own_b), channel_id=1, source_target_pairs={{0,4},{4,0},{1,5},{5,1},{2,6},{6,2},{3,7},{7,3},{8,12},{12,8},{9,1... | collective-permute-start | bytes 2457608 | tf_op jit(solution)/shard_map/ppermute | solution.py:47
  44.9 21.9 %collective-permute-start.9 = (bf16[64,2560]{1,0:T(8,128)(2,1)S(1)}, bf16[64,2560]{1,0:T(8,128)(2,1)S(1)}, u32[]{:S(2)}, u32[]{:S(2)}) collective-permute-start(bf16[64,2560]{1,0:T(8,128)(2,1)S(1)} %collective-permute-done.4.refs_1_), channel_id=1, source_target_pairs={{0,2},{2,0},{1,3},{3,1},{4,6},{6,4},{5,7},{7,5},{8,10},{10,8},{9,1... | collective-permute-start | bytes 983048 | tf_op jit(solution)/shard_map/ppermute | solution.py:47
  45.4 21.4 %collective-permute-start.10 = (bf16[800,256]{1,0:T(8,128)(2,1)S(1)}, bf16[800,256]{1,0:T(8,128)(2,1)S(1)}, u32[]{:S(2)}, u32[]{:S(2)}) collective-permute-start(bf16[800,256]{1,0:T(8,128)(2,1)S(1)} %get-tuple-element.79), channel_id=1, source_target_pairs={{0,24},{8,16},{16,8},{24,0},{1,25},{9,17},{17,9},{25,1},{2,26},{10... | collective-permute-start | bytes 1228808 | tf_op jit(solution)/shard_map/ppermute | solution.py:47
  47.6 19.7 %collective-permute-start.11 = (bf16[800,256]{1,0:T(8,128)(2,1)S(1)}, bf16[800,256]{1,0:T(8,128)(2,1)S(1)}, u32[]{:S(2)}, u32[]{:S(2)}) collective-permute-start(bf16[800,256]{1,0:T(8,128)(2,1)S(1)} %get-tuple-element.80), channel_id=1, source_target_pairs={{0,8},{8,0},{16,24},{24,16},{1,9},{9,1},{17,25},{25,17},{2,10},{10... | collective-permute-start | bytes 1228808 | tf_op jit(solution)/shard_map/ppermute | solution.py:47
  67.3 1.6 %collective-permute-start.14 = (bf16[64,2560]{1,0:T(8,128)(2,1)S(1)}, bf16[64,2560]{1,0:T(8,128)(2,1)S(1)}, u32[]{:S(2)}, u32[]{:S(2)}) collective-permute-start(bf16[64,2560]{1,0:T(8,128)(2,1)S(1)} %collective-permute-done.9.refs_2_), channel_id=1, source_target_pairs={{0,1},{1,0},{2,3},{3,2},{4,5},{5,4},{6,7},{7,6},{8,9},{9,8},{10,11... | collective-permute-start | bytes 983048 | tf_op jit(solution)/shard_map/ppermute | solution.py:47
  72.8 6.4 %collective-permute-start.15 = (bf16[512,2560]{1,0:T(8,128)(2,1)S(1)}, bf16[512,2560]{1,0:T(8,128)(2,1)S(1)}, u32[]{:S(2)}, u32[]{:S(2)}) collective-permute-start(bf16[512,2560]{1,0:T(8,128)(2,1)S(1)} %convolution_convert_fusion.1), channel_id=1, source_target_pairs={{0,1},{1,0},{2,3},{3,2},{4,5},{5,4},{6,7},{7,6},{8,9},{9,8},{10,11... | collective-permute-start | bytes 7864328 | tf_op jit(solution)/shard_map/ppermute | solution.py:47
  73.0 30.1 %collective-permute-start.18 = (bf16[800,256]{1,0:T(8,128)(2,1)S(1)}, bf16[800,256]{1,0:T(8,128)(2,1)S(1)}, u32[]{:S(2)}, u32[]{:S(2)}) collective-permute-start(bf16[800,256]{1,0:T(8,128)(2,1)S(1)} %fusion.24), channel_id=1, source_target_pairs={{0,16},{8,24},{16,0},{24,8},{1,17},{9,25},{17,1},{25,9},{2,18},{10... | collective-permute-start | bytes 1228808 | tf_op jit(solution)/shard_map/ppermute | solution.py:47
  80.3 16.8 %collective-permute-start.17 = (bf16[2,64,2560]{2,1,0:T(8,128)(2,1)S(1)}, bf16[2,64,2560]{2,1,0:T(8,128)(2,1)S(1)}, u32[]{:S(2)}, u32[]{:S(2)}) collective-permute-start(bf16[2,64,2560]{2,1,0:T(8,128)(2,1)S(1)} %get-tuple-element.125), channel_id=1, source_target_pairs={{0,2},{2,0},{1,3},{3,1},{4,6},{6,4},{5,7},{7,5},{8,10},{10,8},{9,1... | collective-permute-start | bytes 1966088 | tf_op jit(solution)/shard_map/ppermute | solution.py:47
  83.1 42.9 %collective-permute-start.20 = (bf16[800,256]{1,0:T(8,128)(2,1)S(1)}, bf16[800,256]{1,0:T(8,128)(2,1)S(1)}, u32[]{:S(2)}, u32[]{:S(2)}) collective-permute-start(bf16[800,256]{1,0:T(8,128)(2,1)S(1)} %fusion.15), channel_id=1, source_target_pairs={{0,24},{8,16},{16,8},{24,0},{1,25},{9,17},{17,9},{25,1},{2,26},{10... | collective-permute-start | bytes 1228808 | tf_op jit(solution)/shard_map/ppermute | solution.py:47
  86.6 39.5 %collective-permute-start.22 = (bf16[800,256]{1,0:T(8,128)(2,1)S(1)}, bf16[800,256]{1,0:T(8,128)(2,1)S(1)}, u32[]{:S(2)}, u32[]{:S(2)}) collective-permute-start(bf16[800,256]{1,0:T(8,128)(2,1)S(1)} %fusion.21), channel_id=1, source_target_pairs={{0,8},{8,0},{16,24},{24,16},{1,9},{9,1},{17,25},{25,17},{2,10},{10... | collective-permute-start | bytes 1228808 | tf_op jit(solution)/shard_map/ppermute | solution.py:47
  87.5 45.7 %collective-permute-start.23 = (bf16[400,2560]{1,0:T(8,128)(2,1)S(1)}, bf16[400,2560]{1,0:T(8,128)(2,1)S(1)}, u32[]{:S(2)}, u32[]{:S(2)}) collective-permute-start(bf16[400,2560]{1,0:T(8,128)(2,1)S(1)} %fusion.3), channel_id=1, source_target_pairs={{0,4},{4,0},{1,5},{5,1},{2,6},{6,2},{3,7},{7,3},{8,12},{12,8},{9,1... | collective-permute-start | bytes 6144008 | tf_op jit(solution)/shard_map/ppermute | solution.py:47
  97.1 15.9 %collective-permute-start.16 = (bf16[2,64,2560]{2,1,0:T(8,128)(2,1)S(1)}, bf16[2,64,2560]{2,1,0:T(8,128)(2,1)S(1)}, u32[]{:S(2)}, u32[]{:S(2)}) collective-permute-start(bf16[2,64,2560]{2,1,0:T(8,128)(2,1)S(1)} %get-tuple-element.124), channel_id=1, source_target_pairs={{0,2},{2,0},{1,3},{3,1},{4,6},{6,4},{5,7},{7,5},{8,10},{10,8},{9,1... | collective-permute-start | bytes 1966088 | tf_op jit(solution)/shard_map/ppermute | solution.py:47
  103.1 22.7 %collective-permute-start.19 = (bf16[2,64,2560]{2,1,0:T(8,128)(2,1)S(1)}, bf16[2,64,2560]{2,1,0:T(8,128)(2,1)S(1)}, u32[]{:S(2)}, u32[]{:S(2)}) collective-permute-start(bf16[2,64,2560]{2,1,0:T(8,128)(2,1)S(1)} %fusion.5), channel_id=1, source_target_pairs={{0,8},{8,0},{16,24},{24,16},{1,9},{9,1},{17,25},{25,17},{2,10},{10... | collective-permute-start | bytes 1966088 | tf_op jit(solution)/shard_map/ppermute | solution.py:47
  114.2 11.9 %copy-start.2 = (bf16[256,3200]{1,0:T(8,128)(2,1)S(1)}, bf16[256,3200]{1,0:T(8,128)(2,1)}, u32[]{:S(2)}) copy-start(bf16[256,3200]{1,0:T(8,128)(2,1)} %up.3) | copy-start | bytes 4915204
  126.0 16.6 %collective-permute-start.21 = (bf16[64,2560]{1,0:T(8,128)(2,1)S(1)}, bf16[64,2560]{1,0:T(8,128)(2,1)S(1)}, u32[]{:S(2)}, u32[]{:S(2)}) collective-permute-start(bf16[64,2560]{1,0:T(8,128)(2,1)S(1)} %fusion.31), channel_id=1, source_target_pairs={{0,16},{8,24},{16,0},{24,8},{1,17},{9,25},{17,1},{25,9},{2,18},{10... | collective-permute-start | bytes 983048 | tf_op jit(solution)/shard_map/ppermute | solution.py:47

commit v7 on v6

--- a/solution.py
+++ b/solution.py
@@ -248,6 +248,7 @@
     far_back = matmul(weight, even[group_rows:], 1, 1, bf16)
     last_y, columns, far_back, even = barrier((last_y, columns, far_back, even))
     last_c = exchange(last_y, "c", 1)
+
     by_rows, by_lanes = (1, 3, 0, 2), (0, 2, 1, 3)
     keep, send, *by_units = call_kernel(
         functools.partial(columns_kernel, parts, by_rows, by_lanes), place, columns, piece_specs,
@@ -256,14 +257,15 @@
         (0, 12 * units * half_tokens, 0),
     )
 
-    send, keep, last_c = barrier((send, keep, last_c))
     odd = gather_tokens(
         (near, last, last_y, other_y, first_c, other_c, last_c),
         ((0, 0), (3, 1), (4, 2), (5, 1), (1, 0), (2, 0), (5, 2), (6, 0)),
     )
+    even, odd, send, keep = barrier((even, odd, send, keep))
     flat = [even, odd]
 
     factor = float(total_tokens) ** (-0.5)
+
 
     def grad_half(r):
         return (matmul(by_units[r], flat[0]) + matmul(by_units[2 + r], flat[1])) * factor
@@ -272,20 +274,16 @@
         rows_of_k = flat[k % 2][k // 2 * group_rows : (k // 2 + 1) * group_rows]
         return matmul(weight, rows_of_k, 1, 1, bf16)
 
-    given = matmul(send, weight, dtype=bf16)
-    given, flat = barrier((given, flat))
-    over_c = exchange(given, "c", 1)
+    over_c = exchange(matmul(send, weight, dtype=bf16), "c", 1)
     theirs = grad_half(1).astype(bf16)
     theirs, keep, flat = barrier((theirs, keep, flat))
     over_x = exchange(theirs, "x", 1)
     kept = matmul(keep, weight, dtype=bf16)
-    back = [None, back_of(1), far_back, back_of(3)]
-    back = [None] + [exchange(back[k], "z", k) for k in range(1, nz)]
+    back = [back_of(0), back_of(1), far_back, back_of(3)]
+    back = [back[0]] + [exchange(back[k], "z", k) for k in range(1, nz)]
     sums = (kept.astype(f32) + over_c.astype(f32)).reshape(2, nz, rows, width)
     odd_y = exchange(sums[1, :2].astype(bf16), "y", 1)
     even_y = exchange(sums[1, 2:].astype(bf16), "y", 1)
-    odd_y, flat = barrier((odd_y, flat))
-    back[0] = back_of(0)
     odd_sum = (sums[0, :2] + odd_y.astype(f32)).astype(bf16)
     odd_sum, back[2] = barrier((odd_sum, back[2]))
     even_y, _ = barrier((even_y, odd_sum))

time: 144 us -> 140 us (0.972)
  waiting for transfers between devices: 78.5 us -> 73.8 us
  other arithmetic: 2.71 us -> 5.23 us
  matrix products: 18.2 us -> 16.4 us
    ppermute x24, waiting for transfers between devices: 78.5 us -> 73.8 us  [exchange(): return lax.ppermute(value, axis, [(i, i ^ offset) for i in range(size)])]
    add x0 -> x1, other arithmetic: none -> 2.54 us  [paired_body(): weight_grad = grad_half(0) + over_x.astype(f32)]
    dot_general x10, matrix products: 18.2 us -> 16.4 us  [matmul(): lax.dot_general(lhs, rhs, dims, preferred_element_type=jnp.float32)]
  transfers between devices with their start and end apart: 24 -> 24, of which waited for: 13 -> 10; matrix products, arithmetic and copies ran while one was open for 12% -> 15% of each run, Pallas kernels for 9% -> 9%
where the time goes in v7:
time: 140 us
  waiting for transfers between devices  73.8 us (53%)
  starting transfers between devices  26.5 us (19%)
  matrix products  16.4 us (12%)
  Pallas kernels  13 us (9%)
  other arithmetic  5.23 us (4%)
  local copies, waits for them, and re-layouts  4 us (3%)
    ppermute x24, waiting for transfers between devices, exchange(): return lax.ppermute(value, axis, [(i, i ^ offset) for i in range(size)])  73.8 us
    ppermute x24, starting transfers between devices, exchange(): return lax.ppermute(value, axis, [(i, i ^ offset) for i in range(size)])  26.5 us
    dot_general x10, matrix products, matmul(): lax.dot_general(lhs, rhs, dims, preferred_element_type=jnp.float32)  16.4 us
    pallas_call x7, Pallas kernels, call_kernel(): pl.pallas_call(kernel, out_shape=out_shapes, grid_spec=pltpu.PrefetchScal...  13 us
    unnamed x11, local copies, waits for them, and re-layouts  3.91 us
  transfers between devices with their start and end apart: 24, of which 10 were waited for; matrix products, arithmetic and copies ran while one was open for 15% of the time, Pallas kernels for 9%

profile of v7, /device:TPU:0, one launch (start us, length us, event | category | flops | bytes accessed | tf_op | source)
XLA Modules:
  0.0 139.9 jit_solution(11331757796139550113)
XLA Ops:
  0.6 3.0 %collective-permute-start.2 = (bf16[64,2560]{1,0:T(8,128)(2,1)}, bf16[64,2560]{1,0:T(8,128)(2,1)S(1)}, u32[]{:S(2)}, u32[]{:S(2)}) collective-permute-start(bf16[64,2560]{1,0:T(8,128)(2,1)} %refs_0_.1), channel_id=1, source_target_pairs={{0,2},{2,0},{1,3},{3,1},{4,6},{6,4},{5,7},{7,5},{8,10},{10,8},{9,1... | collective-permute-start | bytes 983048 | tf_op jit(solution)/shard_map/ppermute | solution.py:47
  3.7 1.6 %collective-permute-start.1 = (bf16[64,2560]{1,0:T(8,128)(2,1)}, bf16[64,2560]{1,0:T(8,128)(2,1)S(1)}, u32[]{:S(2)}, u32[]{:S(2)}) collective-permute-start(bf16[64,2560]{1,0:T(8,128)(2,1)} %refs_0_.1), channel_id=1, source_target_pairs={{0,8},{8,0},{16,24},{24,16},{1,9},{9,1},{17,25},{25,17},{2,10},{10... | collective-permute-start | bytes 983048 | tf_op jit(solution)/shard_map/ppermute | solution.py:47
  5.2 2.6 %collective-permute-start = (bf16[64,2560]{1,0:T(8,128)(2,1)}, bf16[64,2560]{1,0:T(8,128)(2,1)S(1)}, u32[]{:S(2)}, u32[]{:S(2)}) collective-permute-start(bf16[64,2560]{1,0:T(8,128)(2,1)} %refs_0_.1), channel_id=1, source_target_pairs={{0,16},{8,24},{16,0},{24,8},{1,17},{9,25},{17,1},{25,9},{2,18},{10... | collective-permute-start | bytes 983048 | tf_op jit(solution)/shard_map/ppermute | solution.py:47
  7.8 0.9 copy.9.scales
  8.8 1.6 %copy-done.3 = bf16[400,2560]{1,0:T(8,128)(2,1)S(1)} copy-done((bf16[400,2560]{1,0:T(8,128)(2,1)S(1)}, bf16[400,2560]{1,0:T(8,128)(2,1)}, u32[]{:S(2)}) %copy-start.3) | copy-done | bytes 2048024
  10.4 1.1 shard_map.85
  11.5 1.6 %collective-permute-start.7 = (bf16[400,1536]{1,0:T(8,128)(2,1)S(1)}, bf16[400,1536]{1,0:T(8,128)(2,1)S(1)}, u32[]{:S(2)}, u32[]{:S(2)}) collective-permute-start(bf16[400,1536]{1,0:T(8,128)(2,1)S(1)} %get-tuple-element.67.own_a), channel_id=1, source_target_pairs={{0,4},{4,0},{1,5},{5,1},{2,6},{6,2},{3,7},{7,3},{8,12},{12,8},{9,1... | collective-permute-start | bytes 3686408 | tf_op jit(solution)/shard_map/ppermute | solution.py:47
  13.1 1.4 %copy-done.1 = bf16[256,3200]{1,0:T(8,128)(2,1)S(1)} copy-done((bf16[256,3200]{1,0:T(8,128)(2,1)S(1)}, bf16[256,3200]{1,0:T(8,128)(2,1)}, u32[]{:S(2)}) %copy-start.1) | copy-done | bytes 1638424
  14.5 2.8 %shard_map.84 = (bf16[800,256]{1,0:T(8,128)(2,1)S(1)}, bf16[800,256]{1,0:T(8,128)(2,1)S(1)}, bf16[800,256]{1,0:T(8,128)(2,1)S(1)}, bf16[800,256]{1,0:T(8,128)(2,1)S(1)}) custom-call(s32[4]{0:T(128)S(1)} %pad_add_fusion.place, bf16[256,3200]{1,0:T(8,128)(2,1)S(1)} %copy-done, bf16[256,3200]{1,0:T(8,128)(2,1)S(1)} %copy-done.1), custom_call_target="tpu_custom_call" | custom-call | flops 6553600 | bytes 4915200 | tf_op jit(solution)/shard_map/pallas_call | solution.py:52
  17.4 2.5 %collective-permute-done.1.refs_0_ = bf16[64,2560]{1,0:T(8,128)(2,1)S(1)} collective-permute-done((bf16[64,2560]{1,0:T(8,128)(2,1)}, bf16[64,2560]{1,0:T(8,128)(2,1)S(1)}, u32[]{:S(2)}, u32[]{:S(2)}) %collective-permute-start.1) | collective-permute-done | bytes 327712 | tf_op jit(solution)/shard_map/ppermute | solution.py:47
  19.9 2.4 %collective-permute-done.refs_3_ = bf16[64,2560]{1,0:T(8,128)(2,1)S(1)} collective-permute-done((bf16[64,2560]{1,0:T(8,128)(2,1)}, bf16[64,2560]{1,0:T(8,128)(2,1)S(1)}, u32[]{:S(2)}, u32[]{:S(2)}) %collective-permute-start) | collective-permute-done | bytes 327712 | tf_op jit(solution)/shard_map/ppermute | solution.py:47
  23.5 2.7 %collective-permute-start.4 = (bf16[64,2560]{1,0:T(8,128)(2,1)S(1)}, bf16[64,2560]{1,0:T(8,128)(2,1)S(1)}, u32[]{:S(2)}, u32[]{:S(2)}) collective-permute-start(bf16[64,2560]{1,0:T(8,128)(2,1)S(1)} %collective-permute-done.refs_3_), channel_id=1, source_target_pairs={{0,8},{8,0},{16,24},{24,16},{1,9},{9,1},{17,25},{25,17},{2,10},{10... | collective-permute-start | bytes 983048 | tf_op jit(solution)/shard_map/ppermute | solution.py:47
  26.2 13.5 %collective-permute-done.4.refs_1_ = bf16[64,2560]{1,0:T(8,128)(2,1)S(1)} collective-permute-done((bf16[64,2560]{1,0:T(8,128)(2,1)S(1)}, bf16[64,2560]{1,0:T(8,128)(2,1)S(1)}, u32[]{:S(2)}, u32[]{:S(2)}) %collective-permute-start.4) | collective-permute-done | bytes 327712 | tf_op jit(solution)/shard_map/ppermute | solution.py:47
  39.7 4.6 %collective-permute-done.6.refs_1_ = bf16[800,256]{1,0:T(8,128)(2,1)S(1)} collective-permute-done((bf16[800,256]{1,0:T(8,128)(2,1)S(1)}, bf16[800,256]{1,0:T(8,128)(2,1)S(1)}, u32[]{:S(2)}, u32[]{:S(2)}) %collective-permute-start.6) | collective-permute-done | bytes 409632 | tf_op jit(solution)/shard_map/ppermute | solution.py:47
  44.5 1.5 %collective-permute-start.12 = (bf16[400,1024]{1,0:T(8,128)(2,1)S(1)}, bf16[400,1024]{1,0:T(8,128)(2,1)S(1)}, u32[]{:S(2)}, u32[]{:S(2)}) collective-permute-start(bf16[400,1024]{1,0:T(8,128)(2,1)S(1)} %get-tuple-element.76.own_b), channel_id=1, source_target_pairs={{0,4},{4,0},{1,5},{5,1},{2,6},{6,2},{3,7},{7,3},{8,12},{12,8},{9,1... | collective-permute-start | bytes 2457608 | tf_op jit(solution)/shard_map/ppermute | solution.py:47
  46.1 1.5 %collective-permute-start.9 = (bf16[64,2560]{1,0:T(8,128)(2,1)S(1)}, bf16[64,2560]{1,0:T(8,128)(2,1)S(1)}, u32[]{:S(2)}, u32[]{:S(2)}) collective-permute-start(bf16[64,2560]{1,0:T(8,128)(2,1)S(1)} %collective-permute-done.4.refs_1_), channel_id=1, source_target_pairs={{0,2},{2,0},{1,3},{3,1},{4,6},{6,4},{5,7},{7,5},{8,10},{10,8},{9,1... | collective-permute-start | bytes 983048 | tf_op jit(solution)/shard_map/ppermute | solution.py:47
  47.6 1.3 collective-permute-start.10
  48.9 16.2 %collective-permute-done.12.other_b = bf16[400,1024]{1,0:T(8,128)(2,1)S(1)} collective-permute-done((bf16[400,1024]{1,0:T(8,128)(2,1)S(1)}, bf16[400,1024]{1,0:T(8,128)(2,1)S(1)}, u32[]{:S(2)}, u32[]{:S(2)}) %collective-permute-start.12) | collective-permute-done | bytes 819232 | tf_op jit(solution)/shard_map/ppermute | solution.py:47
  65.1 0.8 shard_map.86
  66.0 0.7 shard_map.87
  66.7 1.3 fusion.23
  68.7 1.3 collective-permute-start.18
  70.0 1.1 shard_map.88
  71.2 0.7 shard_map.89
  71.9 3.1 %convolution_convert_fusion = bf16[512,2560]{1,0:T(8,128)(2,1)S(1)} fusion(bf16[512,800]{1,0:T(8,128)(2,1)S(1)} %get-tuple-element.95, bf16[800,2560]{1,0:T(8,128)(2,1)S(1)} %shard_map.86), kind=kOutput, calls=%fused_computation.5 | convolution fusion | flops 2098462720 | bytes 7536640 | tf_op jit(solution)/shard_map/dot_general | solution.py:174
  75.3 1.2 fusion.31
  76.5 1.2 fusion.2
  77.8 1.2 fusion.14
  79.0 1.5 %collective-permute-start.20 = (bf16[800,256]{1,0:T(8,128)(2,1)S(1)}, bf16[800,256]{1,0:T(8,128)(2,1)S(1)}, u32[]{:S(2)}, u32[]{:S(2)}) collective-permute-start(bf16[800,256]{1,0:T(8,128)(2,1)S(1)} %fusion.14), channel_id=1, source_target_pairs={{0,24},{8,16},{16,8},{24,0},{1,25},{9,17},{17,9},{25,1},{2,26},{10... | collective-permute-start | bytes 1228808 | tf_op jit(solution)/shard_map/ppermute | solution.py:47
  80.5 1.2 fusion.20
  81.7 0.8 collective-permute-start.22
  82.6 1.2 fusion.17.refs_0_
  83.8 3.3 %convolution_convert_fusion.1 = bf16[512,2560]{1,0:T(8,128)(2,1)S(1)} fusion(bf16[512,800]{1,0:T(8,128)(2,1)S(1)} %get-tuple-element.94, bf16[800,2560]{1,0:T(8,128)(2,1)S(1)} %shard_map.86), kind=kOutput, calls=%fused_computation.6 | convolution fusion | flops 2098462720 | bytes 7536640 | tf_op jit(solution)/shard_map/dot_general | solution.py:174
  87.1 0.7 convert_add_fusion
  88.3 1.0 collective-permute-start.17
  89.3 1.2 fusion.32
  90.5 1.5 %collective-permute-start.23 = (bf16[400,2560]{1,0:T(8,128)(2,1)S(1)}, bf16[400,2560]{1,0:T(8,128)(2,1)S(1)}, u32[]{:S(2)}, u32[]{:S(2)}) collective-permute-start(bf16[400,2560]{1,0:T(8,128)(2,1)S(1)} %fusion.2), channel_id=1, source_target_pairs={{0,4},{4,0},{1,5},{5,1},{2,6},{6,2},{3,7},{7,3},{8,12},{12,8},{9,1... | collective-permute-start | bytes 6144008 | tf_op jit(solution)/shard_map/ppermute | solution.py:47
  92.0 1.3 fusion
  93.3 11.4 %collective-permute-done.17 = bf16[2,64,2560]{2,1,0:T(8,128)(2,1)S(1)} collective-permute-done((bf16[2,64,2560]{2,1,0:T(8,128)(2,1)S(1)}, bf16[2,64,2560]{2,1,0:T(8,128)(2,1)S(1)}, u32[]{:S(2)}, u32[]{:S(2)}) %collective-permute-start.17) | collective-permute-done | bytes 655392 | tf_op jit(solution)/shard_map/ppermute | solution.py:47
  104.7 1.0 collective-permute-start.16
  105.8 0.9 collective-permute-start.19
  106.7 13.5 %collective-permute-done.16 = bf16[2,64,2560]{2,1,0:T(8,128)(2,1)S(1)} collective-permute-done((bf16[2,64,2560]{2,1,0:T(8,128)(2,1)S(1)}, bf16[2,64,2560]{2,1,0:T(8,128)(2,1)S(1)}, u32[]{:S(2)}, u32[]{:S(2)}) %collective-permute-start.16) | collective-permute-done | bytes 655392 | tf_op jit(solution)/shard_map/ppermute | solution.py:47
  120.3 1.3 collective-permute-done.19
  121.9 1.3 collective-permute-start.21
  123.2 5.7 %shard_map.90 = (bf16[256,3200]{1,0:T(8,128)(2,1)}, bf16[256,3200]{1,0:T(8,128)(2,1)}) custom-call(s32[4]{0:T(128)S(1)} %pad_add_fusion.place, bf16[256,3200]{1,0:T(8,128)(2,1)S(1)} %copy-done, bf16[256,3200]{1,0:T(8,128)(2,1)S(1)} %copy-done.2, bf16[800,256]{1,0:T(8,128)(2,1)S(1)} %fusion.17.refs_0_, bf16[800,256]{1,0:T(8,128)(2,1)S(1)} %collective-permute-done.22.refs_1_, ...), custom_call_target="tpu_custom_call" | custom-call | flops 19660800 | bytes 8192000 | tf_op jit(solution)/shard_map/pallas_call | solution.py:52
  128.8 7.7 %collective-permute-done.23 = bf16[400,2560]{1,0:T(8,128)(2,1)S(1)} collective-permute-done((bf16[400,2560]{1,0:T(8,128)(2,1)S(1)}, bf16[400,2560]{1,0:T(8,128)(2,1)S(1)}, u32[]{:S(2)}, u32[]{:S(2)}) %collective-permute-start.23) | collective-permute-done | bytes 2048032 | tf_op jit(solution)/shard_map/ppermute | solution.py:47
  136.5 2.5 %convert_add_fusion.1 = f32[400,2560]{1,0:T(8,128)} fusion(f32[400,2560]{1,0:T(8,128)S(1)} %fusion, bf16[400,2560]{1,0:T(8,128)(2,1)S(1)} %collective-permute-done.23), kind=kLoop, calls=%fused_computation.8 | loop fusion | flops 2048000 | bytes 10240000 | tf_op jit(solution)/shard_map/add | solution.py:304
  139.1 0.8 fusion.29
  (41 shorter events, 3.3 us)
Async XLA Ops:
  0.6 12.5 %copy-start = (bf16[256,3200]{1,0:T(8,128)(2,1)S(1)}, bf16[256,3200]{1,0:T(8,128)(2,1)}, u32[]{:S(2)}) copy-start(bf16[256,3200]{1,0:T(8,128)(2,1)} %gate.3) | copy-start | bytes 4915204
  0.6 16.8 %collective-permute-start.2 = (bf16[64,2560]{1,0:T(8,128)(2,1)}, bf16[64,2560]{1,0:T(8,128)(2,1)S(1)}, u32[]{:S(2)}, u32[]{:S(2)}) collective-permute-start(bf16[64,2560]{1,0:T(8,128)(2,1)} %refs_0_.1), channel_id=1, source_target_pairs={{0,2},{2,0},{1,3},{3,1},{4,6},{6,4},{5,7},{7,5},{8,10},{10,8},{9,1... | collective-permute-start | bytes 983048 | tf_op jit(solution)/shard_map/ppermute | solution.py:47
  3.7 16.3 %collective-permute-start.1 = (bf16[64,2560]{1,0:T(8,128)(2,1)}, bf16[64,2560]{1,0:T(8,128)(2,1)S(1)}, u32[]{:S(2)}, u32[]{:S(2)}) collective-permute-start(bf16[64,2560]{1,0:T(8,128)(2,1)} %refs_0_.1), channel_id=1, source_target_pairs={{0,8},{8,0},{16,24},{24,16},{1,9},{9,1},{17,25},{25,17},{2,10},{10... | collective-permute-start | bytes 983048 | tf_op jit(solution)/shard_map/ppermute | solution.py:47
  5.2 17.1 %collective-permute-start = (bf16[64,2560]{1,0:T(8,128)(2,1)}, bf16[64,2560]{1,0:T(8,128)(2,1)S(1)}, u32[]{:S(2)}, u32[]{:S(2)}) collective-permute-start(bf16[64,2560]{1,0:T(8,128)(2,1)} %refs_0_.1), channel_id=1, source_target_pairs={{0,16},{8,24},{16,0},{24,8},{1,17},{9,25},{17,1},{25,9},{2,18},{10... | collective-permute-start | bytes 983048 | tf_op jit(solution)/shard_map/ppermute | solution.py:47
  7.8 14.5 %collective-permute-start.3 = (bf16[64,2560]{1,0:T(8,128)(2,1)}, bf16[64,2560]{1,0:T(8,128)(2,1)S(1)}, u32[]{:S(2)}, u32[]{:S(2)}) collective-permute-start(bf16[64,2560]{1,0:T(8,128)(2,1)} %refs_0_.1), channel_id=1, source_target_pairs={{0,1},{1,0},{2,3},{3,2},{4,5},{5,4},{6,7},{7,6},{8,9},{9,8},{10,11... | collective-permute-start | bytes 983048 | tf_op jit(solution)/shard_map/ppermute | solution.py:47
  8.8 1.6 %copy-start.3 = (bf16[400,2560]{1,0:T(8,128)(2,1)S(1)}, bf16[400,2560]{1,0:T(8,128)(2,1)}, u32[]{:S(2)}) copy-start(bf16[400,2560]{1,0:T(8,128)(2,1)} %codes.1) | copy-start | bytes 6144004
  11.5 32.8 %collective-permute-start.7 = (bf16[400,1536]{1,0:T(8,128)(2,1)S(1)}, bf16[400,1536]{1,0:T(8,128)(2,1)S(1)}, u32[]{:S(2)}, u32[]{:S(2)}) collective-permute-start(bf16[400,1536]{1,0:T(8,128)(2,1)S(1)} %get-tuple-element.67.own_a), channel_id=1, source_target_pairs={{0,4},{4,0},{1,5},{5,1},{2,6},{6,2},{3,7},{7,3},{8,12},{12,8},{9,1... | collective-permute-start | bytes 3686408 | tf_op jit(solution)/shard_map/ppermute | solution.py:47
  13.1 1.4 %copy-start.1 = (bf16[256,3200]{1,0:T(8,128)(2,1)S(1)}, bf16[256,3200]{1,0:T(8,128)(2,1)}, u32[]{:S(2)}) copy-start(bf16[256,3200]{1,0:T(8,128)(2,1)} %up.3) | copy-start | bytes 4915204
  22.5 21.9 %collective-permute-start.8 = (bf16[3,64,2560]{2,1,0:T(8,128)(2,1)S(1)}, bf16[3,64,2560]{2,1,0:T(8,128)(2,1)S(1)}, u32[]{:S(2)}, u32[]{:S(2)}) collective-permute-start(bf16[3,64,2560]{2,1,0:T(8,128)(2,1)S(1)} %pad_maximum_fusion), channel_id=1, source_target_pairs={{0,1},{1,0},{2,3},{3,2},{4,5},{5,4},{6,7},{7,6},{8,9},{9,8},{10,11... | collective-permute-start | bytes 2949128 | tf_op jit(solution)/shard_map/ppermute | solution.py:47
  22.6 21.7 %collective-permute-start.5 = (bf16[2,64,2560]{2,1,0:T(8,128)(2,1)S(1)}, bf16[2,64,2560]{2,1,0:T(8,128)(2,1)S(1)}, u32[]{:S(2)}, u32[]{:S(2)}) collective-permute-start(bf16[2,64,2560]{2,1,0:T(8,128)(2,1)S(1)} %pad_maximum_fusion.2), channel_id=1, source_target_pairs={{0,2},{2,0},{1,3},{3,1},{4,6},{6,4},{5,7},{7,5},{8,10},{10,8},{9,1... | collective-permute-start | bytes 1966088 | tf_op jit(solution)/shard_map/ppermute | solution.py:47
  23.2 21.1 %collective-permute-start.6 = (bf16[800,256]{1,0:T(8,128)(2,1)S(1)}, bf16[800,256]{1,0:T(8,128)(2,1)S(1)}, u32[]{:S(2)}, u32[]{:S(2)}) collective-permute-start(bf16[800,256]{1,0:T(8,128)(2,1)S(1)} %get-tuple-element.66), channel_id=1, source_target_pairs={{0,16},{8,24},{16,0},{24,8},{1,17},{9,25},{17,1},{25,9},{2,18},{10... | collective-permute-start | bytes 1228808 | tf_op jit(solution)/shard_map/ppermute | solution.py:47
  23.5 16.2 %collective-permute-start.4 = (bf16[64,2560]{1,0:T(8,128)(2,1)S(1)}, bf16[64,2560]{1,0:T(8,128)(2,1)S(1)}, u32[]{:S(2)}, u32[]{:S(2)}) collective-permute-start(bf16[64,2560]{1,0:T(8,128)(2,1)S(1)} %collective-permute-done.refs_3_), channel_id=1, source_target_pairs={{0,8},{8,0},{16,24},{24,16},{1,9},{9,1},{17,25},{25,17},{2,10},{10... | collective-permute-start | bytes 983048 | tf_op jit(solution)/shard_map/ppermute | solution.py:47
  44.4 21.6 %collective-permute-start.13 = (bf16[3,64,2560]{2,1,0:T(8,128)(2,1)S(1)}, bf16[3,64,2560]{2,1,0:T(8,128)(2,1)S(1)}, u32[]{:S(2)}, u32[]{:S(2)}) collective-permute-start(bf16[3,64,2560]{2,1,0:T(8,128)(2,1)S(1)} %pad_maximum_fusion.1), channel_id=1, source_target_pairs={{0,1},{1,0},{2,3},{3,2},{4,5},{5,4},{6,7},{7,6},{8,9},{9,8},{10,11... | collective-permute-start | bytes 2949128 | tf_op jit(solution)/shard_map/ppermute | solution.py:47
  44.5 21.5 %copy-start.4 = (bf16[64,2560]{1,0:T(8,128)(2,1)S(1)}, bf16[64,2560]{1,0:T(8,128)(2,1)}, u32[]{:S(2)}) copy-start(bf16[64,2560]{1,0:T(8,128)(2,1)} %refs_0_.1) | copy-start | bytes 983044
  44.5 20.6 %collective-permute-start.12 = (bf16[400,1024]{1,0:T(8,128)(2,1)S(1)}, bf16[400,1024]{1,0:T(8,128)(2,1)S(1)}, u32[]{:S(2)}, u32[]{:S(2)}) collective-permute-start(bf16[400,1024]{1,0:T(8,128)(2,1)S(1)} %get-tuple-element.76.own_b), channel_id=1, source_target_pairs={{0,4},{4,0},{1,5},{5,1},{2,6},{6,2},{3,7},{7,3},{8,12},{12,8},{9,1... | collective-permute-start | bytes 2457608 | tf_op jit(solution)/shard_map/ppermute | solution.py:47
  46.1 21.9 %collective-permute-start.9 = (bf16[64,2560]{1,0:T(8,128)(2,1)S(1)}, bf16[64,2560]{1,0:T(8,128)(2,1)S(1)}, u32[]{:S(2)}, u32[]{:S(2)}) collective-permute-start(bf16[64,2560]{1,0:T(8,128)(2,1)S(1)} %collective-permute-done.4.refs_1_), channel_id=1, source_target_pairs={{0,2},{2,0},{1,3},{3,1},{4,6},{6,4},{5,7},{7,5},{8,10},{10,8},{9,1... | collective-permute-start | bytes 983048 | tf_op jit(solution)/shard_map/ppermute | solution.py:47
  47.6 20.4 %collective-permute-start.10 = (bf16[800,256]{1,0:T(8,128)(2,1)S(1)}, bf16[800,256]{1,0:T(8,128)(2,1)S(1)}, u32[]{:S(2)}, u32[]{:S(2)}) collective-permute-start(bf16[800,256]{1,0:T(8,128)(2,1)S(1)} %get-tuple-element.74), channel_id=1, source_target_pairs={{0,24},{8,16},{16,8},{24,0},{1,25},{9,17},{17,9},{25,1},{2,26},{10... | collective-permute-start | bytes 1228808 | tf_op jit(solution)/shard_map/ppermute | solution.py:47
  48.9 19.7 %collective-permute-start.11 = (bf16[800,256]{1,0:T(8,128)(2,1)S(1)}, bf16[800,256]{1,0:T(8,128)(2,1)S(1)}, u32[]{:S(2)}, u32[]{:S(2)}) collective-permute-start(bf16[800,256]{1,0:T(8,128)(2,1)S(1)} %get-tuple-element.75), channel_id=1, source_target_pairs={{0,8},{8,0},{16,24},{24,16},{1,9},{9,1},{17,25},{25,17},{2,10},{10... | collective-permute-start | bytes 1228808 | tf_op jit(solution)/shard_map/ppermute | solution.py:47
  68.7 2.5 %collective-permute-start.14 = (bf16[64,2560]{1,0:T(8,128)(2,1)S(1)}, bf16[64,2560]{1,0:T(8,128)(2,1)S(1)}, u32[]{:S(2)}, u32[]{:S(2)}) collective-permute-start(bf16[64,2560]{1,0:T(8,128)(2,1)S(1)} %collective-permute-done.9.refs_2_), channel_id=1, source_target_pairs={{0,1},{1,0},{2,3},{3,2},{4,5},{5,4},{6,7},{7,6},{8,9},{9,8},{10,11... | collective-permute-start | bytes 983048 | tf_op jit(solution)/shard_map/ppermute | solution.py:47
  68.7 37.1 %collective-permute-start.18 = (bf16[800,256]{1,0:T(8,128)(2,1)S(1)}, bf16[800,256]{1,0:T(8,128)(2,1)S(1)}, u32[]{:S(2)}, u32[]{:S(2)}) collective-permute-start(bf16[800,256]{1,0:T(8,128)(2,1)S(1)} %fusion.23), channel_id=1, source_target_pairs={{0,16},{8,24},{16,0},{24,8},{1,17},{9,25},{17,1},{25,9},{2,18},{10... | collective-permute-start | bytes 1228808 | tf_op jit(solution)/shard_map/ppermute | solution.py:47
  75.0 12.1 %collective-permute-start.15 = (bf16[512,2560]{1,0:T(8,128)(2,1)S(1)}, bf16[512,2560]{1,0:T(8,128)(2,1)S(1)}, u32[]{:S(2)}, u32[]{:S(2)}) collective-permute-start(bf16[512,2560]{1,0:T(8,128)(2,1)S(1)} %convolution_convert_fusion), channel_id=1, source_target_pairs={{0,1},{1,0},{2,3},{3,2},{4,5},{5,4},{6,7},{7,6},{8,9},{9,8},{10,11... | collective-permute-start | bytes 7864328 | tf_op jit(solution)/shard_map/ppermute | solution.py:47
  79.0 42.9 %collective-permute-start.20 = (bf16[800,256]{1,0:T(8,128)(2,1)S(1)}, bf16[800,256]{1,0:T(8,128)(2,1)S(1)}, u32[]{:S(2)}, u32[]{:S(2)}) collective-permute-start(bf16[800,256]{1,0:T(8,128)(2,1)S(1)} %fusion.14), channel_id=1, source_target_pairs={{0,24},{8,16},{16,8},{24,0},{1,25},{9,17},{17,9},{25,1},{2,26},{10... | collective-permute-start | bytes 1228808 | tf_op jit(solution)/shard_map/ppermute | solution.py:47
  81.7 41.5 %collective-permute-start.22 = (bf16[800,256]{1,0:T(8,128)(2,1)S(1)}, bf16[800,256]{1,0:T(8,128)(2,1)S(1)}, u32[]{:S(2)}, u32[]{:S(2)}) collective-permute-start(bf16[800,256]{1,0:T(8,128)(2,1)S(1)} %fusion.20), channel_id=1, source_target_pairs={{0,8},{8,0},{16,24},{24,16},{1,9},{9,1},{17,25},{25,17},{2,10},{10... | collective-permute-start | bytes 1228808 | tf_op jit(solution)/shard_map/ppermute | solution.py:47
  88.3 16.4 %collective-permute-start.17 = (bf16[2,64,2560]{2,1,0:T(8,128)(2,1)S(1)}, bf16[2,64,2560]{2,1,0:T(8,128)(2,1)S(1)}, u32[]{:S(2)}, u32[]{:S(2)}) collective-permute-start(bf16[2,64,2560]{2,1,0:T(8,128)(2,1)S(1)} %get-tuple-element.115), channel_id=1, source_target_pairs={{0,2},{2,0},{1,3},{3,1},{4,6},{6,4},{5,7},{7,5},{8,10},{10,8},{9,1... | collective-permute-start | bytes 1966088 | tf_op jit(solution)/shard_map/ppermute | solution.py:47
  90.5 46.0 %collective-permute-start.23 = (bf16[400,2560]{1,0:T(8,128)(2,1)S(1)}, bf16[400,2560]{1,0:T(8,128)(2,1)S(1)}, u32[]{:S(2)}, u32[]{:S(2)}) collective-permute-start(bf16[400,2560]{1,0:T(8,128)(2,1)S(1)} %fusion.2), channel_id=1, source_target_pairs={{0,4},{4,0},{1,5},{5,1},{2,6},{6,2},{3,7},{7,3},{8,12},{12,8},{9,1... | collective-permute-start | bytes 6144008 | tf_op jit(solution)/shard_map/ppermute | solution.py:47
  104.7 15.5 %collective-permute-start.16 = (bf16[2,64,2560]{2,1,0:T(8,128)(2,1)S(1)}, bf16[2,64,2560]{2,1,0:T(8,128)(2,1)S(1)}, u32[]{:S(2)}, u32[]{:S(2)}) collective-permute-start(bf16[2,64,2560]{2,1,0:T(8,128)(2,1)S(1)} %get-tuple-element.114), channel_id=1, source_target_pairs={{0,2},{2,0},{1,3},{3,1},{4,6},{6,4},{5,7},{7,5},{8,10},{10,8},{9,1... | collective-permute-start | bytes 1966088 | tf_op jit(solution)/shard_map/ppermute | solution.py:47
  105.8 17.4 %copy-start.2 = (bf16[256,3200]{1,0:T(8,128)(2,1)S(1)}, bf16[256,3200]{1,0:T(8,128)(2,1)}, u32[]{:S(2)}) copy-start(bf16[256,3200]{1,0:T(8,128)(2,1)} %up.3) | copy-start | bytes 4915204
  105.8 15.8 %collective-permute-start.19 = (bf16[2,64,2560]{2,1,0:T(8,128)(2,1)S(1)}, bf16[2,64,2560]{2,1,0:T(8,128)(2,1)S(1)}, u32[]{:S(2)}, u32[]{:S(2)}) collective-permute-start(bf16[2,64,2560]{2,1,0:T(8,128)(2,1)S(1)} %fusion.4), channel_id=1, source_target_pairs={{0,8},{8,0},{16,24},{24,16},{1,9},{9,1},{17,25},{25,17},{2,10},{10... | collective-permute-start | bytes 1966088 | tf_op jit(solution)/shard_map/ppermute | solution.py:47
  121.9 17.2 %collective-permute-start.21 = (bf16[64,2560]{1,0:T(8,128)(2,1)S(1)}, bf16[64,2560]{1,0:T(8,128)(2,1)S(1)}, u32[]{:S(2)}, u32[]{:S(2)}) collective-permute-start(bf16[64,2560]{1,0:T(8,128)(2,1)S(1)} %fusion.30), channel_id=1, source_target_pairs={{0,16},{8,24},{16,0},{24,8},{1,17},{9,25},{17,1},{25,9},{2,18},{10... | collective-permute-start | bytes 983048 | tf_op jit(solution)/shard_map/ppermute | solution.py:47
